TPU v7x, 512 devices: a whole 4x8x8 slice. The times are simulated.
512 devices in a mesh: segment: 2 (over core), lat: 16 (over y, x_hi), lon: 16 (over x_lo, z).
Axes of the slice: x: 4 (x_hi: 2, x_lo: 2; x = x_hi * 2 + x_lo), y: 8, z: 8, core: 2. Of those that a mesh axis runs over, the one named last changes fastest.
Arguments:
- saved_inputs: bfloat16 [2, 2, 96, 384, 512], P('segment', None, 'lat', 'lon'), may hold values from -6 to 6
- cotangent: bfloat16 [2, 2, 96, 384, 512], P('segment', None, 'lat', 'lon'), may hold values from -6 to 6
- pole_mask: int32 [96], replicated, may hold values from 0 to 1, as said below
- bias_index: int32 [144, 144], replicated, may hold values from 0 to 758
- table_shallow: float32 [759, 8], replicated, may hold values from -8 to 253
- table_deep: float32 [759, 8], replicated, may hold values from -8 to 253
- qkv_shallow: bfloat16 [512, 1536], P('lat', 'lon'), may hold values from -0.25 to 0.25
- proj_shallow: bfloat16 [512, 512], P('lat', 'lon'), may hold values from -0.25 to 0.25
- qkv_deep: bfloat16 [1024, 1536], P('lat', 'lon'), may hold values from -0.1875 to 0.1875
- proj_deep: bfloat16 [512, 1024], P('lat', 'lon'), may hold values from -0.25 to 0.25
- adapters: float32 [2, 98304], P('segment'), may hold values from -0.3 to 0.3
Outputs:
- passed_input_gradients: bfloat16 [2, 2, 96, 384, 512], P('segment', None, 'lat', 'lon')
- adapter_grads: float32 [2, 98304], P('segment')
Inputs may be any that keep to these rules, and one draw needn't show every extreme that they name: `pole_mask`: zero exactly on the first and on the last few rows (1 to 3 at each pole), one on all others.
All inputs are finite; a program needn't handle non-finite values.
Results may differ from a plain program's by a relative error of at most 0.014.
Values may be sent and summed in bfloat16 or wider, within the bound.
No kernel may reach another device: no remote copies, remote signals or barrier semaphores. Data moves between devices by JAX's collectives and lax.ppermute only.
A program may use at most 128 MiB of HBM per device.

v0:
```python
import jax
import jax.numpy as jnp
from jax import lax
from jax.sharding import PartitionSpec as P

D_S = 512
D_D = 1024
HEAD = 64
WLAT = 6
WLON = 12
RS = 32
RD = 24
QKV = 1536
INNER = 512


epsilon = 1e-05
precise = lax.Precision.HIGHEST


def from_behind(block, axis, distance):
    devices = range(lax.axis_size(axis))
    route = [((i - distance) % len(devices), i) for i in devices]
    return lax.ppermute(block, axis, route)


def from_partner(value, axis, apart):
    mask = 2**apart
    pairs = [(source, source ^ mask) for source in range(lax.axis_size(axis))]
    return lax.ppermute(value, axis, pairs)


def unpack(flat_vector, shapes):
    split_portions = []
    offset = 0
    for row_count, col_count in shapes:
        split_portions.append(
            flat_vector[offset : offset + row_count * col_count].reshape(row_count, col_count)
        )
        offset += row_count * col_count
    return split_portions


def to_windows(token_grid):
    levels, row_count, col_count, features = token_grid.shape
    split_grid = token_grid.reshape(
        levels, row_count // WLAT, WLAT, col_count // WLON, WLON, features
    )
    return split_grid.transpose(1, 3, 0, 2, 4, 5).reshape(-1, levels * WLAT * WLON, features)


def from_windows(windows, levels, row_count, col_count):
    features = windows.shape[-1]
    split_grid = windows.reshape(row_count // WLAT, col_count // WLON, levels, WLAT, WLON, features)
    return split_grid.transpose(2, 0, 3, 1, 4, 5).reshape(levels, row_count, col_count, features)


def row_tokens(row_values, levels, col_count):
    spread = jnp.broadcast_to(
        row_values[None, :, None, None], (levels, row_values.shape[0], col_count, 1)
    )
    return to_windows(spread)[:, :, 0]


def window_block(token_grid, w_qkv, w_proj, table, bias_index, adapter_list, key_ok, region):
    levels, row_count, col_count, features = token_grid.shape
    a_qkv, b_qkv, a_proj, b_proj = adapter_list
    head_count = table.shape[1]
    windows = to_windows(token_grid)
    window_count = windows.shape[0]
    tokens = windows.shape[1]
    value_entries = windows.astype(jnp.float32).reshape(window_count * tokens, features)
    centred = value_entries - jnp.mean(value_entries, axis=-1, keepdims=True)
    normed = (
        centred * lax.rsqrt(jnp.mean(centred * centred, axis=-1, keepdims=True) + epsilon)
    ).astype(jnp.bfloat16)
    low_rank = jnp.dot(
        jnp.dot(normed.astype(jnp.float32), a_qkv, precision=precise), b_qkv, precision=precise
    )
    projected = (jnp.dot(normed, w_qkv, preferred_element_type=jnp.float32) + low_rank).astype(
        jnp.bfloat16
    )
    projected = projected.reshape(window_count, tokens, 3, head_count, HEAD)
    scores = jnp.einsum(
        "wqhd,wkhd->whqk",
        projected[:, :, 0],
        projected[:, :, 1],
        preferred_element_type=jnp.float32,
    ) * HEAD ** (-0.5)
    pos_bias = jnp.take(jnp.transpose(table), bias_index, axis=1)
    scores = scores + pos_bias[None]
    key_valid = row_tokens(key_ok, levels, col_count)
    key_region = row_tokens(region, levels, col_count)
    allowed = (key_valid[:, None, :] > 0) & (key_region[:, :, None] == key_region[:, None, :])
    scores = jnp.where(allowed[:, None], scores, -1000000000.0)
    row_max = jnp.max(scores, axis=-1, keepdims=True)
    exp_scores = jnp.exp(scores - row_max)
    attention = (exp_scores / jnp.sum(exp_scores, axis=-1, keepdims=True)).astype(jnp.bfloat16)
    mixed_out = jnp.einsum(
        "whqk,wkhd->wqhd", attention, projected[:, :, 2], preferred_element_type=jnp.float32
    )
    mixed_out = mixed_out.astype(jnp.bfloat16).reshape(window_count * tokens, head_count * HEAD)
    low_proj = jnp.dot(
        jnp.dot(mixed_out.astype(jnp.float32), a_proj, precision=precise), b_proj, precision=precise
    )
    result = (
        value_entries + jnp.dot(mixed_out, w_proj, preferred_element_type=jnp.float32) + low_proj
    )
    return from_windows(
        result.astype(jnp.bfloat16).reshape(window_count, tokens, features),
        levels,
        row_count,
        col_count,
    )


def shards(
    saved_inputs,
    cotangent,
    pole_mask,
    bias_index,
    table_shallow,
    table_deep,
    qkv_shallow,
    proj_shallow,
    qkv_deep,
    proj_deep,
    adapters,
):
    partial_w = (
        lax.all_gather(qkv_shallow, "lat", axis=0, tiled=True),
        lax.all_gather(proj_shallow, "lat", axis=0, tiled=True),
        lax.all_gather(qkv_deep, "lat", axis=0, tiled=True),
        lax.all_gather(proj_deep, "lat", axis=0, tiled=True),
    )
    full_w = (
        lax.all_gather(partial_w[0], "lon", axis=1, tiled=True),
        lax.all_gather(partial_w[1], "lon", axis=1, tiled=True),
        lax.all_gather(partial_w[2], "lon", axis=1, tiled=True),
        lax.all_gather(partial_w[3], "lon", axis=1, tiled=True),
    )
    shallow_qkv, shallow_proj, deep_qkv, deep_proj = (full_w[0], full_w[1], full_w[2], full_w[3])
    token_grid = saved_inputs[0]
    incoming = cotangent[0]
    flat_vector = adapters[0]
    levels, row_count, col_count, features = token_grid.shape
    segment_index = lax.axis_index("segment")
    lat_index = lax.axis_index("lat")
    total_rows = row_count * lax.axis_size("lat")
    half_lat = WLAT // 2
    half_lon = WLON // 2
    strip_cols = 2 * half_lon
    global_rows = lat_index * row_count + jnp.arange(row_count, dtype=jnp.int32)
    shifted_row_block = global_rows + half_lat
    shift_ok = jnp.take(pole_mask, shifted_row_block % total_rows)
    region = (shifted_row_block >= total_rows).astype(jnp.int32)
    shallow_shapes = ((D_S, RS), (RS, QKV), (INNER, RS), (RS, D_S))
    deep_shapes = ((D_D, RD), (RD, QKV), (INNER, RD), (RD, D_D))

    def shallow_block(grid_in, vector_in):
        return window_block(
            grid_in,
            shallow_qkv,
            shallow_proj,
            table_shallow,
            bias_index,
            unpack(vector_in, shallow_shapes),
            shift_ok,
            region,
        )

    def deep_block(grid_in, vector_in):
        paired = grid_in.reshape(levels, row_count, col_count // 2, 2 * features)
        out_grid = window_block(
            paired,
            deep_qkv,
            deep_proj,
            table_deep,
            bias_index,
            unpack(vector_in, deep_shapes),
            shift_ok,
            region,
        )
        return out_grid.reshape(levels, row_count, col_count, features)

    top_strip = from_behind((token_grid[:, :half_lat], incoming[:, :half_lat]), "lat", -1)
    lat_grid = jnp.concatenate([token_grid[:, half_lat:], top_strip[0]], 1)
    lat_cot = jnp.concatenate([incoming[:, half_lat:], top_strip[1]], 1)
    side_strip = from_behind((lat_grid[:, :, :strip_cols], lat_cot[:, :, :strip_cols]), "lon", -1)

    def rolled(own_grid, strip, shift_cols):
        return jnp.concatenate([own_grid[:, :, shift_cols:], strip[:, :, :shift_cols]], 2)

    def shallow_pass():
        grid_in = rolled(lat_grid, side_strip[0], half_lon)
        cot_in = rolled(lat_cot, side_strip[1], half_lon)
        result_grid, pullback = jax.vjp(shallow_block, grid_in, flat_vector)
        return pullback(cot_in)

    def deep_pass():
        grid_in = rolled(lat_grid, side_strip[0], strip_cols)
        cot_in = rolled(lat_cot, side_strip[1], strip_cols)
        result_grid, pullback = jax.vjp(deep_block, grid_in, flat_vector)
        return pullback(cot_in)

    rolled_grad, block_grads = lax.cond(segment_index == 0, shallow_pass, deep_pass)
    adapter_sum = lax.psum(block_grads, ("lat", "lon"))
    back_strip = from_behind(rolled_grad[:, :, col_count - strip_cols :], "lon", 1)

    def unrolled(shift_cols):
        return jnp.concatenate(
            [
                back_strip[:, :, strip_cols - shift_cols :],
                rolled_grad[:, :, : col_count - shift_cols],
            ],
            2,
        )

    lon_grad = lax.cond(
        segment_index == 0, lambda: unrolled(half_lon), lambda: unrolled(strip_cols)
    )
    bottom_strip = from_behind(lon_grad[:, row_count - half_lat :], "lat", 1)
    input_grad = jnp.concatenate([bottom_strip, lon_grad[:, : row_count - half_lat]], 1)
    handed = from_partner(input_grad, "segment", 0)
    return (handed[None], adapter_sum[None])


def solution(mesh):
    in_specs = (
        P("segment", None, "lat", "lon", None),
        P("segment", None, "lat", "lon", None),
        P(),
        P(),
        P(),
        P(),
        P("lat", "lon"),
        P("lat", "lon"),
        P("lat", "lon"),
        P("lat", "lon"),
        P("segment", None),
    )
    out_specs = (P("segment", None, "lat", "lon", None), P("segment", None))
    return jax.shard_map(shards, mesh=mesh, in_specs=in_specs, out_specs=out_specs, check_vma=False)
```

profile of v0, /device:TPU:1, one launch (start us, length us, event | category | flops | bytes accessed | tf_op | source)
XLA Modules:
  0.0 640.6 jit_solution(8984860880137862959)
XLA Ops:
  7.2 36.2 %all_gather.30 = bf16[512,96]{1,0:T(8,128)(2,1)S(1)} all-gather(bf16[32,96]{1,0:T(8,128)(2,1)} %param.23), channel_id=1, replica_groups=mesh['segment'=2,'lat'=16,'lon'=16] {'lat'}, dimensions={0}, use_global_device_ids=true | all-gather | bytes 104448 | tf_op jit(solution)/shard_map/all_gather | solution.py:131
  44.2 29.9 %all_gather.24 = bf16[512,64]{1,0:T(8,128)(2,1)S(1)} all-gather(bf16[32,64]{1,0:T(8,128)(2,1)} %param.26), channel_id=1, replica_groups=mesh['segment'=2,'lat'=16,'lon'=16] {'lat'}, dimensions={0}, use_global_device_ids=true | all-gather | bytes 69632 | tf_op jit(solution)/shard_map/all_gather | solution.py:134
  75.0 34.1 %all_gather.26 = bf16[1024,96]{1,0:T(8,128)(2,1)S(1)} all-gather(bf16[64,96]{1,0:T(8,128)(2,1)} %param.25), channel_id=1, replica_groups=mesh['segment'=2,'lat'=16,'lon'=16] {'lat'}, dimensions={0}, use_global_device_ids=true | all-gather | bytes 208896 | tf_op jit(solution)/shard_map/all_gather | solution.py:133
  109.0 0.8 copy.176
  110.5 2.7 collective-permute-start
  113.7 3.3 collective-permute-start.2
  117.1 31.4 %all_gather.28 = bf16[512,32]{1,0:T(8,128)(2,1)S(1)} all-gather(bf16[32,32]{1,0:T(8,128)(2,1)S(1)} %copy-done.63), channel_id=1, replica_groups=mesh['segment'=2,'lat'=16,'lon'=16] {'lat'}, dimensions={0}, use_global_device_ids=true | all-gather | bytes 34816 | tf_op jit(solution)/shard_map/all_gather | solution.py:132
  149.2 38.6 %all_gather.29 = bf16[512,512]{0,1:T(8,128)(2,1)} all-gather(bf16[512,32]{0,1:T(8,128)(2,1)S(1)} %copy.177), channel_id=1, replica_groups=mesh['segment'=2,'lat'=16,'lon'=16] {'lon'}, dimensions={1}, use_global_device_ids=true | all-gather | bytes 557056 | tf_op jit(solution)/shard_map/all_gather | solution.py:138
  189.1 1.9 collective-permute-start.1
  191.3 1.9 collective-permute-start.3
  193.2 1.1 pad_maximum_fusion.6
  194.7 1.0 collective-permute-done.1
  195.7 2.1 collective-permute-done.3
  197.8 69.9 %all-gather.6.cloned.1.call-done = bf16[1024,1536]{0,1:T(8,128)(2,1)} async-done(((bf16[1024,96]{0,1:T(8,128)(2,1)}), bf16[1024,1536]{0,1:T(8,128)(2,1)}) %all-gather.6.cloned.1.call-update) | async-done | bytes 3145744 | tf_op jit(solution)/shard_map/all_gather | solution.py:139
  267.7 102.4 %conditional.2 = (bf16[2,6,24,512]{3,2,1,0:T(8,128)(2,1)}, f32[98304]{0:T(1024)}) conditional(s32[]{:T(128)} %convert_element_type.200, (bf16[2,6,24,512]{3,0,2,1:T(2,128)(2,1)}, bf16[2,6,12,512]{3,0,2,1:T(2,128)(2,1)}, bf16[512,1024]{0,1:T(8,128)(2,1)}, f32[98304]{0:T(1024)}, s32[6]{0:T(128)}, /*index=5*/s32[6]{0:T(128)}, ...), branch_computations={%region_0.13_spmd, %region_12.23_spmd} | conditional | flops 2295795456 | bytes 110144008 | solution.py:206
  267.9 1.0 reshape.529
  269.4 0.9 compare_select_fusion
  270.5 38.8 %gather_fusion = f32[20736,8]{1,0:T(8,128)} fusion(f32[8,759]{0,1:T(8,128)S(1)} %bitcast.194, s32[21504]{0:T(1024)S(1)} %pad_clamp_fusion), kind=kCustom, calls=%fused_computation.clone | custom fusion | bytes 1410048 | tf_op jit(solution)/shard_map/cond/branch_0_fun/jvp(jit(_take))/gather | solution.py:90
  309.4 12.4 %copy.142 = f32[144,144,8]{0,1,2:T(8,128)} copy(f32[144,144,8]{2,1,0:T(8,128)} %bitcast.196) | data formatting | bytes 1327104 | tf_op jit(solution)/shard_map/cond/branch_0_fun/jvp(jit(_take))/gather | solution.py:90
  321.8 1.6 compare_and_fusion
  323.3 1.5 copy.140
  325.6 1.3 sub.35
  326.9 1.4 copy.137
  328.4 0.9 multiply_reduce_fusion.1
  330.1 1.2 multiply_convert_fusion
  331.3 2.1 fusion.84
  334.4 0.9 slice.135
  335.4 1.7 fusion
  337.1 2.2 copy.207
  339.8 1.6 fusion.76
  341.6 0.9 copy.180
  343.2 0.8 slice.130
  344.7 1.6 fusion.12
  346.7 1.4 fusion.6
  353.2 0.9 multiply_reduce_fusion
  354.5 0.8 reshape.511
  357.2 1.2 convolution_convert_fusion.5
  370.1 1.0 slice.172
  371.1 1.9 collective-permute-start.4
  373.0 6.6 %collective-permute-done.4 = bf16[2,6,12,512]{3,2,1,0:T(8,128)(2,1)S(1)} collective-permute-done((bf16[2,6,12,512]{3,2,1,0:T(8,128)(2,1)S(1)}, bf16[2,6,12,512]{3,2,1,0:T(8,128)(2,1)S(1)}, u32[]{:S(2)}, u32[]{:S(2)}) %collective-permute-start.4) | collective-permute-done | bytes 147488 | tf_op jit(solution)/shard_map/ppermute | solution.py:24
  379.6 1.0 conditional.3
  379.6 0.9 slice.154
  380.7 4.3 collective-permute-start.5
  385.0 5.2 collective-permute-done.5
  390.2 28.0 %collective-permute-start.6 = (bf16[2,6,24,512]{3,2,1,0:T(8,128)(2,1)S(1)}, bf16[2,6,24,512]{3,2,1,0:T(8,128)(2,1)S(1)}, u32[]{:S(2)}, u32[]{:S(2)}) collective-permute-start(bf16[2,6,24,512]{3,2,1,0:T(8,128)(2,1)S(1)} %pad_maximum_fusion.5), channel_id=1, source_target_pairs={{0,256},{256,0},{1,257},{257,1},{2,258},{258,2},{3,259},{259,3},{4... | collective-permute-start | bytes 884744 | tf_op jit(solution)/shard_map/ppermute | solution.py:30
  418.2 1.2 collective-permute-done.6
  419.4 211.9 %all-reduce.16.cloned.1.call-done = f32[1,98304]{1,0:T(1,128)} async-done(((f32[1,98304]{1,0:T(1,128)}), f32[1,98304]{1,0:T(1,128)}) %all-reduce.16.cloned.1.call-update) | async-done | bytes 393232 | tf_op jit(solution)/shard_map/psum | solution.py:207
  632.0 1.8 copy.226
  (142 shorter events, 21.0 us)
Async XLA Ops:
  7.2 141.4 %copy-start = (s32[96]{0:T(128)S(1)}, s32[96]{0:T(128)}, u32[]{:S(2)}) copy-start(s32[96]{0:T(128)} %param.19) | copy-start | bytes 1156
  7.2 102.8 %copy-start.44 = (bf16[1,2,6,24,512]{4,3,2,1,0:T(8,128)(2,1)S(1)}, bf16[1,2,6,24,512]{4,3,2,1,0:T(8,128)(2,1)}, u32[]{:S(2)}) copy-start(bf16[1,2,6,24,512]{4,3,2,1,0:T(8,128)(2,1)} %param.18) | copy-start | bytes 884740
  7.2 106.0 %copy-start.45 = (bf16[1,2,6,24,512]{4,3,2,1,0:T(8,128)(2,1)S(1)}, bf16[1,2,6,24,512]{4,3,2,1,0:T(8,128)(2,1)}, u32[]{:S(2)}) copy-start(bf16[1,2,6,24,512]{4,3,2,1,0:T(8,128)(2,1)} %param.17) | copy-start | bytes 884740
  7.2 190.6 %all-gather.8.cloned.1.call-start = ((), (), s32[]{:S(2)}) async-start(), calls=%async_computation.2 | async-start | bytes 1671168 | tf_op jit(solution)/shard_map/all_gather | solution.py:137
  44.2 153.6 %all-gather.4.cloned.1.call-start = ((), (), s32[]{:S(2)}) async-start(), calls=%async_computation | async-start | bytes 1114112 | tf_op jit(solution)/shard_map/all_gather | solution.py:140
  74.9 192.7 %all-gather.6.cloned.1.call-start = ((), (), s32[]{:S(2)}) async-start(), calls=%async_computation.1 | async-start | bytes 3342336 | tf_op jit(solution)/shard_map/all_gather | solution.py:139
  109.0 8.0 %copy-start.63 = (bf16[32,32]{1,0:T(8,128)(2,1)S(1)}, bf16[32,32]{1,0:T(8,128)(2,1)}, u32[]{:S(2)}) copy-start(bf16[32,32]{1,0:T(8,128)(2,1)} %param.24) | copy-start | bytes 6148
  109.9 521.4 %all-reduce.16.cloned.1.call-start = ((), (), s32[]{:S(2)}) async-start(), calls=%async_computation.3 | async-start | bytes 786432 | tf_op jit(solution)/shard_map/psum | solution.py:207
  110.5 78.5 %collective-permute-start = (bf16[2,3,24,512]{3,0,2,1:T(2,128)(2,1)S(1)}, bf16[2,3,24,512]{3,0,2,1:T(2,128)(2,1)S(1)}, u32[]{:S(2)}, u32[]{:S(2)}) collective-permute-start(bf16[2,3,24,512]{3,0,2,1:T(2,128)(2,1)S(1)} %get-tuple-element.227), channel_id=1, source_target_pairs={{16,0},{32,16},{48,32},{64,48},{80,64},{96,80},{112,96},{128,112},... | collective-permute-start | bytes 442376 | tf_op jit(solution)/shard_map/ppermute | solution.py:24
  113.7 77.4 %collective-permute-start.2 = (bf16[2,3,24,512]{3,0,2,1:T(2,128)(2,1)S(1)}, bf16[2,3,24,512]{3,0,2,1:T(2,128)(2,1)S(1)}, u32[]{:S(2)}, u32[]{:S(2)}) collective-permute-start(bf16[2,3,24,512]{3,0,2,1:T(2,128)(2,1)S(1)} %get-tuple-element.225), channel_id=1, source_target_pairs={{16,0},{32,16},{48,32},{64,48},{80,64},{96,80},{112,96},{128,112},... | collective-permute-start | bytes 442376 | tf_op jit(solution)/shard_map/ppermute | solution.py:24
  148.6 119.1 %copy-start.59 = (f32[759,8]{0,1:T(8,128)S(1)}, f32[759,8]{0,1:T(8,128)}, u32[]{:S(2)}) copy-start(f32[759,8]{0,1:T(8,128)} %param.22) | copy-start | bytes 72868
  189.1 6.6 %collective-permute-start.1 = (bf16[2,6,12,512]{3,0,2,1:T(2,128)(2,1)S(1)}, bf16[2,6,12,512]{3,0,2,1:T(2,128)(2,1)}, u32[]{:S(2)}, u32[]{:S(2)}) collective-permute-start(bf16[2,6,12,512]{3,0,2,1:T(2,128)(2,1)S(1)} %fusion.71), channel_id=1, source_target_pairs={{1,0},{2,1},{3,2},{4,3},{5,4},{6,5},{7,6},{8,7},{9,8},{10,9},{11,1... | collective-permute-start | bytes 442376 | tf_op jit(solution)/shard_map/ppermute | solution.py:24
  191.3 6.5 %collective-permute-start.3 = (bf16[2,6,12,512]{3,0,2,1:T(2,128)(2,1)S(1)}, bf16[2,6,12,512]{3,0,2,1:T(2,128)(2,1)S(1)}, u32[]{:S(2)}, u32[]{:S(2)}) collective-permute-start(bf16[2,6,12,512]{3,0,2,1:T(2,128)(2,1)S(1)} %fusion.70), channel_id=1, source_target_pairs={{1,0},{2,1},{3,2},{4,3},{5,4},{6,5},{7,6},{8,7},{9,8},{10,9},{11,1... | collective-permute-start | bytes 442376 | tf_op jit(solution)/shard_map/ppermute | solution.py:24
  309.4 21.9 %copy-start.2 = (bf16[1024,1536]{0,1:T(8,128)(2,1)S(1)}, bf16[1024,1536]{0,1:T(8,128)(2,1)}, u32[]{:S(2)}) copy-start(bf16[1024,1536]{0,1:T(8,128)(2,1)} %get-tuple-element.172) | copy-start | bytes 9437188 | tf_op jit(solution)/shard_map/cond
  329.5 0.6 copy-start.61
  331.3 2.1 copy-start.34
  333.4 1.9 copy-start.19
  334.3 4.9 copy-start.52
  335.3 4.0 copy-start.64
  335.3 4.1 copy-start.66
  335.3 4.4 copy-start.9
  335.3 4.4 copy-start.58
  335.4 6.0 copy-start.36
  339.7 1.8 copy-start.56
  339.7 2.8 copy-start.25
  348.1 1.1 copy-start.18
  348.1 1.1 copy-start.57
  349.9 1.9 copy-start.3
  351.8 0.9 copy-start.37
  351.8 1.4 copy-start.4
  352.7 1.4 copy-start.62
  354.4 2.0 copy-start.53
  371.1 8.5 %collective-permute-start.4 = (bf16[2,6,12,512]{3,2,1,0:T(8,128)(2,1)S(1)}, bf16[2,6,12,512]{3,2,1,0:T(8,128)(2,1)S(1)}, u32[]{:S(2)}, u32[]{:S(2)}) collective-permute-start(bf16[2,6,12,512]{3,2,1,0:T(8,128)(2,1)S(1)} %slice.172), channel_id=1, source_target_pairs={{15,0},{0,1},{1,2},{2,3},{3,4},{4,5},{5,6},{6,7},{7,8},{8,9},{9,10... | collective-permute-start | bytes 442376 | tf_op jit(solution)/shard_map/ppermute | solution.py:24
  380.7 253.1 %copy-start.1 = (s32[96]{0:T(128)S(1)}, s32[96]{0:T(128)}, u32[]{:S(2)}) copy-start(s32[96]{0:T(128)} %param.19) | copy-start | bytes 1156
  380.7 9.5 %collective-permute-start.5 = (bf16[2,3,24,512]{3,2,1,0:T(8,128)(2,1)S(1)}, bf16[2,3,24,512]{3,2,1,0:T(8,128)(2,1)S(1)}, u32[]{:S(2)}, u32[]{:S(2)}) collective-permute-start(bf16[2,3,24,512]{3,2,1,0:T(8,128)(2,1)S(1)} %get-tuple-element.222), channel_id=1, source_target_pairs={{240,0},{0,16},{16,32},{32,48},{48,64},{64,80},{80,96},{96,112},{1... | collective-permute-start | bytes 442376 | tf_op jit(solution)/shard_map/ppermute | solution.py:24
  390.2 29.2 %collective-permute-start.6 = (bf16[2,6,24,512]{3,2,1,0:T(8,128)(2,1)S(1)}, bf16[2,6,24,512]{3,2,1,0:T(8,128)(2,1)S(1)}, u32[]{:S(2)}, u32[]{:S(2)}) collective-permute-start(bf16[2,6,24,512]{3,2,1,0:T(8,128)(2,1)S(1)} %pad_maximum_fusion.5), channel_id=1, source_target_pairs={{0,256},{256,0},{1,257},{257,1},{2,258},{258,2},{3,259},{259,3},{4... | collective-permute-start | bytes 884744 | tf_op jit(solution)/shard_map/ppermute | solution.py:30
Sparse Core Ops, SparseCore 0:
  44.3 71.4 all-gather.7
  117.9 70.0 all-gather.3
  190.7 76.9 all-gather.5
  385.2 246.1 all-reduce.15
where the time goes:
time: 650 us; the launch traced here: 641 us
  waiting for transfers between devices  298 us (46%)
  blocking collectives  170 us (26%)
  local copies, waits for them, and re-layouts  75.9 us (12%)
  starting transfers between devices  44.2 us (7%)
  matrix products  17 us (3%)
  between operations  14.3 us (2%)
  other arithmetic  10.7 us (2%)
  loops' own time  10.5 us (2%)
    psum x1, waiting for transfers between devices, shards(): adapter_sum = lax.psum(block_grads, ('lat', 'lon'))  212 us
    all_gather x1, waiting for transfers between devices, shards(): lax.all_gather(partial_w[2], 'lon', axis=1, tiled=True)  69.9 us
    gather x2, local copies, waits for them, and re-layouts, window_block(): pos_bias = jnp.take(jnp.transpose(table), bias_index, axis=1)  51.2 us
    all_gather x1, blocking collectives, shards(): lax.all_gather(partial_w[1], 'lon', axis=1, tiled=True)  38.6 us
    all_gather x1, blocking collectives, shards(): lax.all_gather(qkv_shallow, 'lat', axis=0, tiled=True)  36.2 us
    all_gather x1, blocking collectives, shards(): lax.all_gather(qkv_deep, 'lat', axis=0, tiled=True)  34.1 us
    all_gather x1, blocking collectives, shards(): lax.all_gather(proj_shallow, 'lat', axis=0, tiled=True)  31.4 us
    all_gather x1, blocking collectives, shards(): lax.all_gather(proj_deep, 'lat', axis=0, tiled=True)  29.9 us
  transfers between devices with their start and end apart: 11, of which 7 were waited for; matrix products, arithmetic and copies ran while one was open for 1% of the time, Pallas kernels for 0%

commit v1 on v0

v1 whole, which is shorter than its diff:
```python
import functools

import jax
import jax.numpy as jnp
from jax import lax
from jax.experimental import pallas as pl
from jax.experimental.pallas import tpu as pltpu
from jax.sharding import PartitionSpec as P

WT = 144
HEADS = 8
HEAD = 64
QKV = 1536
INNER = 512
EPSILON = 1e-05
BF = jnp.bfloat16
F32 = jnp.float32
BOTH = ("lat", "lon")

PLACES = [(y, h, w, z) for y in range(8) for h in range(2) for w in range(2) for z in range(8)]
NUMBER = {place: i for i, place in enumerate(PLACES)}


def class_groups():
    groups = []
    for c in range(8):
        members = []
        for w in range(2):
            for z in range(8):
                for h in range(2):
                    members.append(NUMBER[((c - 4 * h - 2 * w - 3 * z) % 8, h, w, z)])
        groups.append(members)
    return groups


def neighbour_send(value, dx, dy, dz):
    route = []
    for y, h, w, z in PLACES:
        x = (2 * h + w + dx) % 4
        route.append((NUMBER[(y, h, w, z)], NUMBER[((y + dy) % 8, x // 2, x % 2, (z + dz) % 8)]))
    return lax.ppermute(value, BOTH, route)


def nt(a, b):
    return lax.dot_general(a, b, (((1,), (1,)), ((), ())), preferred_element_type=F32)


def nn(a, b):
    return lax.dot_general(a, b, (((1,), (0,)), ((), ())), preferred_element_type=F32)


def tn(a, b):
    return lax.dot_general(a, b, (((0,), (0,)), ((), ())), preferred_element_type=F32)


def window_row(shape, dim):
    token = lax.broadcasted_iota(jnp.int32, shape, dim)
    token = jnp.where(token >= 72, token - 72, token)
    row = jnp.zeros(shape, jnp.int32)
    for edge in range(12, 72, 12):
        row = row + (token >= edge).astype(jnp.int32)
    return row


def bias_kernel(place_ref, pole_ref, index_ref, table_ref, bias_ref, allowed_ref):
    for half in range(2):
        lanes = slice(128 * half, 128 * half + 128)
        index = index_ref[:, lanes]
        low = index & 127
        high = index >> 7
        for head in range(HEADS):
            found = jnp.zeros((WT, 128), F32)
            for chunk in range(6):
                entries = jnp.broadcast_to(
                    table_ref[head : head + 1, 128 * chunk : 128 * chunk + 128], (WT, 128)
                )
                taken = jnp.take_along_axis(entries, low, axis=1)
                found = taken if chunk == 0 else jnp.where(high == chunk, taken, found)
            bias_ref[head, :, lanes] = found
    first = place_ref[0] * 6 + 3
    key_row = window_row((WT, 256), 0)
    query_row = window_row((WT, 256), 1)
    key_ok = jnp.zeros((WT, 256), jnp.int32)
    key_region = jnp.zeros((WT, 256), jnp.int32)
    query_region = jnp.zeros((WT, 256), jnp.int32)
    for row in range(6):
        at = first + row
        moved = jnp.where(at >= 96, 1, 0)
        key_ok = jnp.where(key_row == row, pole_ref[at - 96 * moved], key_ok)
        key_region = jnp.where(key_row == row, moved, key_region)
        query_region = jnp.where(query_row == row, moved, query_region)
    good = (key_ok > 0) & (key_region == query_region)
    allowed_ref[...] = jnp.where(good, 1.0, 0.0)


def compact(wide):
    lane = lax.broadcasted_iota(jnp.int32, (wide.shape[0], 128), 1)
    chunks = []
    for group in range(4):
        a = [wide[:, 128 * (4 * group + i) : 128 * (4 * group + i) + 128] for i in range(4)]
        one = pltpu.roll(a[1], 96, 1)
        two = pltpu.roll(a[2], 64, 1)
        three = pltpu.roll(a[3], 32, 1)
        chunks.append(jnp.where(lane < 96, a[0], one))
        chunks.append(jnp.where(lane < 64, one, two))
        chunks.append(jnp.where(lane < 32, two, three))
    return chunks


def expand(chunks):
    lane = lax.broadcasted_iota(jnp.int32, chunks[0].shape, 1)
    wide = []
    for group in range(4):
        b = chunks[3 * group : 3 * group + 3]
        wide.append(jnp.where(lane < 96, b[0], 0.0))
        one = jnp.where(lane < 32, pltpu.roll(b[0], 32, 1), pltpu.roll(b[1], 32, 1))
        wide.append(jnp.where(lane < 96, one, 0.0))
        two = jnp.where(lane < 64, pltpu.roll(b[1], 64, 1), pltpu.roll(b[2], 64, 1))
        wide.append(jnp.where(lane < 96, two, 0.0))
        wide.append(jnp.where(lane < 96, pltpu.roll(b[2], 96, 1), 0.0))
    return [part.astype(BF) for part in wide]


def selector(shape, rank, k):
    row = lax.broadcasted_iota(jnp.int32, shape, 0)
    col = lax.broadcasted_iota(jnp.int32, shape, 1)
    if shape[0] == 32:
        hit = (row < rank) & (col == row + rank * k)
    else:
        hit = (col < rank) & (row == col + rank * k)
    return jnp.where(hit, 1.0, 0.0).astype(BF)


def block_kernel(
    deep,
    place_ref, p0, p1, p2, p3, p4a, p4b, p5, p6, p7,
    x_ref, c_ref, s1_ref, s2_ref, bias_ref, allowed_ref, adapter_ref,
    own_ref, side_ref, below_ref, corner_ref, grads_ref,
    weight, weight_p, xs, cs, cols, aq_s, ap_s, bq_s, bp_s, flat,
):
    features = 1024 if deep else 512
    rank = 24 if deep else 32
    windows = 1 if deep else 2
    tokens = WT * windows
    block = features // 16
    lanes_a = 384 if deep else 128
    strides = lanes_a // rank

    label = place_ref[1]
    for o, piece in enumerate((p0, p1, p2, p3, (p4a, p4b), p5, p6, p7)):
        for j in range(16):
            for h in range(2):
                y = lax.rem(label + o - 4 * h - 2 * (j // 8) - 3 * (j % 8) + 64, 8)
                at = pl.multiple_of((2 * y + h) * block, block)
                k = 2 * j + h
                if o == 4:
                    source = piece[0][k, :block] if k < 16 else piece[1][k - 16, :block]
                else:
                    source = piece[k, :block]
                weight[pl.ds(at, block), 128 * j : 128 * j + 128] = source
    quarter = lax.broadcasted_iota(jnp.int32, (block, 128), 1) // 32
    for j in range(16):
        for m in range(4):
            tile = jnp.zeros((block, 128), F32)
            for k in range(4):
                at = (4 * m + k) * block
                part = weight[at : at + block, 128 * j : 128 * j + 128].astype(F32)
                if k < 3:
                    part = pltpu.roll(part, 32 * (k + 1), 1)
                tile = jnp.where(quarter == k, part, tile)
            weight_p[block * j : block * j + block, 128 * m : 128 * m + 128] = tile.astype(BF)

    n_aq, n_bq = features * rank // 128, rank * 12
    n_ap, n_bp = 512 * rank // 128, rank * features // 128
    off_bq, off_ap, off_bp = n_aq, n_aq + n_bq, n_aq + n_bq + n_ap
    per = lanes_a // 128
    for off, rows, dest in ((0, n_aq, aq_s), (off_ap, n_ap, ap_s)):
        parts = [adapter_ref[pl.ds(off + c, rows // per, stride=per), :] for c in range(per)]
        packed = jnp.concatenate(parts, 1) if per > 1 else parts[0]
        packed = packed.astype(BF)
        for k in range(strides):
            dest[pl.ds(k, rows // per, stride=strides), :] = nn(packed, selector((lanes_a, 128), rank, k))
    if rank < 32:
        bq_s[...] = jnp.zeros_like(bq_s)
        bp_s[...] = jnp.zeros_like(bp_s)
    for c in range(12):
        bq_s[0:rank, 128 * c : 128 * c + 128] = adapter_ref[pl.ds(off_bq + c, rank, stride=12), :]
    for c in range(features // 128):
        bp_s[0:rank, 128 * c : 128 * c + 128] = adapter_ref[
            pl.ds(off_bp + c, rank, stride=features // 128), :
        ]
    a_qkv, b_qkv = aq_s[:, 0:32].astype(BF), bq_s[...].astype(BF)
    a_proj, b_proj = ap_s[:, 0:32].astype(BF), bp_s[...].astype(BF)

    for source, which, dest in ((x_ref, 0, xs), (c_ref, 1, cs)):
        for level in range(2):
            for row in range(6):
                if row < 3:
                    own = source[level, row + 3].astype(F32)
                else:
                    own = s1_ref[which, level, row - 3].astype(F32)
                side = s2_ref[which, level, row].astype(F32)
                at = 72 * level + 12 * row
                if deep:
                    for c in range(4):
                        lanes = slice(128 * c, 128 * c + 128)
                        cols[c, 0:12] = own[12:24, lanes]
                        cols[c, 12:24] = side[:, lanes]
                        for odd in range(2):
                            to = 512 * odd + 128 * c
                            dest[at : at + 12, to : to + 128] = cols[c, pl.ds(odd, 12, stride=2), :]
                else:
                    dest[at : at + 12, :] = own[6:18]
                    dest[at + 144 : at + 150, :] = own[18:24]
                    dest[at + 150 : at + 156, :] = side[0:6]

    x = xs[...]
    cot = cs[...]
    cot_b = cot.astype(BF)
    centred = x - jnp.mean(x, axis=1, keepdims=True)
    scale = lax.rsqrt(jnp.mean(centred * centred, axis=1, keepdims=True) + EPSILON)
    xhat = centred * scale
    normed = xhat.astype(BF)
    low_q = nn(normed, a_qkv).astype(BF)
    chunks = compact(nn(normed, weight[...]))
    low = nn(low_q, b_qkv)
    chunks = [chunks[c] + low[:, 128 * c : 128 * c + 128] for c in range(12)]
    low_c = nt(cot_b, b_proj).astype(BF)
    d_mixed = nn(cot_b, weight_p[...]) + nt(low_c, a_proj)

    lane = lax.broadcasted_iota(jnp.int32, (WT, 128), 1)
    allowed = allowed_ref[:, :WT] > 0.0
    mixed = [[None] * windows for _ in range(4)]
    d_chunks = [[None] * windows for _ in range(12)]
    for w in range(windows):
        rows = slice(WT * w, WT * w + WT)
        for pair in range(4):
            q = chunks[pair][rows].astype(BF)
            k = chunks[4 + pair][rows].astype(BF)
            v = chunks[8 + pair][rows].astype(BF)
            d_o = d_mixed[rows, 128 * pair : 128 * pair + 128].astype(BF)
            found = []
            for half in range(2):
                mine = (lane >= 64) if half else (lane < 64)
                q_half = jnp.where(mine, q * 0.125, jnp.zeros_like(q))
                v_half = jnp.where(mine, v, jnp.zeros_like(v))
                s = nt(k, q_half) + bias_ref[2 * pair + half, :, :WT]
                s = jnp.where(allowed, s, -1000000000.0)
                e = jnp.exp(s - jnp.max(s, axis=0, keepdims=True))
                p = e / jnp.sum(e, axis=0, keepdims=True)
                p_b = p.astype(BF)
                d_p = nt(v_half, d_o)
                d_s = p * (d_p - jnp.sum(d_p * p, axis=0, keepdims=True))
                d_s = jnp.where(allowed, d_s, 0.0).astype(BF)
                found.append((tn(p_b, v), tn(d_s, k), nn(d_s, q), nn(p_b, d_o)))
            both = [jnp.where(lane < 64, one, two) for one, two in zip(*found)]
            mixed[pair][w] = both[0].astype(BF)
            d_chunks[pair][w] = both[1] * 0.125
            d_chunks[4 + pair][w] = both[2] * 0.125
            d_chunks[8 + pair][w] = both[3]

    def joined(parts, axis):
        return parts[0] if len(parts) == 1 else jnp.concatenate(parts, axis)

    mixed = joined([joined(parts, 0) for parts in mixed], 1)
    d_chunks = [joined(parts, 0) for parts in d_chunks]
    d_proj = joined([part.astype(BF) for part in d_chunks], 1)

    low_m = nn(mixed, a_proj).astype(BF)
    back = nt(d_proj, b_qkv).astype(BF)
    d_wide = joined(expand(d_chunks), 1)
    d_n = nt(d_wide, weight[...]) + nt(back, a_qkv)
    mean_1 = jnp.mean(d_n, axis=1, keepdims=True)
    mean_2 = jnp.mean(d_n * xhat, axis=1, keepdims=True)
    xs[...] = cot + scale * (d_n - mean_1 - xhat * mean_2)

    aq_s[:, 0:32] = tn(normed, back)
    ap_s[:, 0:32] = tn(mixed, low_c)
    d_bq = tn(low_q, d_proj)
    d_bp = tn(low_m, cot_b)
    for off, rows, source in ((0, n_aq, aq_s), (off_ap, n_ap, ap_s)):
        total = jnp.zeros((rows // per, lanes_a), F32)
        for k in range(strides):
            part = source[pl.ds(k, rows // per, stride=strides), :][:, 0:32].astype(BF)
            total = total + nn(part, selector((32, lanes_a), rank, k))
        for c in range(per):
            flat[pl.ds(off + c, rows // per, stride=per), :] = total[:, 128 * c : 128 * c + 128]
    for c in range(12):
        flat[pl.ds(off_bq + c, rank, stride=12), :] = d_bq[0:rank, 128 * c : 128 * c + 128]
    for c in range(features // 128):
        flat[pl.ds(off_bp + c, rank, stride=features // 128), :] = d_bp[
            0:rank, 128 * c : 128 * c + 128
        ]
    grads_ref[...] = flat[...].astype(BF)

    for level in range(2):
        for row in range(6):
            at = 72 * level + 12 * row
            main, strip = (own_ref, side_ref) if row < 3 else (below_ref, corner_ref)
            if deep:
                for c in range(4):
                    lanes = slice(128 * c, 128 * c + 128)
                    for odd in range(2):
                        to = 512 * odd + 128 * c
                        cols[c, pl.ds(odd, 12, stride=2), :] = xs[at : at + 12, to : to + 128]
                    main[level, row % 3, 12:24, lanes] = cols[c, 0:12].astype(BF)
                    strip[level, row % 3, :, lanes] = cols[c, 12:24].astype(BF)
            else:
                for c in range(4):
                    lanes = slice(128 * c, 128 * c + 128)
                    cols[c, 0:6] = xs[at + 150 : at + 156, lanes]
                    cols[c, 6:18] = xs[at : at + 12, lanes]
                    cols[c, 18:24] = xs[at + 144 : at + 150, lanes]
                    whole = cols[c].astype(BF)
                    main[level, row % 3, :, lanes] = whole
                    strip[level, row % 3, :, lanes] = whole[0:12]


def run_block(deep, operands):
    features = 1024 if deep else 512
    tokens = WT if deep else 2 * WT
    spec = pl.BlockSpec(memory_space=pltpu.VMEM)
    return pl.pallas_call(
        functools.partial(block_kernel, deep),
        out_shape=(
            jax.ShapeDtypeStruct((2, 3, 24, 512), BF),
            jax.ShapeDtypeStruct((2, 3, 12, 512), BF),
            jax.ShapeDtypeStruct((2, 3, 24, 512), BF),
            jax.ShapeDtypeStruct((2, 3, 12, 512), BF),
            jax.ShapeDtypeStruct((768, 128), BF),
        ),
        in_specs=[pl.BlockSpec(memory_space=pltpu.SMEM)] + [spec] * (len(operands) - 1),
        out_specs=(spec,) * 5,
        scratch_shapes=[
            pltpu.VMEM((features, 2048), BF),
            pltpu.VMEM((features, 512), BF),
            pltpu.VMEM((tokens, features), F32),
            pltpu.VMEM((tokens, features), F32),
            pltpu.VMEM((4, 24, 128), F32),
            pltpu.VMEM((features, 128), F32),
            pltpu.VMEM((512, 128), F32),
            pltpu.VMEM((32, QKV), F32),
            pltpu.VMEM((32, features), F32),
            pltpu.VMEM((768, 128), F32),
        ],
        compiler_params=pltpu.CompilerParams(vmem_limit_bytes=56 * 1024 * 1024),
        name="deep_block" if deep else "shallow_block",
    )(*operands)


def sum_kernel(parts_ref, out_ref):
    total = parts_ref[0].astype(F32)
    for i in range(1, 16):
        total = total + parts_ref[i].astype(F32)
    out_ref[...] = jnp.broadcast_to(total.astype(BF)[None], out_ref.shape)


def summed(parts):
    return pl.pallas_call(
        sum_kernel,
        out_shape=jax.ShapeDtypeStruct((16, 48, 128), BF),
        in_specs=[pl.BlockSpec(memory_space=pltpu.VMEM)],
        out_specs=pl.BlockSpec(memory_space=pltpu.VMEM),
        name="sum_parts",
    )(parts)


def shards(
    saved_inputs, cotangent, pole_mask, bias_index, table_shallow, table_deep,
    qkv_shallow, proj_shallow, qkv_deep, proj_deep, adapters,
):
    segment = lax.axis_index("segment")
    lat = lax.axis_index("lat")
    lon = lax.axis_index("lon")
    x, cot = saved_inputs[0], cotangent[0]

    with jax.named_scope("pack"):
        shallow_w = jnp.concatenate([qkv_shallow, proj_shallow.T], 1)
        deep_w = jnp.concatenate([qkv_deep, proj_deep.T], 1)
        own_w = jnp.where(segment == 1, deep_w, jnp.pad(shallow_w, ((0, 32), (0, 0))))
        own_w = jnp.broadcast_to(own_w[None], (32, 64, 128))
    with jax.named_scope("halo_rows"):
        top = jnp.stack([x[:, :3], cot[:, :3]])
        s1 = lax.ppermute(top, "lat", [((i + 1) % 16, i) for i in range(16)])
    with jax.named_scope("weights_class"):
        piece = lax.all_to_all(own_w, BOTH, 0, 0, axis_index_groups=class_groups())
    with jax.named_scope("halo_columns"):
        left = jnp.stack([x[:, 3:, :12], cot[:, 3:, :12]])
        left = jnp.concatenate([left, s1[:, :, :, :12]], 2)
        s2 = lax.ppermute(left, "lon", [((i + 1) % 16, i) for i in range(16)])
    with jax.named_scope("weights_neighbours"):
        p6 = neighbour_send(piece, 1, 0, 0)
        p2 = neighbour_send(piece, -1, 0, 0)
        p7 = neighbour_send(piece, 0, 1, 0)
        p1 = neighbour_send(piece, 0, -1, 0)
        p5 = neighbour_send(piece, 0, 0, 1)
        p3 = neighbour_send(piece, 0, 0, -1)
        p4a = neighbour_send(piece[:16], 0, 1, 1)
        p4b = neighbour_send(piece[16:], 0, -1, -1)

    with jax.named_scope("bias"):
        label = (4 * (lat % 2) + 2 * (lon // 8) + lat // 2 + 3 * (lon % 8)) % 8
        place = jnp.stack([lat, label]).astype(jnp.int32)
        table = jnp.where(segment == 1, table_deep, table_shallow)
        table = jnp.pad(table.T, ((0, 0), (0, 768 - table.shape[0])))
        index = jnp.pad(bias_index.T, ((0, 0), (0, 256 - WT)))
        smem = pl.BlockSpec(memory_space=pltpu.SMEM)
        vmem = pl.BlockSpec(memory_space=pltpu.VMEM)
        bias, allowed = pl.pallas_call(
            bias_kernel,
            out_shape=(
                jax.ShapeDtypeStruct((HEADS, WT, 256), F32),
                jax.ShapeDtypeStruct((WT, 256), F32),
            ),
            in_specs=[smem, smem, vmem, vmem],
            out_specs=(vmem, vmem),
            name="bias_table",
        )(place, pole_mask, index, table)

    flat = adapters.reshape(768, 128)
    operands = (
        place, piece, p1, p2, p3, p4a, p4b, p5, p6, p7, x, cot, s1, s2, bias, allowed, flat,
    )
    own, side, below, corner, grads = lax.cond(
        segment == 0,
        functools.partial(run_block, False),
        functools.partial(run_block, True),
        operands,
    )

    every = ("segment", "lat", "lon")

    def hand(value, d_lat, d_lon):
        route = []
        for s in range(2):
            for a in range(16):
                for b in range(16):
                    to = (1 - s) * 256 + (a + d_lat) % 16 * 16 + (b + d_lon) % 16
                    route.append((s * 256 + a * 16 + b, to))
        return lax.ppermute(value, every, route)

    with jax.named_scope("hand_over"):
        own = hand(own, 0, 0)
        side = hand(side, 0, 1)
        below = hand(below, 1, 0)
        corner = hand(corner, 1, 1)
    with jax.named_scope("adapter_sum"):
        grads = lax.all_to_all(grads.reshape(16, 48, 128), "lon", 0, 0)
        grads = lax.all_to_all(summed(grads), "lat", 0, 0)
        grads = lax.all_to_all(summed(grads), "lon", 0, 0)
        adapter_sum = grads.astype(F32).reshape(1, 98304)
    with jax.named_scope("assemble"):
        edge = jnp.where(segment == 0, 12, 6)
        column = lax.broadcasted_iota(jnp.int32, (1, 1, 24, 1), 2)
        main = jnp.concatenate([below, own], 1)
        strip = jnp.concatenate([corner, side], 1)
        strip = jnp.pad(strip, ((0, 0), (0, 0), (0, 12), (0, 0)))
        gradient = jnp.where(column < edge, strip, main)
    return gradient[None], adapter_sum


def solution(mesh):
    tokens = P("segment", None, "lat", "lon", None)
    in_specs = (
        tokens, tokens, P(), P(), P(), P(),
        P("lat", "lon"), P("lat", "lon"), P("lat", "lon"), P("lat", "lon"), P("segment", None),
    )
    return jax.shard_map(
        shards, mesh=mesh, in_specs=in_specs, out_specs=(tokens, P("segment", None)), check_vma=False
    )
```

time: 650 us -> 159 us (0.24); the launches traced: 641 us -> 158 us
  waiting for transfers between devices: 298 us -> 24.6 us
  blocking collectives: 170 us -> 12.2 us
  local copies, waits for them, and re-layouts: 75.9 us -> 4.74 us
  starting transfers between devices: 44.2 us -> 90.7 us
  Pallas kernels: 0 us -> 22 us
  matrix products: 17 us -> 0 us
  between operations: 14.3 us -> 1.14 us
  loops' own time: 10.5 us -> 0.01 us
  other arithmetic: 10.7 us -> 2.65 us
    psum x1 -> x0, waiting for transfers between devices: 212 us -> none  [shards(): adapter_sum = lax.psum(block_grads, ('lat', 'lon'))]
    all_gather x5 -> x0, blocking collectives: 170 us -> none  [the longest x1 38.6 us: shards(): lax.all_gather(partial_w[1], 'lon', axis=1, tiled=True)]
    all_gather x3 -> x0, waiting for transfers between devices: 69.9 us -> none  [the longest x1 69.9 us: shards(): lax.all_gather(partial_w[2], 'lon', axis=1, tiled=True)]
    gather x3 -> x0, local copies, waits for them, and re-layouts: 51.9 us -> none  [the longest x2 51.2 us: window_block(): pos_bias = jnp.take(jnp.transpose(table), bias_index, axis=1)]
    all_to_all x0 -> x3, starting transfers between devices: none -> 27.3 us  [the longest x1 18.2 us: shards(): piece = lax.all_to_all(own_w, BOTH, 0, 0, axis_index_groups=class_groups())]
    pallas_call x0 -> x4, Pallas kernels: none -> 22 us  [the longest x1 12.3 us: run_block(): pl.pallas_call(functools.partial(block_kernel, deep), out_shape=(jax.Shap...]
    ppermute x7 -> x14, starting transfers between devices: 44.1 us -> 63.4 us  [the longest x8 28.5 us: neighbour_send(): return lax.ppermute(value, BOTH, route)]
    dot_general x20 -> x0, matrix products: 17 us -> none  [the longest x3 3.01 us: window_block(): jnp.einsum('wqhd,wkhd->whqk', projected[:, :, 0], projected[:, :, 1], pre...]
  transfers between devices with their start and end apart: 11 -> 17, of which waited for: 7 -> 6; matrix products, arithmetic and copies ran while one was open for 1% -> 2% of each run, Pallas kernels for 0% -> 5%
where the time goes in v1:
time: 159 us; the launch traced here: 158 us
  starting transfers between devices  90.7 us (57%)
  waiting for transfers between devices  24.6 us (15%)
  Pallas kernels  22 us (14%)
  blocking collectives  12.2 us (8%)
  local copies, waits for them, and re-layouts  4.74 us (3%)
  other arithmetic  2.65 us (2%)
    ppermute x8, starting transfers between devices, neighbour_send(): return lax.ppermute(value, BOTH, route)  28.5 us
    ppermute x4, starting transfers between devices, hand(): return lax.ppermute(value, every, route)  24.3 us
    all_to_all x1, starting transfers between devices, shards(): piece = lax.all_to_all(own_w, BOTH, 0, 0, axis_index_groups=class_groups())  18.2 us
    pallas_call x1, Pallas kernels, run_block(): pl.pallas_call(functools.partial(block_kernel, deep), out_shape=(jax.Shap...  12.3 us
    all_to_all x1, blocking collectives, shards(): grads = lax.all_to_all(grads.reshape(16, 48, 128), 'lon', 0, 0)  12.2 us
    ppermute x1, waiting for transfers between devices, shards(): s1 = lax.ppermute(top, 'lat', [((i + 1) % 16, i) for i in range(16)])  10.4 us
    ppermute x1, starting transfers between devices, shards(): s1 = lax.ppermute(top, 'lat', [((i + 1) % 16, i) for i in range(16)])  7.66 us
    pallas_call x1, Pallas kernels, shards(): pl.pallas_call(bias_kernel, out_shape=(jax.ShapeDtypeStruct((HEADS, WT, 2...  6.46 us
  transfers between devices with their start and end apart: 17, of which 6 were waited for; matrix products, arithmetic and copies ran while one was open for 2% of the time, Pallas kernels for 5%

profile of v1, /device:TPU:1, one launch (start us, length us, event | category | flops | bytes accessed | tf_op | source)
XLA Modules:
  0.0 158.0 jit_solution(1585676970364048350)
XLA Ops:
  0.7 0.8 copy.14
  1.5 0.8 copy.13
  2.3 0.8 fusion.8
  3.1 0.9 broadcast_in_dim.18
  4.0 18.2 %all-to-all-start = ((bf16[32,64,128]{2,1,0:T(8,128)(2,1)}), bf16[32,64,128]{2,1,0:T(8,128)(2,1)S(1)}, u32[]{:S(2)}, u32[]{:S(2)}) async-start(bf16[32,64,128]{2,1,0:T(8,128)(2,1)} %broadcast_in_dim.18), calls=%async_computation | async-start | bytes 1048576 | tf_op jit(solution)/shard_map/weights_class/all_to_all | solution.py:386
  22.3 7.7 %collective-permute-start.8 = (bf16[2,2,3,24,512]{4,3,2,1,0:T(8,128)(2,1)S(1)}, bf16[2,2,3,24,512]{4,3,2,1,0:T(8,128)(2,1)S(1)}, u32[]{:S(2)}, u32[]{:S(2)}) collective-permute-start(bf16[2,2,3,24,512]{4,3,2,1,0:T(8,128)(2,1)S(1)} %pad_maximum_fusion.1), channel_id=1, source_target_pairs={{16,0},{32,16},{48,32},{64,48},{80,64},{96,80},{112,96},{128,112},... | collective-permute-start | bytes 884744 | tf_op jit(solution)/shard_map/halo_rows/ppermute | solution.py:384
  30.0 0.0 copy-start.7
  30.0 10.4 %collective-permute-done.8 = bf16[2,2,3,24,512]{4,3,2,1,0:T(8,128)(2,1)S(1)} collective-permute-done((bf16[2,2,3,24,512]{4,3,2,1,0:T(8,128)(2,1)S(1)}, bf16[2,2,3,24,512]{4,3,2,1,0:T(8,128)(2,1)S(1)}, u32[]{:S(2)}, u32[]{:S(2)}) %collective-permute-start.8) | collective-permute-done | bytes 294944 | tf_op jit(solution)/shard_map/halo_rows/ppermute | solution.py:384
  40.3 3.5 %all-to-all-done = bf16[32,64,128]{2,1,0:T(8,128)(2,1)S(1)} async-done(((bf16[32,64,128]{2,1,0:T(8,128)(2,1)}), bf16[32,64,128]{2,1,0:T(8,128)(2,1)S(1)}, u32[]{:S(2)}, u32[]{:S(2)}) %all-to-all-start) | async-done | bytes 524320 | tf_op jit(solution)/shard_map/weights_class/all_to_all | solution.py:386
  43.9 2.0 %collective-permute-start.7 = (bf16[32,64,128]{2,1,0:T(8,128)(2,1)S(1)}, bf16[32,64,128]{2,1,0:T(8,128)(2,1)S(1)}, u32[]{:S(2)}, u32[]{:S(2)}) collective-permute-start(bf16[32,64,128]{2,1,0:T(8,128)(2,1)S(1)} %all-to-all-done), channel_id=1, source_target_pairs={{0,32},{1,33},{2,34},{3,35},{4,36},{5,37},{6,38},{7,39},{8,40},{9,... | collective-permute-start | bytes 1572872 | tf_op jit(solution)/shard_map/weights_neighbours/ppermute | solution.py:41
  45.9 0.0 copy-start.8
  45.9 0.0 copy-start.9
  45.9 0.1 pad_maximum_fusion
  45.9 0.0 copy-start.2
  46.0 2.9 %collective-permute-start.9 = (bf16[2,2,6,12,512]{4,3,2,1,0:T(8,128)(2,1)S(1)}, bf16[2,2,6,12,512]{4,3,2,1,0:T(8,128)(2,1)S(1)}, u32[]{:S(2)}, u32[]{:S(2)}) collective-permute-start(bf16[2,2,6,12,512]{4,3,2,1,0:T(8,128)(2,1)S(1)} %pad_maximum_fusion), channel_id=1, source_target_pairs={{1,0},{2,1},{3,2},{4,3},{5,4},{6,5},{7,6},{8,7},{9,8},{10,9},{11,1... | collective-permute-start | bytes 884744 | tf_op jit(solution)/shard_map/halo_columns/ppermute | solution.py:390
  48.9 3.9 %collective-permute-start.4 = (bf16[16,64,128]{2,1,0:T(8,128)(2,1)S(1)}, bf16[16,64,128]{2,1,0:T(8,128)(2,1)S(1)}, u32[]{:S(2)}, u32[]{:S(2)}) collective-permute-start(bf16[16,64,128]{2,1,0:T(8,128)(2,1)S(1)} %get-tuple-element.118), channel_id=1, source_target_pairs={{0,231},{1,224},{2,225},{3,226},{4,227},{5,228},{6,229},{7,230},{8... | collective-permute-start | bytes 786440 | tf_op jit(solution)/shard_map/weights_neighbours/ppermute | solution.py:41
  52.8 2.3 %collective-permute-start.3 = (bf16[16,64,128]{2,1,0:T(8,128)(2,1)S(1)}, bf16[16,64,128]{2,1,0:T(8,128)(2,1)S(1)}, u32[]{:S(2)}, u32[]{:S(2)}) collective-permute-start(bf16[16,64,128]{2,1,0:T(8,128)(2,1)S(1)} %get-tuple-element.119), channel_id=1, source_target_pairs={{0,33},{1,34},{2,35},{3,36},{4,37},{5,38},{6,39},{7,32},{8,41},{9,... | collective-permute-start | bytes 786440 | tf_op jit(solution)/shard_map/weights_neighbours/ppermute | solution.py:41
  55.1 2.8 %collective-permute-start.6 = (bf16[32,64,128]{2,1,0:T(8,128)(2,1)S(1)}, bf16[32,64,128]{2,1,0:T(8,128)(2,1)}, u32[]{:S(2)}, u32[]{:S(2)}) collective-permute-start(bf16[32,64,128]{2,1,0:T(8,128)(2,1)S(1)} %all-to-all-done), channel_id=1, source_target_pairs={{0,8},{1,9},{2,10},{3,11},{4,12},{5,13},{6,14},{7,15},{8,16},{9,17... | collective-permute-start | bytes 1572872 | tf_op jit(solution)/shard_map/weights_neighbours/ppermute | solution.py:41
  57.9 3.5 %collective-permute-done.9 = bf16[2,2,6,12,512]{4,3,2,1,0:T(8,128)(2,1)S(1)} collective-permute-done((bf16[2,2,6,12,512]{4,3,2,1,0:T(8,128)(2,1)S(1)}, bf16[2,2,6,12,512]{4,3,2,1,0:T(8,128)(2,1)S(1)}, u32[]{:S(2)}, u32[]{:S(2)}) %collective-permute-start.9) | collective-permute-done | bytes 294944 | tf_op jit(solution)/shard_map/halo_columns/ppermute | solution.py:390
  61.4 2.7 %collective-permute-start.5 = (bf16[32,64,128]{2,1,0:T(8,128)(2,1)S(1)}, bf16[32,64,128]{2,1,0:T(8,128)(2,1)}, u32[]{:S(2)}, u32[]{:S(2)}) collective-permute-start(bf16[32,64,128]{2,1,0:T(8,128)(2,1)S(1)} %all-to-all-done), channel_id=1, source_target_pairs={{0,1},{1,2},{2,3},{3,4},{4,5},{5,6},{6,7},{7,0},{8,9},{9,10},{10,1... | collective-permute-start | bytes 1572872 | tf_op jit(solution)/shard_map/weights_neighbours/ppermute | solution.py:41
  64.1 0.0 collective-permute-done.4
  64.1 4.7 %collective-permute-start.2 = (bf16[32,64,128]{2,1,0:T(8,128)(2,1)S(1)}, bf16[32,64,128]{2,1,0:T(8,128)(2,1)}, u32[]{:S(2)}, u32[]{:S(2)}) collective-permute-start(bf16[32,64,128]{2,1,0:T(8,128)(2,1)S(1)} %all-to-all-done), channel_id=1, source_target_pairs={{0,7},{1,0},{2,1},{3,2},{4,3},{5,4},{6,5},{7,6},{8,15},{9,8},{10,9... | collective-permute-start | bytes 1572872 | tf_op jit(solution)/shard_map/weights_neighbours/ppermute | solution.py:41
  68.9 0.0 copy-start.5
  68.9 6.7 %collective-permute-start.1 = (bf16[32,64,128]{2,1,0:T(8,128)(2,1)S(1)}, bf16[32,64,128]{2,1,0:T(8,128)(2,1)}, u32[]{:S(2)}, u32[]{:S(2)}) collective-permute-start(bf16[32,64,128]{2,1,0:T(8,128)(2,1)S(1)} %all-to-all-done), channel_id=1, source_target_pairs={{0,24},{1,25},{2,26},{3,27},{4,28},{5,29},{6,30},{7,31},{8,0},{9,1... | collective-permute-start | bytes 1572872 | tf_op jit(solution)/shard_map/weights_neighbours/ppermute | solution.py:41
  75.6 3.5 %collective-permute-start = (bf16[32,64,128]{2,1,0:T(8,128)(2,1)S(1)}, bf16[32,64,128]{2,1,0:T(8,128)(2,1)}, u32[]{:S(2)}, u32[]{:S(2)}) collective-permute-start(bf16[32,64,128]{2,1,0:T(8,128)(2,1)S(1)} %all-to-all-done), channel_id=1, source_target_pairs={{0,224},{1,225},{2,226},{3,227},{4,228},{5,229},{6,230},{7,231},{8... | collective-permute-start | bytes 1572872 | tf_op jit(solution)/shard_map/weights_neighbours/ppermute | solution.py:41
  79.2 0.1 copy.15
  79.3 0.7 pad.17.index_ref
  80.0 0.6 pad.18.table_ref
  80.6 0.1 pad_add_fusion.place_ref
  80.7 6.5 %bias_table.1 = (f32[8,144,256]{2,1,0:T(8,128)S(1)}, f32[144,256]{1,0:T(8,128)}) custom-call(s32[2]{0:T(128)S(1)} %pad_add_fusion.place_ref, s32[96]{0:T(128)} %pole_ref.1, s32[144,256]{1,0:T(8,128)} %pad.17.index_ref, f32[8,768]{1,0:T(8,128)} %pad.18.table_ref), custom_call_target="tpu_custom_call" | custom-call | tf_op jit(solution)/shard_map/bias/bias_table/pallas_call | solution.py:409
  87.1 1.1 collective-permute-done
  88.2 12.3 %conditional.1 = ((bf16[2,3,24,512]{3,2,1,0:T(8,128)(2,1)}, bf16[2,3,12,512]{3,2,1,0:T(8,128)(2,1)}, bf16[2,3,24,512]{3,2,1,0:T(8,128)(2,1)}, bf16[2,3,12,512]{3,2,1,0:T(8,128)(2,1)}, bf16[768,128]{1,0:T(8,128)(2,1)})) conditional(s32[]{:T(128)} %convert_element_type.10, (s32[2]{0:T(128)S(1)}, bf16[32,64,128]{2,1,0:T(8,128)(2,1)S(1)}, ...), branch_computations={%region_0.1_spmd, %region_1.2_spmd} | conditional | bytes 8 | solution.py:424
  88.2 12.3 %deep_block.1 = (bf16[2,3,24,512]{3,2,1,0:T(8,128)(2,1)}, bf16[2,3,12,512]{3,2,1,0:T(8,128)(2,1)}, bf16[2,3,24,512]{3,2,1,0:T(8,128)(2,1)}, bf16[2,3,12,512]{3,2,1,0:T(8,128)(2,1)}, bf16[768,128]{1,0:T(8,128)(2,1)}) custom-call(s32[2]{0:T(128)S(1)} %get-tuple-element.68.place_ref, bf16[32,64,128]{2,1,0:T(8,128)(2,1)S(1)} %get-tuple-element.69.p0, ...), custom_call_target="tpu_custom_call" | custom-call | tf_op jit(solution)/shard_map/cond/branch_0_fun/deep_block/pallas_call | solution.py:323
  100.5 12.2 %all_to_all.20.parts_ref = bf16[16,48,128]{2,1,0:T(8,128)(2,1)} all-to-all(bf16[16,48,128]{2,1,0:T(8,128)(2,1)} %bitcast.34), channel_id=1, replica_groups=mesh['segment'=2,'lat'=16,'lon'=16] {'lon'}, dimensions={0} | all-to-all | bytes 393216 | tf_op jit(solution)/shard_map/adapter_sum/all_to_all | solution.py:448
  112.7 1.6 %sum_parts.2 = bf16[16,48,128]{2,1,0:T(8,128)(2,1)} custom-call(bf16[16,48,128]{2,1,0:T(8,128)(2,1)} %all_to_all.20.parts_ref), custom_call_target="tpu_custom_call" | custom-call | tf_op jit(solution)/shard_map/adapter_sum/sum_parts/pallas_call | solution.py:359
  114.3 5.7 %all-to-all-start.2 = ((bf16[16,48,128]{2,1,0:T(8,128)(2,1)}), bf16[16,48,128]{2,1,0:T(8,128)(2,1)S(1)}, u32[]{:S(2)}, u32[]{:S(2)}) async-start(bf16[16,48,128]{2,1,0:T(8,128)(2,1)} %sum_parts.2), calls=%async_computation.2 | async-start | bytes 393216 | tf_op jit(solution)/shard_map/adapter_sum/all_to_all | solution.py:449
  120.0 11.5 %collective-permute-start.12 = (bf16[2,3,24,512]{3,2,1,0:T(8,128)(2,1)S(1)}, bf16[2,3,24,512]{3,2,1,0:T(8,128)(2,1)S(1)}, u32[]{:S(2)}, u32[]{:S(2)}) collective-permute-start(bf16[2,3,24,512]{3,2,1,0:T(8,128)(2,1)S(1)} %copy-done.11), channel_id=1, source_target_pairs={{0,272},{1,273},{2,274},{3,275},{4,276},{5,277},{6,278},{7,279},{8... | collective-permute-start | bytes 442376 | tf_op jit(solution)/shard_map/hand_over/ppermute | solution.py:440
  131.6 1.9 %collective-permute-start.13 = (bf16[2,3,24,512]{3,2,1,0:T(8,128)(2,1)S(1)}, bf16[2,3,24,512]{3,2,1,0:T(8,128)(2,1)S(1)}, u32[]{:S(2)}, u32[]{:S(2)}) collective-permute-start(bf16[2,3,24,512]{3,2,1,0:T(8,128)(2,1)S(1)} %copy-done.10), channel_id=1, source_target_pairs={{0,256},{1,257},{2,258},{3,259},{4,260},{5,261},{6,262},{7,263},{8... | collective-permute-start | bytes 442376 | tf_op jit(solution)/shard_map/hand_over/ppermute | solution.py:440
  133.5 0.0 copy-start.6
  133.5 0.7 copy-done.6
  134.2 1.6 %sum_parts.3 = bf16[16,48,128]{2,1,0:T(8,128)(2,1)} custom-call(bf16[16,48,128]{2,1,0:T(8,128)(2,1)} %copy-done.6), custom_call_target="tpu_custom_call" | custom-call | tf_op jit(solution)/shard_map/adapter_sum/sum_parts/pallas_call | solution.py:359
  135.8 3.5 %all-to-all-start.3 = ((bf16[16,48,128]{2,1,0:T(8,128)(2,1)}), bf16[16,48,128]{2,1,0:T(8,128)(2,1)S(1)}, u32[]{:S(2)}, u32[]{:S(2)}) async-start(bf16[16,48,128]{2,1,0:T(8,128)(2,1)} %sum_parts.3), calls=%async_computation.3 | async-start | bytes 393216 | tf_op jit(solution)/shard_map/adapter_sum/all_to_all | solution.py:450
  139.4 8.9 %collective-permute-start.10 = (bf16[2,3,12,512]{3,2,1,0:T(8,128)(2,1)S(1)}, bf16[2,3,12,512]{3,2,1,0:T(8,128)(2,1)S(1)}, u32[]{:S(2)}, u32[]{:S(2)}) collective-permute-start(bf16[2,3,12,512]{3,2,1,0:T(8,128)(2,1)S(1)} %copy-done.13), channel_id=1, source_target_pairs={{0,273},{1,274},{2,275},{3,276},{4,277},{5,278},{6,279},{7,280},{8... | collective-permute-start | bytes 221192 | tf_op jit(solution)/shard_map/hand_over/ppermute | solution.py:440
  148.3 1.9 %collective-permute-start.11 = (bf16[2,3,12,512]{3,2,1,0:T(8,128)(2,1)S(1)}, bf16[2,3,12,512]{3,2,1,0:T(8,128)(2,1)S(1)}, u32[]{:S(2)}, u32[]{:S(2)}) collective-permute-start(bf16[2,3,12,512]{3,2,1,0:T(8,128)(2,1)S(1)} %copy-done.12), channel_id=1, source_target_pairs={{0,257},{1,258},{2,259},{3,260},{4,261},{5,262},{6,263},{7,264},{8... | collective-permute-start | bytes 221192 | tf_op jit(solution)/shard_map/hand_over/ppermute | solution.py:440
  150.2 1.7 %collective-permute-done.10 = bf16[2,3,12,512]{3,2,1,0:T(8,128)(2,1)S(1)} collective-permute-done((bf16[2,3,12,512]{3,2,1,0:T(8,128)(2,1)S(1)}, bf16[2,3,12,512]{3,2,1,0:T(8,128)(2,1)S(1)}, u32[]{:S(2)}, u32[]{:S(2)}) %collective-permute-start.10) | collective-permute-done | bytes 73760 | tf_op jit(solution)/shard_map/hand_over/ppermute | solution.py:440
  151.9 4.4 %collective-permute-done.11 = bf16[2,3,12,512]{3,2,1,0:T(8,128)(2,1)S(1)} collective-permute-done((bf16[2,3,12,512]{3,2,1,0:T(8,128)(2,1)S(1)}, bf16[2,3,12,512]{3,2,1,0:T(8,128)(2,1)S(1)}, u32[]{:S(2)}, u32[]{:S(2)}) %collective-permute-start.11) | collective-permute-done | bytes 73760 | tf_op jit(solution)/shard_map/hand_over/ppermute | solution.py:440
  156.3 0.9 fusion.4
  157.2 0.8 reshape.26
  (38 shorter events, 0.2 us)
Async XLA Ops:
  0.6 21.6 %copy-start.1 = (bf16[1,2,6,24,512]{4,3,2,1,0:T(8,128)(2,1)S(1)}, bf16[1,2,6,24,512]{4,3,2,1,0:T(8,128)(2,1)}, u32[]{:S(2)}) copy-start(bf16[1,2,6,24,512]{4,3,2,1,0:T(8,128)(2,1)} %param.14) | copy-start | bytes 884740
  0.6 21.6 %copy-start = (bf16[1,2,6,24,512]{4,3,2,1,0:T(8,128)(2,1)S(1)}, bf16[1,2,6,24,512]{4,3,2,1,0:T(8,128)(2,1)}, u32[]{:S(2)}) copy-start(bf16[1,2,6,24,512]{4,3,2,1,0:T(8,128)(2,1)} %param.13) | copy-start | bytes 884740
  4.0 39.9 %all-to-all-start = ((bf16[32,64,128]{2,1,0:T(8,128)(2,1)}), bf16[32,64,128]{2,1,0:T(8,128)(2,1)S(1)}, u32[]{:S(2)}, u32[]{:S(2)}) async-start(bf16[32,64,128]{2,1,0:T(8,128)(2,1)} %broadcast_in_dim.18), calls=%async_computation | async-start | bytes 1048576 | tf_op jit(solution)/shard_map/weights_class/all_to_all | solution.py:386
  22.3 18.1 %collective-permute-start.8 = (bf16[2,2,3,24,512]{4,3,2,1,0:T(8,128)(2,1)S(1)}, bf16[2,2,3,24,512]{4,3,2,1,0:T(8,128)(2,1)S(1)}, u32[]{:S(2)}, u32[]{:S(2)}) collective-permute-start(bf16[2,2,3,24,512]{4,3,2,1,0:T(8,128)(2,1)S(1)} %pad_maximum_fusion.1), channel_id=1, source_target_pairs={{16,0},{32,16},{48,32},{64,48},{80,64},{96,80},{112,96},{128,112},... | collective-permute-start | bytes 884744 | tf_op jit(solution)/shard_map/halo_rows/ppermute | solution.py:384
  30.0 49.2 %copy-start.7 = (s32[144,144]{1,0:T(8,128)S(1)}, s32[144,144]{1,0:T(8,128)}, u32[]{:S(2)}) copy-start(s32[144,144]{1,0:T(8,128)} %param.16) | copy-start | bytes 248836
  43.9 31.7 %collective-permute-start.7 = (bf16[32,64,128]{2,1,0:T(8,128)(2,1)S(1)}, bf16[32,64,128]{2,1,0:T(8,128)(2,1)S(1)}, u32[]{:S(2)}, u32[]{:S(2)}) collective-permute-start(bf16[32,64,128]{2,1,0:T(8,128)(2,1)S(1)} %all-to-all-done), channel_id=1, source_target_pairs={{0,32},{1,33},{2,34},{3,35},{4,36},{5,37},{6,38},{7,39},{8,40},{9,... | collective-permute-start | bytes 1572872 | tf_op jit(solution)/shard_map/weights_neighbours/ppermute | solution.py:41
  45.9 34.1 %copy-start.8 = (f32[759,8]{0,1:T(8,128)S(1)}, f32[759,8]{0,1:T(8,128)}, u32[]{:S(2)}) copy-start(f32[759,8]{0,1:T(8,128)} %param.18) | copy-start | bytes 72868
  45.9 34.1 %copy-start.9 = (f32[759,8]{0,1:T(8,128)S(1)}, f32[759,8]{0,1:T(8,128)}, u32[]{:S(2)}) copy-start(f32[759,8]{0,1:T(8,128)} %param.17) | copy-start | bytes 72868
  45.9 42.3 %copy-start.2 = (f32[1,98304]{1,0:T(1,128)S(1)}, f32[1,98304]{1,0:T(1,128)}, u32[]{:S(2)}) copy-start(f32[1,98304]{1,0:T(1,128)} %param.23) | copy-start | bytes 1179652
  46.0 15.5 %collective-permute-start.9 = (bf16[2,2,6,12,512]{4,3,2,1,0:T(8,128)(2,1)S(1)}, bf16[2,2,6,12,512]{4,3,2,1,0:T(8,128)(2,1)S(1)}, u32[]{:S(2)}, u32[]{:S(2)}) collective-permute-start(bf16[2,2,6,12,512]{4,3,2,1,0:T(8,128)(2,1)S(1)} %pad_maximum_fusion), channel_id=1, source_target_pairs={{1,0},{2,1},{3,2},{4,3},{5,4},{6,5},{7,6},{8,7},{9,8},{10,9},{11,1... | collective-permute-start | bytes 884744 | tf_op jit(solution)/shard_map/halo_columns/ppermute | solution.py:390
  48.9 15.2 %collective-permute-start.4 = (bf16[16,64,128]{2,1,0:T(8,128)(2,1)S(1)}, bf16[16,64,128]{2,1,0:T(8,128)(2,1)S(1)}, u32[]{:S(2)}, u32[]{:S(2)}) collective-permute-start(bf16[16,64,128]{2,1,0:T(8,128)(2,1)S(1)} %get-tuple-element.118), channel_id=1, source_target_pairs={{0,231},{1,224},{2,225},{3,226},{4,227},{5,228},{6,229},{7,230},{8... | collective-permute-start | bytes 786440 | tf_op jit(solution)/shard_map/weights_neighbours/ppermute | solution.py:41
  52.8 16.0 %collective-permute-start.3 = (bf16[16,64,128]{2,1,0:T(8,128)(2,1)S(1)}, bf16[16,64,128]{2,1,0:T(8,128)(2,1)S(1)}, u32[]{:S(2)}, u32[]{:S(2)}) collective-permute-start(bf16[16,64,128]{2,1,0:T(8,128)(2,1)S(1)} %get-tuple-element.119), channel_id=1, source_target_pairs={{0,33},{1,34},{2,35},{3,36},{4,37},{5,38},{6,39},{7,32},{8,41},{9,... | collective-permute-start | bytes 786440 | tf_op jit(solution)/shard_map/weights_neighbours/ppermute | solution.py:41
  55.1 32.0 %collective-permute-start.6 = (bf16[32,64,128]{2,1,0:T(8,128)(2,1)S(1)}, bf16[32,64,128]{2,1,0:T(8,128)(2,1)}, u32[]{:S(2)}, u32[]{:S(2)}) collective-permute-start(bf16[32,64,128]{2,1,0:T(8,128)(2,1)S(1)} %all-to-all-done), channel_id=1, source_target_pairs={{0,8},{1,9},{2,10},{3,11},{4,12},{5,13},{6,14},{7,15},{8,16},{9,17... | collective-permute-start | bytes 1572872 | tf_op jit(solution)/shard_map/weights_neighbours/ppermute | solution.py:41
  61.4 14.1 %copy-start.3 = (bf16[2,2,6,12,512]{4,3,2,1,0:T(8,128)(2,1)}, bf16[2,2,6,12,512]{4,3,2,1,0:T(8,128)(2,1)S(1)}, u32[]{:S(2)}) copy-start(bf16[2,2,6,12,512]{4,3,2,1,0:T(8,128)(2,1)S(1)} %collective-permute-done.9) | copy-start | bytes 884740
  61.4 25.7 %collective-permute-start.5 = (bf16[32,64,128]{2,1,0:T(8,128)(2,1)S(1)}, bf16[32,64,128]{2,1,0:T(8,128)(2,1)}, u32[]{:S(2)}, u32[]{:S(2)}) collective-permute-start(bf16[32,64,128]{2,1,0:T(8,128)(2,1)S(1)} %all-to-all-done), channel_id=1, source_target_pairs={{0,1},{1,2},{2,3},{3,4},{4,5},{5,6},{6,7},{7,0},{8,9},{9,10},{10,1... | collective-permute-start | bytes 1572872 | tf_op jit(solution)/shard_map/weights_neighbours/ppermute | solution.py:41
  64.1 11.4 %copy-start.4 = (bf16[16,64,128]{2,1,0:T(8,128)(2,1)}, bf16[16,64,128]{2,1,0:T(8,128)(2,1)S(1)}, u32[]{:S(2)}) copy-start(bf16[16,64,128]{2,1,0:T(8,128)(2,1)S(1)} %collective-permute-done.4) | copy-start | bytes 786436
  64.1 23.0 %collective-permute-start.2 = (bf16[32,64,128]{2,1,0:T(8,128)(2,1)S(1)}, bf16[32,64,128]{2,1,0:T(8,128)(2,1)}, u32[]{:S(2)}, u32[]{:S(2)}) collective-permute-start(bf16[32,64,128]{2,1,0:T(8,128)(2,1)S(1)} %all-to-all-done), channel_id=1, source_target_pairs={{0,7},{1,0},{2,1},{3,2},{4,3},{5,4},{6,5},{7,6},{8,15},{9,8},{10,9... | collective-permute-start | bytes 1572872 | tf_op jit(solution)/shard_map/weights_neighbours/ppermute | solution.py:41
  68.9 6.7 %copy-start.5 = (bf16[16,64,128]{2,1,0:T(8,128)(2,1)}, bf16[16,64,128]{2,1,0:T(8,128)(2,1)S(1)}, u32[]{:S(2)}) copy-start(bf16[16,64,128]{2,1,0:T(8,128)(2,1)S(1)} %collective-permute-done.3) | copy-start | bytes 786436
  68.9 18.3 %collective-permute-start.1 = (bf16[32,64,128]{2,1,0:T(8,128)(2,1)S(1)}, bf16[32,64,128]{2,1,0:T(8,128)(2,1)}, u32[]{:S(2)}, u32[]{:S(2)}) collective-permute-start(bf16[32,64,128]{2,1,0:T(8,128)(2,1)S(1)} %all-to-all-done), channel_id=1, source_target_pairs={{0,24},{1,25},{2,26},{3,27},{4,28},{5,29},{6,30},{7,31},{8,0},{9,1... | collective-permute-start | bytes 1572872 | tf_op jit(solution)/shard_map/weights_neighbours/ppermute | solution.py:41
  75.6 12.6 %collective-permute-start = (bf16[32,64,128]{2,1,0:T(8,128)(2,1)S(1)}, bf16[32,64,128]{2,1,0:T(8,128)(2,1)}, u32[]{:S(2)}, u32[]{:S(2)}) collective-permute-start(bf16[32,64,128]{2,1,0:T(8,128)(2,1)S(1)} %all-to-all-done), channel_id=1, source_target_pairs={{0,224},{1,225},{2,226},{3,227},{4,228},{5,229},{6,230},{7,231},{8... | collective-permute-start | bytes 1572872 | tf_op jit(solution)/shard_map/weights_neighbours/ppermute | solution.py:41
  100.5 19.5 %copy-start.11 = (bf16[2,3,24,512]{3,2,1,0:T(8,128)(2,1)S(1)}, bf16[2,3,24,512]{3,2,1,0:T(8,128)(2,1)}, u32[]{:S(2)}) copy-start(bf16[2,3,24,512]{3,2,1,0:T(8,128)(2,1)} %get-tuple-element.115) | copy-start | bytes 442372
  100.5 31.1 %copy-start.10 = (bf16[2,3,24,512]{3,2,1,0:T(8,128)(2,1)S(1)}, bf16[2,3,24,512]{3,2,1,0:T(8,128)(2,1)}, u32[]{:S(2)}) copy-start(bf16[2,3,24,512]{3,2,1,0:T(8,128)(2,1)} %get-tuple-element.116) | copy-start | bytes 442372
  100.5 38.9 %copy-start.13 = (bf16[2,3,12,512]{3,2,1,0:T(8,128)(2,1)S(1)}, bf16[2,3,12,512]{3,2,1,0:T(8,128)(2,1)}, u32[]{:S(2)}) copy-start(bf16[2,3,12,512]{3,2,1,0:T(8,128)(2,1)} %get-tuple-element.113) | copy-start | bytes 221188
  100.5 47.7 %copy-start.12 = (bf16[2,3,12,512]{3,2,1,0:T(8,128)(2,1)S(1)}, bf16[2,3,12,512]{3,2,1,0:T(8,128)(2,1)}, u32[]{:S(2)}) copy-start(bf16[2,3,12,512]{3,2,1,0:T(8,128)(2,1)} %get-tuple-element.114) | copy-start | bytes 221188
  114.3 19.2 %all-to-all-start.2 = ((bf16[16,48,128]{2,1,0:T(8,128)(2,1)}), bf16[16,48,128]{2,1,0:T(8,128)(2,1)S(1)}, u32[]{:S(2)}, u32[]{:S(2)}) async-start(bf16[16,48,128]{2,1,0:T(8,128)(2,1)} %sum_parts.2), calls=%async_computation.2 | async-start | bytes 393216 | tf_op jit(solution)/shard_map/adapter_sum/all_to_all | solution.py:449
  120.0 36.3 %collective-permute-start.12 = (bf16[2,3,24,512]{3,2,1,0:T(8,128)(2,1)S(1)}, bf16[2,3,24,512]{3,2,1,0:T(8,128)(2,1)S(1)}, u32[]{:S(2)}, u32[]{:S(2)}) collective-permute-start(bf16[2,3,24,512]{3,2,1,0:T(8,128)(2,1)S(1)} %copy-done.11), channel_id=1, source_target_pairs={{0,272},{1,273},{2,274},{3,275},{4,276},{5,277},{6,278},{7,279},{8... | collective-permute-start | bytes 442376 | tf_op jit(solution)/shard_map/hand_over/ppermute | solution.py:440
  131.6 24.7 %collective-permute-start.13 = (bf16[2,3,24,512]{3,2,1,0:T(8,128)(2,1)S(1)}, bf16[2,3,24,512]{3,2,1,0:T(8,128)(2,1)S(1)}, u32[]{:S(2)}, u32[]{:S(2)}) collective-permute-start(bf16[2,3,24,512]{3,2,1,0:T(8,128)(2,1)S(1)} %copy-done.10), channel_id=1, source_target_pairs={{0,256},{1,257},{2,258},{3,259},{4,260},{5,261},{6,262},{7,263},{8... | collective-permute-start | bytes 442376 | tf_op jit(solution)/shard_map/hand_over/ppermute | solution.py:440
  133.5 0.7 copy-start.6
  135.8 21.4 %all-to-all-start.3 = ((bf16[16,48,128]{2,1,0:T(8,128)(2,1)}), bf16[16,48,128]{2,1,0:T(8,128)(2,1)S(1)}, u32[]{:S(2)}, u32[]{:S(2)}) async-start(bf16[16,48,128]{2,1,0:T(8,128)(2,1)} %sum_parts.3), calls=%async_computation.3 | async-start | bytes 393216 | tf_op jit(solution)/shard_map/adapter_sum/all_to_all | solution.py:450
  139.4 12.5 %collective-permute-start.10 = (bf16[2,3,12,512]{3,2,1,0:T(8,128)(2,1)S(1)}, bf16[2,3,12,512]{3,2,1,0:T(8,128)(2,1)S(1)}, u32[]{:S(2)}, u32[]{:S(2)}) collective-permute-start(bf16[2,3,12,512]{3,2,1,0:T(8,128)(2,1)S(1)} %copy-done.13), channel_id=1, source_target_pairs={{0,273},{1,274},{2,275},{3,276},{4,277},{5,278},{6,279},{7,280},{8... | collective-permute-start | bytes 221192 | tf_op jit(solution)/shard_map/hand_over/ppermute | solution.py:440
  148.3 8.0 %collective-permute-start.11 = (bf16[2,3,12,512]{3,2,1,0:T(8,128)(2,1)S(1)}, bf16[2,3,12,512]{3,2,1,0:T(8,128)(2,1)S(1)}, u32[]{:S(2)}, u32[]{:S(2)}) collective-permute-start(bf16[2,3,12,512]{3,2,1,0:T(8,128)(2,1)S(1)} %copy-done.12), channel_id=1, source_target_pairs={{0,257},{1,258},{2,259},{3,260},{4,261},{5,262},{6,263},{7,264},{8... | collective-permute-start | bytes 221192 | tf_op jit(solution)/shard_map/hand_over/ppermute | solution.py:440

commit v2 on v1

--- a/solution.py
+++ b/solution.py
@@ -51,6 +51,23 @@
 
 def tn(a, b):
     return lax.dot_general(a, b, (((0,), (0,)), ((), ())), preferred_element_type=F32)
+
+
+def pack_kernel(place_ref, qs_ref, ps_ref, qd_ref, pd_ref, out_ref):
+    @pl.when(place_ref[2] == 0)
+    def _():
+        out_ref[0, 0:32, 0:96] = qs_ref[...]
+        out_ref[0, 0:32, 96:128] = ps_ref[...].astype(F32).T.astype(BF)
+        out_ref[0, 32:64, :] = jnp.zeros((32, 128), BF)
+
+    @pl.when(place_ref[2] == 1)
+    def _():
+        out_ref[0, :, 0:96] = qd_ref[...]
+        out_ref[0, :, 96:128] = pd_ref[...].astype(F32).T.astype(BF)
+
+    own = out_ref[0]
+    for i in range(1, 32):
+        out_ref[i] = own
 
 
 def window_row(shape, dim):
@@ -131,33 +148,110 @@
     return jnp.where(hit, 1.0, 0.0).astype(BF)
 
 
+def sizes(deep):
+    features, rank, windows = (1024, 24, 1) if deep else (512, 32, 2)
+    counts = (features * rank // 128, rank * 12, 512 * rank // 128, rank * features // 128)
+    starts = (0, counts[0], sum(counts[:2]), sum(counts[:3]))
+    return features, rank, windows, counts, starts
+
+
+def by_half(deep, ref):
+    return jnp.concatenate([ref[0:WT], ref[WT : 2 * WT]], 1) if deep else ref[...]
+
+
+def prep_kernel(
+    deep,
+    x_ref, c_ref, s1_ref, s2_ref, s3_ref, adapter_ref,
+    normed_ref, cot_ref, scale_ref, low_q_ref, low_c_ref, aq_ref, bq_ref, ap_ref,
+    xs, cols, aq_s, ap_s, bq_s, bp_s,
+):
+    features, rank, windows, counts, starts = sizes(deep)
+    wide_row = 384 if deep else 128
+    steps, per = wide_row // rank, wide_row // 128
+
+    for i, dest in ((0, aq_s), (2, ap_s)):
+        n = counts[i] // per
+        parts = [adapter_ref[pl.ds(starts[i] + c, n, stride=per), :] for c in range(per)]
+        packed = jnp.concatenate(parts, 1) if per > 1 else parts[0]
+        packed = packed.astype(BF)
+        for k in range(steps):
+            dest[pl.ds(k, n, stride=steps), :] = nn(packed, selector((wide_row, 128), rank, k))
+    if rank < 32:
+        bq_s[...] = jnp.zeros_like(bq_s)
+        bp_s[...] = jnp.zeros_like(bp_s)
+    for c in range(12):
+        bq_s[0:rank, 128 * c : 128 * c + 128] = adapter_ref[
+            pl.ds(starts[1] + c, rank, stride=12), :
+        ]
+    for c in range(features // 128):
+        bp_s[0:rank, 128 * c : 128 * c + 128] = adapter_ref[
+            pl.ds(starts[3] + c, rank, stride=features // 128), :
+        ]
+    a_qkv = aq_s[0:features, 0:32].astype(BF)
+    aq_ref[0:features] = a_qkv
+    bq_ref[...] = bq_s[...].astype(BF)
+    ap_ref[...] = ap_s[:, 0:32].astype(BF)
+    b_proj = bp_s[:, 0:features].astype(BF)
+
+    for source, which in ((c_ref, 1), (x_ref, 0)):
+        for level in range(2):
+            for row in range(6):
+                if row < 3:
+                    own = source[level, row + 3].astype(F32)
+                else:
+                    own = s1_ref[which, level, row - 3].astype(F32)
+                strip = s2_ref if row < 3 else s3_ref
+                side = strip[which, level, row % 3].astype(F32)
+                at = 72 * level + 12 * row
+                if deep:
+                    for c in range(4):
+                        lanes = slice(128 * c, 128 * c + 128)
+                        cols[c, 0:12] = own[12:24, lanes]
+                        cols[c, 12:24] = side[:, lanes]
+                        for odd in range(2):
+                            to = WT * odd + at
+                            xs[to : to + 12, lanes] = cols[c, pl.ds(odd, 12, stride=2), :]
+                else:
+                    xs[at : at + 12, :] = own[6:18]
+                    xs[at + 144 : at + 150, :] = own[18:24]
+                    xs[at + 150 : at + 156, :] = side[0:6]
+        if which == 1:
+            cot_ref[...] = xs[...].astype(BF)
+    x = by_half(deep, xs)
+    centred = x - jnp.mean(x, axis=1, keepdims=True)
+    scale = lax.rsqrt(jnp.mean(centred * centred, axis=1, keepdims=True) + EPSILON)
+    normed = (centred * scale).astype(BF)
+    if deep:
+        normed_ref[0:WT] = normed[:, 0:512]
+        normed_ref[WT : 2 * WT] = normed[:, 512:1024]
+    else:
+        normed_ref[...] = normed
+    tokens = WT * windows
+    scale_ref[0:tokens] = jnp.broadcast_to(scale, (tokens, 128))
+    low_q_ref[0:tokens] = nn(normed, a_qkv).astype(BF)
+    low_c_ref[0:tokens] = nt(by_half(deep, cot_ref), b_proj).astype(BF)
+
+
 def block_kernel(
     deep,
-    place_ref, p0, p1, p2, p3, p4a, p4b, p5, p6, p7,
-    x_ref, c_ref, s1_ref, s2_ref, bias_ref, allowed_ref, adapter_ref,
+    place_ref, p0, p1, p2, p3, p4, p5, p6, p7, bias_ref, allowed_ref,
+    normed_ref, cot_ref, scale_ref, low_q_ref, low_c_ref, aq_ref, bq_ref, ap_ref,
     own_ref, side_ref, below_ref, corner_ref, grads_ref,
-    weight, weight_p, xs, cs, cols, aq_s, ap_s, bq_s, bp_s, flat,
+    weight, weight_p, xs, cols, aq_s, ap_s, flat,
 ):
-    features = 1024 if deep else 512
-    rank = 24 if deep else 32
-    windows = 1 if deep else 2
+    features, rank, windows, counts, starts = sizes(deep)
+    wide_row = 384 if deep else 128
+    steps, per = wide_row // rank, wide_row // 128
     tokens = WT * windows
     block = features // 16
-    lanes_a = 384 if deep else 128
-    strides = lanes_a // rank
 
     label = place_ref[1]
-    for o, piece in enumerate((p0, p1, p2, p3, (p4a, p4b), p5, p6, p7)):
+    for o, piece in enumerate((p0, p1, p2, p3, p4, p5, p6, p7)):
         for j in range(16):
             for h in range(2):
                 y = lax.rem(label + o - 4 * h - 2 * (j // 8) - 3 * (j % 8) + 64, 8)
                 at = pl.multiple_of((2 * y + h) * block, block)
-                k = 2 * j + h
-                if o == 4:
-                    source = piece[0][k, :block] if k < 16 else piece[1][k - 16, :block]
-                else:
-                    source = piece[k, :block]
-                weight[pl.ds(at, block), 128 * j : 128 * j + 128] = source
+                weight[pl.ds(at, block), 128 * j : 128 * j + 128] = piece[2 * j + h, :block]
     quarter = lax.broadcasted_iota(jnp.int32, (block, 128), 1) // 32
     for j in range(16):
         for m in range(4):
@@ -170,62 +264,13 @@
                 tile = jnp.where(quarter == k, part, tile)
             weight_p[block * j : block * j + block, 128 * m : 128 * m + 128] = tile.astype(BF)
 
-    n_aq, n_bq = features * rank // 128, rank * 12
-    n_ap, n_bp = 512 * rank // 128, rank * features // 128
-    off_bq, off_ap, off_bp = n_aq, n_aq + n_bq, n_aq + n_bq + n_ap
-    per = lanes_a // 128
-    for off, rows, dest in ((0, n_aq, aq_s), (off_ap, n_ap, ap_s)):
-        parts = [adapter_ref[pl.ds(off + c, rows // per, stride=per), :] for c in range(per)]
-        packed = jnp.concatenate(parts, 1) if per > 1 else parts[0]
-        packed = packed.astype(BF)
-        for k in range(strides):
-            dest[pl.ds(k, rows // per, stride=strides), :] = nn(packed, selector((lanes_a, 128), rank, k))
-    if rank < 32:
-        bq_s[...] = jnp.zeros_like(bq_s)
-        bp_s[...] = jnp.zeros_like(bp_s)
-    for c in range(12):
-        bq_s[0:rank, 128 * c : 128 * c + 128] = adapter_ref[pl.ds(off_bq + c, rank, stride=12), :]
-    for c in range(features // 128):
-        bp_s[0:rank, 128 * c : 128 * c + 128] = adapter_ref[
-            pl.ds(off_bp + c, rank, stride=features // 128), :
-        ]
-    a_qkv, b_qkv = aq_s[:, 0:32].astype(BF), bq_s[...].astype(BF)
-    a_proj, b_proj = ap_s[:, 0:32].astype(BF), bp_s[...].astype(BF)
-
-    for source, which, dest in ((x_ref, 0, xs), (c_ref, 1, cs)):
-        for level in range(2):
-            for row in range(6):
-                if row < 3:
-                    own = source[level, row + 3].astype(F32)
-                else:
-                    own = s1_ref[which, level, row - 3].astype(F32)
-                side = s2_ref[which, level, row].astype(F32)
-                at = 72 * level + 12 * row
-                if deep:
-                    for c in range(4):
-                        lanes = slice(128 * c, 128 * c + 128)
-                        cols[c, 0:12] = own[12:24, lanes]
-                        cols[c, 12:24] = side[:, lanes]
-                        for odd in range(2):
-                            to = 512 * odd + 128 * c
-                            dest[at : at + 12, to : to + 128] = cols[c, pl.ds(odd, 12, stride=2), :]
-                else:
-                    dest[at : at + 12, :] = own[6:18]
-                    dest[at + 144 : at + 150, :] = own[18:24]
-                    dest[at + 150 : at + 156, :] = side[0:6]
-
-    x = xs[...]
-    cot = cs[...]
-    cot_b = cot.astype(BF)
-    centred = x - jnp.mean(x, axis=1, keepdims=True)
-    scale = lax.rsqrt(jnp.mean(centred * centred, axis=1, keepdims=True) + EPSILON)
-    xhat = centred * scale
-    normed = xhat.astype(BF)
-    low_q = nn(normed, a_qkv).astype(BF)
+    normed = by_half(deep, normed_ref)
+    cot_b = by_half(deep, cot_ref)
+    low_q, low_c = low_q_ref[0:tokens], low_c_ref[0:tokens]
+    a_qkv, b_qkv, a_proj = aq_ref[0:features], bq_ref[...], ap_ref[...]
     chunks = compact(nn(normed, weight[...]))
     low = nn(low_q, b_qkv)
     chunks = [chunks[c] + low[:, 128 * c : 128 * c + 128] for c in range(12)]
-    low_c = nt(cot_b, b_proj).astype(BF)
     d_mixed = nn(cot_b, weight_p[...]) + nt(low_c, a_proj)
 
     lane = lax.broadcasted_iota(jnp.int32, (WT, 128), 1)
@@ -270,25 +315,28 @@
     back = nt(d_proj, b_qkv).astype(BF)
     d_wide = joined(expand(d_chunks), 1)
     d_n = nt(d_wide, weight[...]) + nt(back, a_qkv)
+    xhat = normed.astype(F32)
     mean_1 = jnp.mean(d_n, axis=1, keepdims=True)
     mean_2 = jnp.mean(d_n * xhat, axis=1, keepdims=True)
-    xs[...] = cot + scale * (d_n - mean_1 - xhat * mean_2)
+    scale = scale_ref[0:tokens, 0:1]
+    xs[...] = cot_b.astype(F32) + scale * (d_n - mean_1 - xhat * mean_2)
 
     aq_s[:, 0:32] = tn(normed, back)
     ap_s[:, 0:32] = tn(mixed, low_c)
     d_bq = tn(low_q, d_proj)
     d_bp = tn(low_m, cot_b)
-    for off, rows, source in ((0, n_aq, aq_s), (off_ap, n_ap, ap_s)):
-        total = jnp.zeros((rows // per, lanes_a), F32)
-        for k in range(strides):
-            part = source[pl.ds(k, rows // per, stride=strides), :][:, 0:32].astype(BF)
-            total = total + nn(part, selector((32, lanes_a), rank, k))
+    for i, source in ((0, aq_s), (2, ap_s)):
+        n = counts[i] // per
+        total = jnp.zeros((n, wide_row), F32)
+        for k in range(steps):
+            part = source[pl.ds(k, n, stride=steps), :][:, 0:32].astype(BF)
+            total = total + nn(part, selector((32, wide_row), rank, k))
         for c in range(per):
-            flat[pl.ds(off + c, rows // per, stride=per), :] = total[:, 128 * c : 128 * c + 128]
+            flat[pl.ds(starts[i] + c, n, stride=per), :] = total[:, 128 * c : 128 * c + 128]
     for c in range(12):
-        flat[pl.ds(off_bq + c, rank, stride=12), :] = d_bq[0:rank, 128 * c : 128 * c + 128]
+        flat[pl.ds(starts[1] + c, rank, stride=12), :] = d_bq[0:rank, 128 * c : 128 * c + 128]
     for c in range(features // 128):
-        flat[pl.ds(off_bp + c, rank, stride=features // 128), :] = d_bp[
+        flat[pl.ds(starts[3] + c, rank, stride=features // 128), :] = d_bp[
             0:rank, 128 * c : 128 * c + 128
         ]
     grads_ref[...] = flat[...].astype(BF)
@@ -316,31 +364,53 @@
                     strip[level, row % 3, :, lanes] = whole[0:12]
 
 
-def run_block(deep, operands):
+VMEM = pl.BlockSpec(memory_space=pltpu.VMEM)
+SMEM = pl.BlockSpec(memory_space=pltpu.SMEM)
+
+
+def run_prep(deep, operands):
     features = 1024 if deep else 512
-    tokens = WT if deep else 2 * WT
-    spec = pl.BlockSpec(memory_space=pltpu.VMEM)
+    shapes = (
+        ((2 * WT, 512), BF), ((2 * WT, 512), BF), ((2 * WT, 128), F32), ((2 * WT, 32), BF),
+        ((2 * WT, 32), BF), ((1024, 32), BF), ((32, QKV), BF), ((512, 32), BF),
+    )
     return pl.pallas_call(
-        functools.partial(block_kernel, deep),
-        out_shape=(
-            jax.ShapeDtypeStruct((2, 3, 24, 512), BF),
-            jax.ShapeDtypeStruct((2, 3, 12, 512), BF),
-            jax.ShapeDtypeStruct((2, 3, 24, 512), BF),
-            jax.ShapeDtypeStruct((2, 3, 12, 512), BF),
-            jax.ShapeDtypeStruct((768, 128), BF),
-        ),
-        in_specs=[pl.BlockSpec(memory_space=pltpu.SMEM)] + [spec] * (len(operands) - 1),
-        out_specs=(spec,) * 5,
+        functools.partial(prep_kernel, deep),
+        out_shape=tuple(jax.ShapeDtypeStruct(*shape) for shape in shapes),
+        in_specs=[VMEM] * len(operands),
+        out_specs=(VMEM,) * len(shapes),
         scratch_shapes=[
-            pltpu.VMEM((features, 2048), BF),
-            pltpu.VMEM((features, 512), BF),
-            pltpu.VMEM((tokens, features), F32),
-            pltpu.VMEM((tokens, features), F32),
+            pltpu.VMEM((2 * WT, 512), F32),
             pltpu.VMEM((4, 24, 128), F32),
             pltpu.VMEM((features, 128), F32),
             pltpu.VMEM((512, 128), F32),
             pltpu.VMEM((32, QKV), F32),
             pltpu.VMEM((32, features), F32),
+        ],
+        compiler_params=pltpu.CompilerParams(vmem_limit_bytes=32 * 1024 * 1024),
+        name="deep_prep" if deep else "shallow_prep",
+    )(*operands)
+
+
+def run_block(deep, operands):
+    features = 1024 if deep else 512
+    tokens = WT if deep else 2 * WT
+    shapes = (
+        ((2, 3, 24, 512), BF), ((2, 3, 12, 512), BF), ((2, 3, 24, 512), BF),
+        ((2, 3, 12, 512), BF), ((768, 128), BF),
+    )
+    return pl.pallas_call(
+        functools.partial(block_kernel, deep),
+        out_shape=tuple(jax.ShapeDtypeStruct(*shape) for shape in shapes),
+        in_specs=[SMEM] + [VMEM] * (len(operands) - 1),
+        out_specs=(VMEM,) * 5,
+        scratch_shapes=[
+            pltpu.VMEM((features, 2048), BF),
+            pltpu.VMEM((features, 512), BF),
+            pltpu.VMEM((tokens, features), F32),
+            pltpu.VMEM((4, 24, 128), F32),
+            pltpu.VMEM((features, 128), F32),
+            pltpu.VMEM((512, 128), F32),
             pltpu.VMEM((768, 128), F32),
         ],
         compiler_params=pltpu.CompilerParams(vmem_limit_bytes=56 * 1024 * 1024),
@@ -365,6 +435,24 @@
     )(parts)
 
 
+def hand(value, d_lat, d_lon):
+    route = []
+    for s in range(2):
+        for a in range(16):
+            for b in range(16):
+                to = (1 - s) * 256 + (a + d_lat) % 16 * 16 + (b + d_lon) % 16
+                route.append((s * 256 + a * 16 + b, to))
+    return lax.ppermute(value, ("segment", "lat", "lon"), route)
+
+
+def shift(value, d_lat, d_lon):
+    route = []
+    for a in range(16):
+        for b in range(16):
+            route.append((a * 16 + b, (a + d_lat) % 16 * 16 + (b + d_lon) % 16))
+    return lax.ppermute(value, BOTH, route)
+
+
 def shards(
     saved_inputs, cotangent, pole_mask, bias_index, table_shallow, table_deep,
     qkv_shallow, proj_shallow, qkv_deep, proj_deep, adapters,
@@ -374,76 +462,63 @@
     lon = lax.axis_index("lon")
     x, cot = saved_inputs[0], cotangent[0]
 
+    label = (4 * (lat % 2) + 2 * (lon // 8) + lat // 2 + 3 * (lon % 8)) % 8
+    place = jnp.stack([lat, label, segment]).astype(jnp.int32)
     with jax.named_scope("pack"):
-        shallow_w = jnp.concatenate([qkv_shallow, proj_shallow.T], 1)
-        deep_w = jnp.concatenate([qkv_deep, proj_deep.T], 1)
-        own_w = jnp.where(segment == 1, deep_w, jnp.pad(shallow_w, ((0, 32), (0, 0))))
-        own_w = jnp.broadcast_to(own_w[None], (32, 64, 128))
-    with jax.named_scope("halo_rows"):
-        top = jnp.stack([x[:, :3], cot[:, :3]])
-        s1 = lax.ppermute(top, "lat", [((i + 1) % 16, i) for i in range(16)])
+        own_w = pl.pallas_call(
+            pack_kernel,
+            out_shape=jax.ShapeDtypeStruct((32, 64, 128), BF),
+            in_specs=[SMEM] + [VMEM] * 4,
+            out_specs=VMEM,
+            name="pack_weights",
+        )(place, qkv_shallow, proj_shallow, qkv_deep, proj_deep)
     with jax.named_scope("weights_class"):
         piece = lax.all_to_all(own_w, BOTH, 0, 0, axis_index_groups=class_groups())
-    with jax.named_scope("halo_columns"):
-        left = jnp.stack([x[:, 3:, :12], cot[:, 3:, :12]])
-        left = jnp.concatenate([left, s1[:, :, :, :12]], 2)
-        s2 = lax.ppermute(left, "lon", [((i + 1) % 16, i) for i in range(16)])
+    with jax.named_scope("halos"):
+        s1 = shift(jnp.stack([x[:, :3], cot[:, :3]]), -1, 0)
+        s2 = shift(jnp.stack([x[:, 3:, :12], cot[:, 3:, :12]]), 0, -1)
+        s3 = shift(jnp.stack([x[:, :3, :12], cot[:, :3, :12]]), -1, -1)
+    with jax.named_scope("prep"):
+        prep = lax.cond(
+            segment == 0,
+            functools.partial(run_prep, False),
+            functools.partial(run_prep, True),
+            (x, cot, s1, s2, s3, adapters.reshape(768, 128)),
+        )
+        piece, prep = lax.optimization_barrier((piece, prep))
     with jax.named_scope("weights_neighbours"):
+        p4 = neighbour_send(piece, 0, 1, 1)
         p6 = neighbour_send(piece, 1, 0, 0)
         p2 = neighbour_send(piece, -1, 0, 0)
         p7 = neighbour_send(piece, 0, 1, 0)
         p1 = neighbour_send(piece, 0, -1, 0)
         p5 = neighbour_send(piece, 0, 0, 1)
         p3 = neighbour_send(piece, 0, 0, -1)
-        p4a = neighbour_send(piece[:16], 0, 1, 1)
-        p4b = neighbour_send(piece[16:], 0, -1, -1)
 
     with jax.named_scope("bias"):
-        label = (4 * (lat % 2) + 2 * (lon // 8) + lat // 2 + 3 * (lon % 8)) % 8
-        place = jnp.stack([lat, label]).astype(jnp.int32)
         table = jnp.where(segment == 1, table_deep, table_shallow)
         table = jnp.pad(table.T, ((0, 0), (0, 768 - table.shape[0])))
         index = jnp.pad(bias_index.T, ((0, 0), (0, 256 - WT)))
-        smem = pl.BlockSpec(memory_space=pltpu.SMEM)
-        vmem = pl.BlockSpec(memory_space=pltpu.VMEM)
         bias, allowed = pl.pallas_call(
             bias_kernel,
             out_shape=(
                 jax.ShapeDtypeStruct((HEADS, WT, 256), F32),
                 jax.ShapeDtypeStruct((WT, 256), F32),
             ),
-            in_specs=[smem, smem, vmem, vmem],
-            out_specs=(vmem, vmem),
+            in_specs=[SMEM, SMEM, VMEM, VMEM],
+            out_specs=(VMEM, VMEM),
             name="bias_table",
         )(place, pole_mask, index, table)
-
-    flat = adapters.reshape(768, 128)
-    operands = (
-        place, piece, p1, p2, p3, p4a, p4b, p5, p6, p7, x, cot, s1, s2, bias, allowed, flat,
-    )
     own, side, below, corner, grads = lax.cond(
         segment == 0,
         functools.partial(run_block, False),
         functools.partial(run_block, True),
-        operands,
+        (place, piece, p1, p2, p3, p4, p5, p6, p7, bias, allowed, *prep),
     )
 
-    every = ("segment", "lat", "lon")
-
-    def hand(value, d_lat, d_lon):
-        route = []
-        for s in range(2):
-            for a in range(16):
-                for b in range(16):
-                    to = (1 - s) * 256 + (a + d_lat) % 16 * 16 + (b + d_lon) % 16
-                    route.append((s * 256 + a * 16 + b, to))
-        return lax.ppermute(value, every, route)
-
     with jax.named_scope("hand_over"):
-        own = hand(own, 0, 0)
-        side = hand(side, 0, 1)
-        below = hand(below, 1, 0)
-        corner = hand(corner, 1, 1)
+        own, side = hand(own, 0, 0), hand(side, 0, 1)
+        below, corner = hand(below, 1, 0), hand(corner, 1, 1)
     with jax.named_scope("adapter_sum"):
         grads = lax.all_to_all(grads.reshape(16, 48, 128), "lon", 0, 0)
         grads = lax.all_to_all(summed(grads), "lat", 0, 0)

time: 159 us -> 155 us (0.975)
  waiting for transfers between devices: 24.6 us -> 17.2 us
  blocking collectives: 12.2 us -> 17.2 us
  Pallas kernels: 22 us -> 24.6 us
  local copies, waits for them, and re-layouts: 4.74 us -> 2.16 us
    ppermute x6 -> x7, starting transfers between devices: 34.8 us -> 40 us  [the longest x4 24.1 us: hand(): return lax.ppermute(value, ('segment', 'lat', 'lon'), route)]
    all_to_all x1, blocking collectives: 12.2 us -> 17.2 us  [shards(): grads = lax.all_to_all(grads.reshape(16, 48, 128), 'lon', 0, 0)]
    ppermute x8 -> x7, starting transfers between devices: 28.5 us -> 23.7 us  [neighbour_send(): return lax.ppermute(value, BOTH, route)]
    ppermute x6 -> x7, waiting for transfers between devices: 19.9 us -> 15.3 us  [the longest x3 9.22 us: shift(): return lax.ppermute(value, BOTH, route)]
    all_to_all x1, waiting for transfers between devices: 3.54 us -> 0.01 us  [shards(): piece = lax.all_to_all(own_w, BOTH, 0, 0, axis_index_groups=class_groups())]
    pallas_call x1 -> x3, Pallas kernels: 12.3 us -> 14.8 us  [the longest x1 10.9 us: run_block(): pl.pallas_call(functools.partial(block_kernel, deep), out_shape=tuple((ja...]
  transfers between devices with their start and end apart: 17 -> 17, of which waited for: 6 -> 6; matrix products, arithmetic and copies ran while one was open for 2% -> 2% of each run, Pallas kernels for 5% -> 7%
where the time goes in v2:
time: 155 us; the launch traced here: 154 us
  starting transfers between devices  89.9 us (58%)
  Pallas kernels  24.6 us (16%)
  waiting for transfers between devices  17.2 us (11%)
  blocking collectives  17.2 us (11%)
  local copies, waits for them, and re-layouts  2.16 us (1%)
  other arithmetic  1.83 us (1%)
    ppermute x4, starting transfers between devices, hand(): return lax.ppermute(value, ('segment', 'lat', 'lon'), route)  24.1 us
    ppermute x7, starting transfers between devices, neighbour_send(): return lax.ppermute(value, BOTH, route)  23.7 us
    all_to_all x1, starting transfers between devices, shards(): piece = lax.all_to_all(own_w, BOTH, 0, 0, axis_index_groups=class_groups())  18.2 us
    all_to_all x1, blocking collectives, shards(): grads = lax.all_to_all(grads.reshape(16, 48, 128), 'lon', 0, 0)  17.2 us
    ppermute x3, starting transfers between devices, shift(): return lax.ppermute(value, BOTH, route)  15.9 us
    pallas_call x1, Pallas kernels, run_block(): pl.pallas_call(functools.partial(block_kernel, deep), out_shape=tuple((ja...  10.9 us
    ppermute x3, waiting for transfers between devices, shift(): return lax.ppermute(value, BOTH, route)  9.22 us
    pallas_call x1, Pallas kernels, shards(): pl.pallas_call(bias_kernel, out_shape=(jax.ShapeDtypeStruct((HEADS, WT, 2...  6.48 us
  transfers between devices with their start and end apart: 17, of which 6 were waited for; matrix products, arithmetic and copies ran while one was open for 2% of the time, Pallas kernels for 7%

profile of v2, /device:TPU:1, one launch (start us, length us, event | category | flops | bytes accessed | tf_op | source)
XLA Modules:
  0.0 154.1 jit_solution(7596462910560152186)
XLA Ops:
  0.7 0.1 pad_add_fusion.place_ref
  0.8 1.9 %pack_weights.1 = bf16[32,64,128]{2,1,0:T(8,128)(2,1)} custom-call(s32[3]{0:T(128)S(1)} %pad_add_fusion.place_ref, bf16[32,96]{1,0:T(8,128)(2,1)} %qs_ref.1, bf16[32,32]{1,0:T(8,128)(2,1)} %ps_ref.1, bf16[64,96]{1,0:T(8,128)(2,1)} %qd_ref.1, bf16[32,64]{1,0:T(8,128)(2,1)} %pd_ref.1), custom_call_target="tpu_custom_call" | custom-call | tf_op jit(solution)/shard_map/pack/pack_weights/pallas_call | solution.py:468
  2.7 18.2 %all-to-all-start = ((bf16[32,64,128]{2,1,0:T(8,128)(2,1)}), bf16[32,64,128]{2,1,0:T(8,128)(2,1)S(1)}, u32[]{:S(2)}, u32[]{:S(2)}) async-start(bf16[32,64,128]{2,1,0:T(8,128)(2,1)} %pack_weights.1), calls=%async_computation | async-start | bytes 1048576 | tf_op jit(solution)/shard_map/weights_class/all_to_all | solution.py:476
  20.9 0.0 copy-start.2
  20.9 7.8 %collective-permute-start = (bf16[2,2,3,24,512]{4,3,2,1,0:T(8,128)(2,1)S(1)}, bf16[2,2,3,24,512]{4,3,2,1,0:T(8,128)(2,1)S(1)}, u32[]{:S(2)}, u32[]{:S(2)}) collective-permute-start(bf16[2,2,3,24,512]{4,3,2,1,0:T(8,128)(2,1)S(1)} %pad_maximum_fusion), channel_id=1, source_target_pairs={{0,240},{1,241},{2,242},{3,243},{4,244},{5,245},{6,246},{7,247},{8... | collective-permute-start | bytes 884744 | tf_op jit(solution)/shard_map/halos/ppermute | solution.py:453
  28.8 4.3 %collective-permute-start.1 = (bf16[2,2,3,12,512]{4,3,2,1,0:T(8,128)(2,1)S(1)}, bf16[2,2,3,12,512]{4,3,2,1,0:T(8,128)(2,1)S(1)}, u32[]{:S(2)}, u32[]{:S(2)}) collective-permute-start(bf16[2,2,3,12,512]{4,3,2,1,0:T(8,128)(2,1)S(1)} %pad_maximum_fusion.1), channel_id=1, source_target_pairs={{0,15},{1,0},{2,1},{3,2},{4,3},{5,4},{6,5},{7,6},{8,7},{9,8},{10,9... | collective-permute-start | bytes 442376 | tf_op jit(solution)/shard_map/halos/ppermute | solution.py:453
  33.1 3.8 %collective-permute-start.2 = (bf16[2,2,3,12,512]{4,3,2,1,0:T(8,128)(2,1)S(1)}, bf16[2,2,3,12,512]{4,3,2,1,0:T(8,128)(2,1)S(1)}, u32[]{:S(2)}, u32[]{:S(2)}) collective-permute-start(bf16[2,2,3,12,512]{4,3,2,1,0:T(8,128)(2,1)S(1)} %pad_maximum_fusion.2), channel_id=1, source_target_pairs={{0,255},{1,240},{2,241},{3,242},{4,243},{5,244},{6,245},{7,246},{8... | collective-permute-start | bytes 442376 | tf_op jit(solution)/shard_map/halos/ppermute | solution.py:453
  36.9 3.6 %collective-permute-done.1 = bf16[2,2,3,12,512]{4,3,2,1,0:T(8,128)(2,1)S(1)} collective-permute-done((bf16[2,2,3,12,512]{4,3,2,1,0:T(8,128)(2,1)S(1)}, bf16[2,2,3,12,512]{4,3,2,1,0:T(8,128)(2,1)S(1)}, u32[]{:S(2)}, u32[]{:S(2)}) %collective-permute-start.1) | collective-permute-done | bytes 147488 | tf_op jit(solution)/shard_map/halos/ppermute | solution.py:453
  40.5 5.6 %collective-permute-done.2 = bf16[2,2,3,12,512]{4,3,2,1,0:T(8,128)(2,1)S(1)} collective-permute-done((bf16[2,2,3,12,512]{4,3,2,1,0:T(8,128)(2,1)S(1)}, bf16[2,2,3,12,512]{4,3,2,1,0:T(8,128)(2,1)S(1)}, u32[]{:S(2)}, u32[]{:S(2)}) %collective-permute-start.2) | collective-permute-done | bytes 147488 | tf_op jit(solution)/shard_map/halos/ppermute | solution.py:453
  46.2 0.0 collective-permute-done
  46.2 0.0 copy-start.5
  46.2 0.0 copy-start.6
  46.2 2.0 %conditional.2 = ((bf16[288,512]{1,0:T(8,128)(2,1)}, bf16[288,512]{1,0:T(8,128)(2,1)}, f32[288,128]{1,0:T(8,128)}, bf16[288,32]{1,0:T(8,128)(2,1)}, bf16[288,32]...) conditional(s32[]{:T(128)} %convert_element_type.5, ...), branch_computations={%region_0.1_spmd, %region_1.2_spmd} | conditional | bytes 8 | solution.py:482
  46.2 2.0 %deep_prep.1 = (bf16[288,512]{1,0:T(8,128)(2,1)}, bf16[288,512]{1,0:T(8,128)(2,1)}, f32[288,128]{1,0:T(8,128)}, bf16[288,32]{1,0:T(8,128)(2,1)}, bf16[288,32]{1,...) custom-call(bf16[2,6,24,512]{3,2,1,0:T(8,128)(2,1)S(1)} %get-tuple-element.100.x_re, ...), custom_call_target="tpu_custom_call" | custom-call | tf_op jit(solution)/shard_map/prep/cond/branch_0_fun/deep_prep/pallas_call | solution.py:377
  48.2 0.0 all-to-all-done
  48.2 3.2 %collective-permute-start.9 = (bf16[32,64,128]{2,1,0:T(8,128)(2,1)S(1)}, bf16[32,64,128]{2,1,0:T(8,128)(2,1)S(1)}, u32[]{:S(2)}, u32[]{:S(2)}) collective-permute-start(bf16[32,64,128]{2,1,0:T(8,128)(2,1)S(1)} %all-to-all-done), channel_id=1, source_target_pairs={{0,32},{1,33},{2,34},{3,35},{4,36},{5,37},{6,38},{7,39},{8,40},{9,... | collective-permute-start | bytes 1572872 | tf_op jit(solution)/shard_map/weights_neighbours/ppermute | solution.py:41
  51.4 2.1 %collective-permute-start.8 = (bf16[32,64,128]{2,1,0:T(8,128)(2,1)S(1)}, bf16[32,64,128]{2,1,0:T(8,128)(2,1)S(1)}, u32[]{:S(2)}, u32[]{:S(2)}) collective-permute-start(bf16[32,64,128]{2,1,0:T(8,128)(2,1)S(1)} %all-to-all-done), channel_id=1, source_target_pairs={{0,8},{1,9},{2,10},{3,11},{4,12},{5,13},{6,14},{7,15},{8,16},{9,17... | collective-permute-start | bytes 1572872 | tf_op jit(solution)/shard_map/weights_neighbours/ppermute | solution.py:41
  53.5 3.7 %collective-permute-start.7 = (bf16[32,64,128]{2,1,0:T(8,128)(2,1)S(1)}, bf16[32,64,128]{2,1,0:T(8,128)(2,1)S(1)}, u32[]{:S(2)}, u32[]{:S(2)}) collective-permute-start(bf16[32,64,128]{2,1,0:T(8,128)(2,1)S(1)} %all-to-all-done), channel_id=1, source_target_pairs={{0,1},{1,2},{2,3},{3,4},{4,5},{5,6},{6,7},{7,0},{8,9},{9,10},{10,1... | collective-permute-start | bytes 1572872 | tf_op jit(solution)/shard_map/weights_neighbours/ppermute | solution.py:41
  57.2 3.3 %collective-permute-start.6 = (bf16[32,64,128]{2,1,0:T(8,128)(2,1)S(1)}, bf16[32,64,128]{2,1,0:T(8,128)(2,1)}, u32[]{:S(2)}, u32[]{:S(2)}) collective-permute-start(bf16[32,64,128]{2,1,0:T(8,128)(2,1)S(1)} %all-to-all-done), channel_id=1, source_target_pairs={{0,33},{1,34},{2,35},{3,36},{4,37},{5,38},{6,39},{7,32},{8,41},{9,... | collective-permute-start | bytes 1572872 | tf_op jit(solution)/shard_map/weights_neighbours/ppermute | solution.py:41
  60.6 3.7 %collective-permute-start.5 = (bf16[32,64,128]{2,1,0:T(8,128)(2,1)S(1)}, bf16[32,64,128]{2,1,0:T(8,128)(2,1)}, u32[]{:S(2)}, u32[]{:S(2)}) collective-permute-start(bf16[32,64,128]{2,1,0:T(8,128)(2,1)S(1)} %all-to-all-done), channel_id=1, source_target_pairs={{0,7},{1,0},{2,1},{3,2},{4,3},{5,4},{6,5},{7,6},{8,15},{9,8},{10,9... | collective-permute-start | bytes 1572872 | tf_op jit(solution)/shard_map/weights_neighbours/ppermute | solution.py:41
  64.2 0.2 collective-permute-done.9
  64.5 4.8 %collective-permute-start.4 = (bf16[32,64,128]{2,1,0:T(8,128)(2,1)S(1)}, bf16[32,64,128]{2,1,0:T(8,128)(2,1)}, u32[]{:S(2)}, u32[]{:S(2)}) collective-permute-start(bf16[32,64,128]{2,1,0:T(8,128)(2,1)S(1)} %all-to-all-done), channel_id=1, source_target_pairs={{0,24},{1,25},{2,26},{3,27},{4,28},{5,29},{6,30},{7,31},{8,0},{9,1... | collective-permute-start | bytes 1572872 | tf_op jit(solution)/shard_map/weights_neighbours/ppermute | solution.py:41
  69.3 0.0 collective-permute-done.8
  69.3 3.0 %collective-permute-start.3 = (bf16[32,64,128]{2,1,0:T(8,128)(2,1)S(1)}, bf16[32,64,128]{2,1,0:T(8,128)(2,1)}, u32[]{:S(2)}, u32[]{:S(2)}) collective-permute-start(bf16[32,64,128]{2,1,0:T(8,128)(2,1)S(1)} %all-to-all-done), channel_id=1, source_target_pairs={{0,224},{1,225},{2,226},{3,227},{4,228},{5,229},{6,230},{7,231},{8... | collective-permute-start | bytes 1572872 | tf_op jit(solution)/shard_map/weights_neighbours/ppermute | solution.py:41
  72.2 0.1 copy.13
  72.3 0.7 pad.12.index_ref
  73.0 0.6 pad.13.table_ref
  73.6 6.5 %bias_table.1 = (f32[8,144,256]{2,1,0:T(8,128)S(1)}, f32[144,256]{1,0:T(8,128)}) custom-call(s32[3]{0:T(128)S(1)} %pad_add_fusion.place_ref, s32[96]{0:T(128)} %pole_ref.1, s32[144,256]{1,0:T(8,128)} %pad.12.index_ref, f32[8,768]{1,0:T(8,128)} %pad.13.table_ref), custom_call_target="tpu_custom_call" | custom-call | tf_op jit(solution)/shard_map/bias/bias_table/pallas_call | solution.py:502
  80.1 1.6 %collective-permute-done.7 = bf16[32,64,128]{2,1,0:T(8,128)(2,1)S(1)} collective-permute-done((bf16[32,64,128]{2,1,0:T(8,128)(2,1)S(1)}, bf16[32,64,128]{2,1,0:T(8,128)(2,1)S(1)}, u32[]{:S(2)}, u32[]{:S(2)}) %collective-permute-start.7) | collective-permute-done | bytes 524320 | tf_op jit(solution)/shard_map/weights_neighbours/ppermute | solution.py:41
  81.7 0.0 collective-permute-done.3
  81.7 11.1 %conditional.3 = ((bf16[2,3,24,512]{3,2,1,0:T(8,128)(2,1)}, bf16[2,3,12,512]{3,2,1,0:T(8,128)(2,1)}, bf16[2,3,24,512]{3,2,1,0:T(8,128)(2,1)}, bf16[2,3,12,512]{3,2,1,0:T(8,128)(2,1)}, bf16[768,128]{1,0:T(8,128)(2,1)})) conditional(s32[]{:T(128)} %convert_element_type.5, (s32[3]{0:T(128)S(1)}, bf16[32,64,128]{2,1,0:T(8,128)(2,1)S(1)}, ...), branch_computations={%region_2.3_spmd, %region_3.4_spmd} | conditional | bytes 8 | solution.py:512
  81.9 10.9 %deep_block.1 = (bf16[2,3,24,512]{3,2,1,0:T(8,128)(2,1)}, bf16[2,3,12,512]{3,2,1,0:T(8,128)(2,1)}, bf16[2,3,24,512]{3,2,1,0:T(8,128)(2,1)}, bf16[2,3,12,512]{3,2,1,0:T(8,128)(2,1)}, bf16[768,128]{1,0:T(8,128)(2,1)}) custom-call(s32[3]{0:T(128)S(1)} %get-tuple-element.112.place_ref, bf16[32,64,128]{2,1,0:T(8,128)(2,1)S(1)} %get-tuple-element.113.p0, ...), custom_call_target="tpu_custom_call" | custom-call | tf_op jit(solution)/shard_map/cond/branch_0_fun/deep_block/pallas_call | solution.py:402
  92.9 17.2 %all_to_all.20.parts_ref = bf16[16,48,128]{2,1,0:T(8,128)(2,1)} all-to-all(bf16[16,48,128]{2,1,0:T(8,128)(2,1)} %bitcast.37), channel_id=1, replica_groups=mesh['segment'=2,'lat'=16,'lon'=16] {'lon'}, dimensions={0} | all-to-all | bytes 393216 | tf_op jit(solution)/shard_map/adapter_sum/all_to_all | solution.py:523
  110.1 1.6 %sum_parts.2 = bf16[16,48,128]{2,1,0:T(8,128)(2,1)} custom-call(bf16[16,48,128]{2,1,0:T(8,128)(2,1)} %all_to_all.20.parts_ref), custom_call_target="tpu_custom_call" | custom-call | tf_op jit(solution)/shard_map/adapter_sum/sum_parts/pallas_call | solution.py:429
  111.8 4.5 %all-to-all-start.2 = ((bf16[16,48,128]{2,1,0:T(8,128)(2,1)}), bf16[16,48,128]{2,1,0:T(8,128)(2,1)S(1)}, u32[]{:S(2)}, u32[]{:S(2)}) async-start(bf16[16,48,128]{2,1,0:T(8,128)(2,1)} %sum_parts.2), calls=%async_computation.2 | async-start | bytes 393216 | tf_op jit(solution)/shard_map/adapter_sum/all_to_all | solution.py:524
  116.3 11.4 %collective-permute-start.12 = (bf16[2,3,24,512]{3,2,1,0:T(8,128)(2,1)S(1)}, bf16[2,3,24,512]{3,2,1,0:T(8,128)(2,1)S(1)}, u32[]{:S(2)}, u32[]{:S(2)}) collective-permute-start(bf16[2,3,24,512]{3,2,1,0:T(8,128)(2,1)S(1)} %copy-done.8), channel_id=1, source_target_pairs={{0,272},{1,273},{2,274},{3,275},{4,276},{5,277},{6,278},{7,279},{8... | collective-permute-start | bytes 442376 | tf_op jit(solution)/shard_map/hand_over/ppermute | solution.py:445
  127.7 1.9 %collective-permute-start.13 = (bf16[2,3,24,512]{3,2,1,0:T(8,128)(2,1)S(1)}, bf16[2,3,24,512]{3,2,1,0:T(8,128)(2,1)S(1)}, u32[]{:S(2)}, u32[]{:S(2)}) collective-permute-start(bf16[2,3,24,512]{3,2,1,0:T(8,128)(2,1)S(1)} %copy-done.7), channel_id=1, source_target_pairs={{0,256},{1,257},{2,258},{3,259},{4,260},{5,261},{6,262},{7,263},{8... | collective-permute-start | bytes 442376 | tf_op jit(solution)/shard_map/hand_over/ppermute | solution.py:445
  129.6 0.0 all-to-all-done.2.parts_ref
  129.6 0.0 copy-start.3
  129.7 0.7 copy-done.3
  130.3 1.6 %sum_parts.3 = bf16[16,48,128]{2,1,0:T(8,128)(2,1)} custom-call(bf16[16,48,128]{2,1,0:T(8,128)(2,1)} %copy-done.3), custom_call_target="tpu_custom_call" | custom-call | tf_op jit(solution)/shard_map/adapter_sum/sum_parts/pallas_call | solution.py:429
  132.0 3.5 %all-to-all-start.3 = ((bf16[16,48,128]{2,1,0:T(8,128)(2,1)}), bf16[16,48,128]{2,1,0:T(8,128)(2,1)S(1)}, u32[]{:S(2)}, u32[]{:S(2)}) async-start(bf16[16,48,128]{2,1,0:T(8,128)(2,1)} %sum_parts.3), calls=%async_computation.3 | async-start | bytes 393216 | tf_op jit(solution)/shard_map/adapter_sum/all_to_all | solution.py:525
  135.5 8.9 %collective-permute-start.10 = (bf16[2,3,12,512]{3,2,1,0:T(8,128)(2,1)S(1)}, bf16[2,3,12,512]{3,2,1,0:T(8,128)(2,1)S(1)}, u32[]{:S(2)}, u32[]{:S(2)}) collective-permute-start(bf16[2,3,12,512]{3,2,1,0:T(8,128)(2,1)S(1)} %copy-done.10), channel_id=1, source_target_pairs={{0,273},{1,274},{2,275},{3,276},{4,277},{5,278},{6,279},{7,280},{8... | collective-permute-start | bytes 221192 | tf_op jit(solution)/shard_map/hand_over/ppermute | solution.py:445
  144.4 1.9 %collective-permute-start.11 = (bf16[2,3,12,512]{3,2,1,0:T(8,128)(2,1)S(1)}, bf16[2,3,12,512]{3,2,1,0:T(8,128)(2,1)S(1)}, u32[]{:S(2)}, u32[]{:S(2)}) collective-permute-start(bf16[2,3,12,512]{3,2,1,0:T(8,128)(2,1)S(1)} %copy-done.9), channel_id=1, source_target_pairs={{0,257},{1,258},{2,259},{3,260},{4,261},{5,262},{6,263},{7,264},{8... | collective-permute-start | bytes 221192 | tf_op jit(solution)/shard_map/hand_over/ppermute | solution.py:445
  146.3 1.7 %collective-permute-done.10 = bf16[2,3,12,512]{3,2,1,0:T(8,128)(2,1)S(1)} collective-permute-done((bf16[2,3,12,512]{3,2,1,0:T(8,128)(2,1)S(1)}, bf16[2,3,12,512]{3,2,1,0:T(8,128)(2,1)S(1)}, u32[]{:S(2)}, u32[]{:S(2)}) %collective-permute-start.10) | collective-permute-done | bytes 73760 | tf_op jit(solution)/shard_map/hand_over/ppermute | solution.py:445
  148.0 4.4 %collective-permute-done.11 = bf16[2,3,12,512]{3,2,1,0:T(8,128)(2,1)S(1)} collective-permute-done((bf16[2,3,12,512]{3,2,1,0:T(8,128)(2,1)S(1)}, bf16[2,3,12,512]{3,2,1,0:T(8,128)(2,1)S(1)}, u32[]{:S(2)}, u32[]{:S(2)}) %collective-permute-start.11) | collective-permute-done | bytes 73760 | tf_op jit(solution)/shard_map/hand_over/ppermute | solution.py:445
  152.4 0.9 fusion.4
  153.3 0.8 reshape.25
  (30 shorter events, 0.2 us)
Async XLA Ops:
  0.6 20.2 %copy-start.1 = (bf16[1,2,6,24,512]{4,3,2,1,0:T(8,128)(2,1)S(1)}, bf16[1,2,6,24,512]{4,3,2,1,0:T(8,128)(2,1)}, u32[]{:S(2)}) copy-start(bf16[1,2,6,24,512]{4,3,2,1,0:T(8,128)(2,1)} %param.16) | copy-start | bytes 884740
  0.6 20.2 %copy-start = (bf16[1,2,6,24,512]{4,3,2,1,0:T(8,128)(2,1)S(1)}, bf16[1,2,6,24,512]{4,3,2,1,0:T(8,128)(2,1)}, u32[]{:S(2)}) copy-start(bf16[1,2,6,24,512]{4,3,2,1,0:T(8,128)(2,1)} %param.15) | copy-start | bytes 884740
  2.7 45.5 %all-to-all-start = ((bf16[32,64,128]{2,1,0:T(8,128)(2,1)}), bf16[32,64,128]{2,1,0:T(8,128)(2,1)S(1)}, u32[]{:S(2)}, u32[]{:S(2)}) async-start(bf16[32,64,128]{2,1,0:T(8,128)(2,1)} %pack_weights.1), calls=%async_computation | async-start | bytes 1048576 | tf_op jit(solution)/shard_map/weights_class/all_to_all | solution.py:476
  20.9 25.3 %copy-start.2 = (f32[1,98304]{1,0:T(1,128)S(1)}, f32[1,98304]{1,0:T(1,128)}, u32[]{:S(2)}) copy-start(f32[1,98304]{1,0:T(1,128)} %param.25) | copy-start | bytes 1179652
  20.9 25.2 %collective-permute-start = (bf16[2,2,3,24,512]{4,3,2,1,0:T(8,128)(2,1)S(1)}, bf16[2,2,3,24,512]{4,3,2,1,0:T(8,128)(2,1)S(1)}, u32[]{:S(2)}, u32[]{:S(2)}) collective-permute-start(bf16[2,2,3,24,512]{4,3,2,1,0:T(8,128)(2,1)S(1)} %pad_maximum_fusion), channel_id=1, source_target_pairs={{0,240},{1,241},{2,242},{3,243},{4,244},{5,245},{6,246},{7,247},{8... | collective-permute-start | bytes 884744 | tf_op jit(solution)/shard_map/halos/ppermute | solution.py:453
  28.8 11.7 %collective-permute-start.1 = (bf16[2,2,3,12,512]{4,3,2,1,0:T(8,128)(2,1)S(1)}, bf16[2,2,3,12,512]{4,3,2,1,0:T(8,128)(2,1)S(1)}, u32[]{:S(2)}, u32[]{:S(2)}) collective-permute-start(bf16[2,2,3,12,512]{4,3,2,1,0:T(8,128)(2,1)S(1)} %pad_maximum_fusion.1), channel_id=1, source_target_pairs={{0,15},{1,0},{2,1},{3,2},{4,3},{5,4},{6,5},{7,6},{8,7},{9,8},{10,9... | collective-permute-start | bytes 442376 | tf_op jit(solution)/shard_map/halos/ppermute | solution.py:453
  33.1 13.0 %collective-permute-start.2 = (bf16[2,2,3,12,512]{4,3,2,1,0:T(8,128)(2,1)S(1)}, bf16[2,2,3,12,512]{4,3,2,1,0:T(8,128)(2,1)S(1)}, u32[]{:S(2)}, u32[]{:S(2)}) collective-permute-start(bf16[2,2,3,12,512]{4,3,2,1,0:T(8,128)(2,1)S(1)} %pad_maximum_fusion.2), channel_id=1, source_target_pairs={{0,255},{1,240},{2,241},{3,242},{4,243},{5,244},{6,245},{7,246},{8... | collective-permute-start | bytes 442376 | tf_op jit(solution)/shard_map/halos/ppermute | solution.py:453
  46.2 26.1 %copy-start.4 = (s32[144,144]{1,0:T(8,128)S(1)}, s32[144,144]{1,0:T(8,128)}, u32[]{:S(2)}) copy-start(s32[144,144]{1,0:T(8,128)} %param.18) | copy-start | bytes 248836
  46.2 26.9 %copy-start.5 = (f32[759,8]{0,1:T(8,128)S(1)}, f32[759,8]{0,1:T(8,128)}, u32[]{:S(2)}) copy-start(f32[759,8]{0,1:T(8,128)} %param.20) | copy-start | bytes 72868
  46.2 26.8 %copy-start.6 = (f32[759,8]{0,1:T(8,128)S(1)}, f32[759,8]{0,1:T(8,128)}, u32[]{:S(2)}) copy-start(f32[759,8]{0,1:T(8,128)} %param.19) | copy-start | bytes 72868
  48.2 16.3 %collective-permute-start.9 = (bf16[32,64,128]{2,1,0:T(8,128)(2,1)S(1)}, bf16[32,64,128]{2,1,0:T(8,128)(2,1)S(1)}, u32[]{:S(2)}, u32[]{:S(2)}) collective-permute-start(bf16[32,64,128]{2,1,0:T(8,128)(2,1)S(1)} %all-to-all-done), channel_id=1, source_target_pairs={{0,32},{1,33},{2,34},{3,35},{4,36},{5,37},{6,38},{7,39},{8,40},{9,... | collective-permute-start | bytes 1572872 | tf_op jit(solution)/shard_map/weights_neighbours/ppermute | solution.py:41
  51.4 17.8 %collective-permute-start.8 = (bf16[32,64,128]{2,1,0:T(8,128)(2,1)S(1)}, bf16[32,64,128]{2,1,0:T(8,128)(2,1)S(1)}, u32[]{:S(2)}, u32[]{:S(2)}) collective-permute-start(bf16[32,64,128]{2,1,0:T(8,128)(2,1)S(1)} %all-to-all-done), channel_id=1, source_target_pairs={{0,8},{1,9},{2,10},{3,11},{4,12},{5,13},{6,14},{7,15},{8,16},{9,17... | collective-permute-start | bytes 1572872 | tf_op jit(solution)/shard_map/weights_neighbours/ppermute | solution.py:41
  53.5 28.2 %collective-permute-start.7 = (bf16[32,64,128]{2,1,0:T(8,128)(2,1)S(1)}, bf16[32,64,128]{2,1,0:T(8,128)(2,1)S(1)}, u32[]{:S(2)}, u32[]{:S(2)}) collective-permute-start(bf16[32,64,128]{2,1,0:T(8,128)(2,1)S(1)} %all-to-all-done), channel_id=1, source_target_pairs={{0,1},{1,2},{2,3},{3,4},{4,5},{5,6},{6,7},{7,0},{8,9},{9,10},{10,1... | collective-permute-start | bytes 1572872 | tf_op jit(solution)/shard_map/weights_neighbours/ppermute | solution.py:41
  57.2 24.5 %collective-permute-start.6 = (bf16[32,64,128]{2,1,0:T(8,128)(2,1)S(1)}, bf16[32,64,128]{2,1,0:T(8,128)(2,1)}, u32[]{:S(2)}, u32[]{:S(2)}) collective-permute-start(bf16[32,64,128]{2,1,0:T(8,128)(2,1)S(1)} %all-to-all-done), channel_id=1, source_target_pairs={{0,33},{1,34},{2,35},{3,36},{4,37},{5,38},{6,39},{7,32},{8,41},{9,... | collective-permute-start | bytes 1572872 | tf_op jit(solution)/shard_map/weights_neighbours/ppermute | solution.py:41
  60.6 21.2 %collective-permute-start.5 = (bf16[32,64,128]{2,1,0:T(8,128)(2,1)S(1)}, bf16[32,64,128]{2,1,0:T(8,128)(2,1)}, u32[]{:S(2)}, u32[]{:S(2)}) collective-permute-start(bf16[32,64,128]{2,1,0:T(8,128)(2,1)S(1)} %all-to-all-done), channel_id=1, source_target_pairs={{0,7},{1,0},{2,1},{3,2},{4,3},{5,4},{6,5},{7,6},{8,15},{9,8},{10,9... | collective-permute-start | bytes 1572872 | tf_op jit(solution)/shard_map/weights_neighbours/ppermute | solution.py:41
  64.5 17.2 %collective-permute-start.4 = (bf16[32,64,128]{2,1,0:T(8,128)(2,1)S(1)}, bf16[32,64,128]{2,1,0:T(8,128)(2,1)}, u32[]{:S(2)}, u32[]{:S(2)}) collective-permute-start(bf16[32,64,128]{2,1,0:T(8,128)(2,1)S(1)} %all-to-all-done), channel_id=1, source_target_pairs={{0,24},{1,25},{2,26},{3,27},{4,28},{5,29},{6,30},{7,31},{8,0},{9,1... | collective-permute-start | bytes 1572872 | tf_op jit(solution)/shard_map/weights_neighbours/ppermute | solution.py:41
  69.3 12.5 %collective-permute-start.3 = (bf16[32,64,128]{2,1,0:T(8,128)(2,1)S(1)}, bf16[32,64,128]{2,1,0:T(8,128)(2,1)}, u32[]{:S(2)}, u32[]{:S(2)}) collective-permute-start(bf16[32,64,128]{2,1,0:T(8,128)(2,1)S(1)} %all-to-all-done), channel_id=1, source_target_pairs={{0,224},{1,225},{2,226},{3,227},{4,228},{5,229},{6,230},{7,231},{8... | collective-permute-start | bytes 1572872 | tf_op jit(solution)/shard_map/weights_neighbours/ppermute | solution.py:41
  92.9 23.4 %copy-start.8 = (bf16[2,3,24,512]{3,2,1,0:T(8,128)(2,1)S(1)}, bf16[2,3,24,512]{3,2,1,0:T(8,128)(2,1)}, u32[]{:S(2)}) copy-start(bf16[2,3,24,512]{3,2,1,0:T(8,128)(2,1)} %get-tuple-element.197) | copy-start | bytes 442372
  92.9 34.8 %copy-start.7 = (bf16[2,3,24,512]{3,2,1,0:T(8,128)(2,1)S(1)}, bf16[2,3,24,512]{3,2,1,0:T(8,128)(2,1)}, u32[]{:S(2)}) copy-start(bf16[2,3,24,512]{3,2,1,0:T(8,128)(2,1)} %get-tuple-element.198) | copy-start | bytes 442372
  92.9 42.6 %copy-start.10 = (bf16[2,3,12,512]{3,2,1,0:T(8,128)(2,1)S(1)}, bf16[2,3,12,512]{3,2,1,0:T(8,128)(2,1)}, u32[]{:S(2)}) copy-start(bf16[2,3,12,512]{3,2,1,0:T(8,128)(2,1)} %get-tuple-element.195) | copy-start | bytes 221188
  92.9 51.5 %copy-start.9 = (bf16[2,3,12,512]{3,2,1,0:T(8,128)(2,1)S(1)}, bf16[2,3,12,512]{3,2,1,0:T(8,128)(2,1)}, u32[]{:S(2)}) copy-start(bf16[2,3,12,512]{3,2,1,0:T(8,128)(2,1)} %get-tuple-element.196) | copy-start | bytes 221188
  111.8 17.9 %all-to-all-start.2 = ((bf16[16,48,128]{2,1,0:T(8,128)(2,1)}), bf16[16,48,128]{2,1,0:T(8,128)(2,1)S(1)}, u32[]{:S(2)}, u32[]{:S(2)}) async-start(bf16[16,48,128]{2,1,0:T(8,128)(2,1)} %sum_parts.2), calls=%async_computation.2 | async-start | bytes 393216 | tf_op jit(solution)/shard_map/adapter_sum/all_to_all | solution.py:524
  116.3 36.1 %collective-permute-start.12 = (bf16[2,3,24,512]{3,2,1,0:T(8,128)(2,1)S(1)}, bf16[2,3,24,512]{3,2,1,0:T(8,128)(2,1)S(1)}, u32[]{:S(2)}, u32[]{:S(2)}) collective-permute-start(bf16[2,3,24,512]{3,2,1,0:T(8,128)(2,1)S(1)} %copy-done.8), channel_id=1, source_target_pairs={{0,272},{1,273},{2,274},{3,275},{4,276},{5,277},{6,278},{7,279},{8... | collective-permute-start | bytes 442376 | tf_op jit(solution)/shard_map/hand_over/ppermute | solution.py:445
  127.7 24.7 %collective-permute-start.13 = (bf16[2,3,24,512]{3,2,1,0:T(8,128)(2,1)S(1)}, bf16[2,3,24,512]{3,2,1,0:T(8,128)(2,1)S(1)}, u32[]{:S(2)}, u32[]{:S(2)}) collective-permute-start(bf16[2,3,24,512]{3,2,1,0:T(8,128)(2,1)S(1)} %copy-done.7), channel_id=1, source_target_pairs={{0,256},{1,257},{2,258},{3,259},{4,260},{5,261},{6,262},{7,263},{8... | collective-permute-start | bytes 442376 | tf_op jit(solution)/shard_map/hand_over/ppermute | solution.py:445
  129.6 0.7 copy-start.3
  132.0 21.4 %all-to-all-start.3 = ((bf16[16,48,128]{2,1,0:T(8,128)(2,1)}), bf16[16,48,128]{2,1,0:T(8,128)(2,1)S(1)}, u32[]{:S(2)}, u32[]{:S(2)}) async-start(bf16[16,48,128]{2,1,0:T(8,128)(2,1)} %sum_parts.3), calls=%async_computation.3 | async-start | bytes 393216 | tf_op jit(solution)/shard_map/adapter_sum/all_to_all | solution.py:525
  135.5 12.5 %collective-permute-start.10 = (bf16[2,3,12,512]{3,2,1,0:T(8,128)(2,1)S(1)}, bf16[2,3,12,512]{3,2,1,0:T(8,128)(2,1)S(1)}, u32[]{:S(2)}, u32[]{:S(2)}) collective-permute-start(bf16[2,3,12,512]{3,2,1,0:T(8,128)(2,1)S(1)} %copy-done.10), channel_id=1, source_target_pairs={{0,273},{1,274},{2,275},{3,276},{4,277},{5,278},{6,279},{7,280},{8... | collective-permute-start | bytes 221192 | tf_op jit(solution)/shard_map/hand_over/ppermute | solution.py:445
  144.4 8.0 %collective-permute-start.11 = (bf16[2,3,12,512]{3,2,1,0:T(8,128)(2,1)S(1)}, bf16[2,3,12,512]{3,2,1,0:T(8,128)(2,1)S(1)}, u32[]{:S(2)}, u32[]{:S(2)}) collective-permute-start(bf16[2,3,12,512]{3,2,1,0:T(8,128)(2,1)S(1)} %copy-done.9), channel_id=1, source_target_pairs={{0,257},{1,258},{2,259},{3,260},{4,261},{5,262},{6,263},{7,264},{8... | collective-permute-start | bytes 221192 | tf_op jit(solution)/shard_map/hand_over/ppermute | solution.py:445

commit v3 on v2

--- a/solution.py
+++ b/solution.py
@@ -161,7 +161,7 @@
 
 def prep_kernel(
     deep,
-    x_ref, c_ref, s1_ref, s2_ref, s3_ref, adapter_ref,
+    x_ref, c_ref, s1_ref, s2_ref, adapter_ref,
     normed_ref, cot_ref, scale_ref, low_q_ref, low_c_ref, aq_ref, bq_ref, ap_ref,
     xs, cols, aq_s, ap_s, bq_s, bp_s,
 ):
@@ -200,8 +200,7 @@
                     own = source[level, row + 3].astype(F32)
                 else:
                     own = s1_ref[which, level, row - 3].astype(F32)
-                strip = s2_ref if row < 3 else s3_ref
-                side = strip[which, level, row % 3].astype(F32)
+                side = s2_ref[which, level, row].astype(F32)
                 at = 72 * level + 12 * row
                 if deep:
                     for c in range(4):
@@ -474,27 +473,6 @@
         )(place, qkv_shallow, proj_shallow, qkv_deep, proj_deep)
     with jax.named_scope("weights_class"):
         piece = lax.all_to_all(own_w, BOTH, 0, 0, axis_index_groups=class_groups())
-    with jax.named_scope("halos"):
-        s1 = shift(jnp.stack([x[:, :3], cot[:, :3]]), -1, 0)
-        s2 = shift(jnp.stack([x[:, 3:, :12], cot[:, 3:, :12]]), 0, -1)
-        s3 = shift(jnp.stack([x[:, :3, :12], cot[:, :3, :12]]), -1, -1)
-    with jax.named_scope("prep"):
-        prep = lax.cond(
-            segment == 0,
-            functools.partial(run_prep, False),
-            functools.partial(run_prep, True),
-            (x, cot, s1, s2, s3, adapters.reshape(768, 128)),
-        )
-        piece, prep = lax.optimization_barrier((piece, prep))
-    with jax.named_scope("weights_neighbours"):
-        p4 = neighbour_send(piece, 0, 1, 1)
-        p6 = neighbour_send(piece, 1, 0, 0)
-        p2 = neighbour_send(piece, -1, 0, 0)
-        p7 = neighbour_send(piece, 0, 1, 0)
-        p1 = neighbour_send(piece, 0, -1, 0)
-        p5 = neighbour_send(piece, 0, 0, 1)
-        p3 = neighbour_send(piece, 0, 0, -1)
-
     with jax.named_scope("bias"):
         table = jnp.where(segment == 1, table_deep, table_shallow)
         table = jnp.pad(table.T, ((0, 0), (0, 768 - table.shape[0])))
@@ -509,6 +487,27 @@
             out_specs=(VMEM, VMEM),
             name="bias_table",
         )(place, pole_mask, index, table)
+        piece, bias, allowed = lax.optimization_barrier((piece, bias, allowed))
+    with jax.named_scope("halos"):
+        s1 = shift(jnp.stack([x[:, :3], cot[:, :3]]), -1, 0)
+        left = jnp.stack([x[:, 3:, :12], cot[:, 3:, :12]])
+        s2 = shift(jnp.concatenate([left, s1[:, :, :, :12]], 2), 0, -1)
+    with jax.named_scope("prep"):
+        prep = lax.cond(
+            segment == 0,
+            functools.partial(run_prep, False),
+            functools.partial(run_prep, True),
+            (x, cot, s1, s2, adapters.reshape(768, 128)),
+        )
+    with jax.named_scope("weights_neighbours"):
+        p4 = neighbour_send(piece, 0, 1, 1)
+        p6 = neighbour_send(piece, 1, 0, 0)
+        p2 = neighbour_send(piece, -1, 0, 0)
+        p7 = neighbour_send(piece, 0, 1, 0)
+        p1 = neighbour_send(piece, 0, -1, 0)
+        p5 = neighbour_send(piece, 0, 0, 1)
+        p3 = neighbour_send(piece, 0, 0, -1)
+
     own, side, below, corner, grads = lax.cond(
         segment == 0,
         functools.partial(run_block, False),

time: 155 us -> 146 us (0.942)
  starting transfers between devices: 89.9 us -> 83 us
  blocking collectives: 17.2 us -> 11.8 us
  waiting for transfers between devices: 17.2 us -> 18.8 us
    ppermute x3 -> x2, waiting for transfers between devices: 9.22 us -> 2.49 us  [shift(): return lax.ppermute(value, BOTH, route)]
    ppermute x3 -> x2, starting transfers between devices: 15.9 us -> 9.82 us  [shift(): return lax.ppermute(value, BOTH, route)]
    all_to_all x1, blocking collectives: 17.2 us -> 11.8 us  [shards(): grads = lax.all_to_all(grads.reshape(16, 48, 128), 'lon', 0, 0)]
    all_to_all x1, waiting for transfers between devices: 0.01 us -> 5.35 us  [shards(): piece = lax.all_to_all(own_w, BOTH, 0, 0, axis_index_groups=class_groups())]
    ppermute x7, waiting for transfers between devices: 1.81 us -> 4.87 us  [neighbour_send(): return lax.ppermute(value, BOTH, route)]
    ppermute x7, starting transfers between devices: 23.7 us -> 21.1 us  [neighbour_send(): return lax.ppermute(value, BOTH, route)]
    all_to_all x1, starting transfers between devices: 4.49 us -> 6.35 us  [shards(): grads = lax.all_to_all(summed(grads), 'lat', 0, 0)]
  transfers between devices with their start and end apart: 17 -> 16, of which waited for: 6 -> 6; matrix products, arithmetic and copies ran while one was open for 2% -> 2% of each run, Pallas kernels for 7% -> 8%
where the time goes in v3:
time: 146 us
  starting transfers between devices  83 us (57%)
  Pallas kernels  25.2 us (17%)
  waiting for transfers between devices  18.8 us (13%)
  blocking collectives  11.8 us (8%)
  local copies, waits for them, and re-layouts  2.92 us (2%)
  other arithmetic  2.54 us (2%)
    ppermute x4, starting transfers between devices, hand(): return lax.ppermute(value, ('segment', 'lat', 'lon'), route)  23.9 us
    ppermute x7, starting transfers between devices, neighbour_send(): return lax.ppermute(value, BOTH, route)  21.1 us
    all_to_all x1, starting transfers between devices, shards(): piece = lax.all_to_all(own_w, BOTH, 0, 0, axis_index_groups=class_groups())  18.3 us
    all_to_all x1, blocking collectives, shards(): grads = lax.all_to_all(grads.reshape(16, 48, 128), 'lon', 0, 0)  11.8 us
    pallas_call x1, Pallas kernels, run_block(): pl.pallas_call(functools.partial(block_kernel, deep), out_shape=tuple((ja...  10.5 us
    ppermute x2, starting transfers between devices, shift(): return lax.ppermute(value, BOTH, route)  9.82 us
    pallas_call x1, Pallas kernels, shards(): pl.pallas_call(bias_kernel, out_shape=(jax.ShapeDtypeStruct((HEADS, WT, 2...  6.46 us
    all_to_all x1, starting transfers between devices, shards(): grads = lax.all_to_all(summed(grads), 'lat', 0, 0)  6.35 us
  transfers between devices with their start and end apart: 16, of which 6 were waited for; matrix products, arithmetic and copies ran while one was open for 2% of the time, Pallas kernels for 8%

profile of v3, /device:TPU:1, one launch (start us, length us, event | category | flops | bytes accessed | tf_op | source)
XLA Modules:
  0.0 145.6 jit_solution(13915730112131361361)
XLA Ops:
  0.7 0.1 pad_add_fusion.place_ref
  0.8 1.9 %pack_weights.1 = bf16[32,64,128]{2,1,0:T(8,128)(2,1)} custom-call(s32[3]{0:T(128)S(1)} %pad_add_fusion.place_ref, bf16[32,96]{1,0:T(8,128)(2,1)} %qs_ref.1, bf16[32,32]{1,0:T(8,128)(2,1)} %ps_ref.1, bf16[64,96]{1,0:T(8,128)(2,1)} %qd_ref.1, bf16[32,64]{1,0:T(8,128)(2,1)} %pd_ref.1), custom_call_target="tpu_custom_call" | custom-call | tf_op jit(solution)/shard_map/pack/pack_weights/pallas_call | solution.py:467
  2.7 18.3 %all-to-all-start = ((bf16[32,64,128]{2,1,0:T(8,128)(2,1)}), bf16[32,64,128]{2,1,0:T(8,128)(2,1)S(1)}, u32[]{:S(2)}, u32[]{:S(2)}) async-start(bf16[32,64,128]{2,1,0:T(8,128)(2,1)} %pack_weights.1), calls=%async_computation | async-start | bytes 1048576 | tf_op jit(solution)/shard_map/weights_class/all_to_all | solution.py:475
  21.0 0.7 pad_maximum_fusion.1
  21.8 7.6 %collective-permute-start.7 = (bf16[2,2,3,24,512]{4,3,2,1,0:T(8,128)(2,1)}, bf16[2,2,3,24,512]{4,3,2,1,0:T(8,128)(2,1)S(1)}, u32[]{:S(2)}, u32[]{:S(2)}) collective-permute-start(bf16[2,2,3,24,512]{4,3,2,1,0:T(8,128)(2,1)} %pad_maximum_fusion.1), channel_id=1, source_target_pairs={{0,240},{1,241},{2,242},{3,243},{4,244},{5,245},{6,246},{7,247},{8... | collective-permute-start | bytes 884744 | tf_op jit(solution)/shard_map/halos/ppermute | solution.py:452
  29.5 0.0 copy-start.3
  29.5 0.1 copy.13
  29.6 0.7 pad.12.index_ref
  30.3 0.6 pad.13.table_ref
  30.9 6.5 %bias_table.1 = (f32[8,144,256]{2,1,0:T(8,128)S(1)}, f32[144,256]{1,0:T(8,128)}) custom-call(s32[3]{0:T(128)S(1)} %pad_add_fusion.place_ref, s32[96]{0:T(128)} %pole_ref.1, s32[144,256]{1,0:T(8,128)} %pad.12.index_ref, f32[8,768]{1,0:T(8,128)} %pad.13.table_ref), custom_call_target="tpu_custom_call" | custom-call | tf_op jit(solution)/shard_map/bias/bias_table/pallas_call | solution.py:480
  37.3 5.3 %all-to-all-done = bf16[32,64,128]{2,1,0:T(8,128)(2,1)S(1)} async-done(((bf16[32,64,128]{2,1,0:T(8,128)(2,1)}), bf16[32,64,128]{2,1,0:T(8,128)(2,1)S(1)}, u32[]{:S(2)}, u32[]{:S(2)}) %all-to-all-start) | async-done | bytes 524320 | tf_op jit(solution)/shard_map/weights_class/all_to_all | solution.py:475
  42.7 2.0 %collective-permute-start.6 = (bf16[32,64,128]{2,1,0:T(8,128)(2,1)S(1)}, bf16[32,64,128]{2,1,0:T(8,128)(2,1)S(1)}, u32[]{:S(2)}, u32[]{:S(2)}) collective-permute-start(bf16[32,64,128]{2,1,0:T(8,128)(2,1)S(1)} %all-to-all-done), channel_id=1, source_target_pairs={{0,32},{1,33},{2,34},{3,35},{4,36},{5,37},{6,38},{7,39},{8,40},{9,... | collective-permute-start | bytes 1572872 | tf_op jit(solution)/shard_map/weights_neighbours/ppermute | solution.py:41
  44.7 1.9 %collective-permute-start.5 = (bf16[32,64,128]{2,1,0:T(8,128)(2,1)S(1)}, bf16[32,64,128]{2,1,0:T(8,128)(2,1)S(1)}, u32[]{:S(2)}, u32[]{:S(2)}) collective-permute-start(bf16[32,64,128]{2,1,0:T(8,128)(2,1)S(1)} %all-to-all-done), channel_id=1, source_target_pairs={{0,8},{1,9},{2,10},{3,11},{4,12},{5,13},{6,14},{7,15},{8,16},{9,17... | collective-permute-start | bytes 1572872 | tf_op jit(solution)/shard_map/weights_neighbours/ppermute | solution.py:41
  46.6 0.0 collective-permute-done.7
  46.6 0.1 pad_maximum_fusion
  46.7 2.2 %collective-permute-start.8 = (bf16[2,2,6,12,512]{4,3,2,1,0:T(8,128)(2,1)S(1)}, bf16[2,2,6,12,512]{4,3,2,1,0:T(8,128)(2,1)S(1)}, u32[]{:S(2)}, u32[]{:S(2)}) collective-permute-start(bf16[2,2,6,12,512]{4,3,2,1,0:T(8,128)(2,1)S(1)} %pad_maximum_fusion), channel_id=1, source_target_pairs={{0,15},{1,0},{2,1},{3,2},{4,3},{5,4},{6,5},{7,6},{8,7},{9,8},{10,9... | collective-permute-start | bytes 884744 | tf_op jit(solution)/shard_map/halos/ppermute | solution.py:452
  48.9 3.1 %collective-permute-start.4 = (bf16[32,64,128]{2,1,0:T(8,128)(2,1)S(1)}, bf16[32,64,128]{2,1,0:T(8,128)(2,1)}, u32[]{:S(2)}, u32[]{:S(2)}) collective-permute-start(bf16[32,64,128]{2,1,0:T(8,128)(2,1)S(1)} %all-to-all-done), channel_id=1, source_target_pairs={{0,1},{1,2},{2,3},{3,4},{4,5},{5,6},{6,7},{7,0},{8,9},{9,10},{10,1... | collective-permute-start | bytes 1572872 | tf_op jit(solution)/shard_map/weights_neighbours/ppermute | solution.py:41
  52.0 1.9 %collective-permute-start.3 = (bf16[32,64,128]{2,1,0:T(8,128)(2,1)S(1)}, bf16[32,64,128]{2,1,0:T(8,128)(2,1)}, u32[]{:S(2)}, u32[]{:S(2)}) collective-permute-start(bf16[32,64,128]{2,1,0:T(8,128)(2,1)S(1)} %all-to-all-done), channel_id=1, source_target_pairs={{0,33},{1,34},{2,35},{3,36},{4,37},{5,38},{6,39},{7,32},{8,41},{9,... | collective-permute-start | bytes 1572872 | tf_op jit(solution)/shard_map/weights_neighbours/ppermute | solution.py:41
  53.9 2.5 %collective-permute-done.8 = bf16[2,2,6,12,512]{4,3,2,1,0:T(8,128)(2,1)S(1)} collective-permute-done((bf16[2,2,6,12,512]{4,3,2,1,0:T(8,128)(2,1)S(1)}, bf16[2,2,6,12,512]{4,3,2,1,0:T(8,128)(2,1)S(1)}, u32[]{:S(2)}, u32[]{:S(2)}) %collective-permute-start.8) | collective-permute-done | bytes 294944 | tf_op jit(solution)/shard_map/halos/ppermute | solution.py:452
  56.4 2.4 %collective-permute-start.2 = (bf16[32,64,128]{2,1,0:T(8,128)(2,1)S(1)}, bf16[32,64,128]{2,1,0:T(8,128)(2,1)}, u32[]{:S(2)}, u32[]{:S(2)}) collective-permute-start(bf16[32,64,128]{2,1,0:T(8,128)(2,1)S(1)} %all-to-all-done), channel_id=1, source_target_pairs={{0,7},{1,0},{2,1},{3,2},{4,3},{5,4},{6,5},{7,6},{8,15},{9,8},{10,9... | collective-permute-start | bytes 1572872 | tf_op jit(solution)/shard_map/weights_neighbours/ppermute | solution.py:41
  58.9 0.0 collective-permute-done.6
  58.9 4.0 %collective-permute-start.1 = (bf16[32,64,128]{2,1,0:T(8,128)(2,1)S(1)}, bf16[32,64,128]{2,1,0:T(8,128)(2,1)}, u32[]{:S(2)}, u32[]{:S(2)}) collective-permute-start(bf16[32,64,128]{2,1,0:T(8,128)(2,1)S(1)} %all-to-all-done), channel_id=1, source_target_pairs={{0,24},{1,25},{2,26},{3,27},{4,28},{5,29},{6,30},{7,31},{8,0},{9,1... | collective-permute-start | bytes 1572872 | tf_op jit(solution)/shard_map/weights_neighbours/ppermute | solution.py:41
  62.9 0.8 copy-done.2
  63.7 5.8 %collective-permute-start = (bf16[32,64,128]{2,1,0:T(8,128)(2,1)S(1)}, bf16[32,64,128]{2,1,0:T(8,128)(2,1)}, u32[]{:S(2)}, u32[]{:S(2)}) collective-permute-start(bf16[32,64,128]{2,1,0:T(8,128)(2,1)S(1)} %all-to-all-done), channel_id=1, source_target_pairs={{0,224},{1,225},{2,226},{3,227},{4,228},{5,229},{6,230},{7,231},{8... | collective-permute-start | bytes 1572872 | tf_op jit(solution)/shard_map/weights_neighbours/ppermute | solution.py:41
  69.5 3.1 %conditional.2 = ((bf16[288,512]{1,0:T(8,128)(2,1)}, bf16[288,512]{1,0:T(8,128)(2,1)}, f32[288,128]{1,0:T(8,128)}, bf16[288,32]{1,0:T(8,128)(2,1)}, bf16[288,32]...) conditional(s32[]{:T(128)} %convert_element_type.5, ...), branch_computations={%region_0.1_spmd, %region_1.2_spmd} | conditional | bytes 8 | solution.py:496
  69.5 3.1 %deep_prep.1 = (bf16[288,512]{1,0:T(8,128)(2,1)}, bf16[288,512]{1,0:T(8,128)(2,1)}, f32[288,128]{1,0:T(8,128)}, bf16[288,32]{1,0:T(8,128)(2,1)}, bf16[288,32]{1,...) custom-call(bf16[2,6,24,512]{3,2,1,0:T(8,128)(2,1)S(1)} %get-tuple-element.96.x_ref, ...), custom_call_target="tpu_custom_call" | custom-call | tf_op jit(solution)/shard_map/prep/cond/branch_0_fun/deep_prep/pallas_call | solution.py:376
  72.5 0.2 collective-permute-done.4
  72.8 0.0 collective-permute-done.2
  72.8 0.0 collective-permute-done.1
  72.8 4.6 %collective-permute-done = bf16[32,64,128]{2,1,0:T(8,128)(2,1)} collective-permute-done((bf16[32,64,128]{2,1,0:T(8,128)(2,1)S(1)}, bf16[32,64,128]{2,1,0:T(8,128)(2,1)}, u32[]{:S(2)}, u32[]{:S(2)}) %collective-permute-start) | collective-permute-done | bytes 524320 | tf_op jit(solution)/shard_map/weights_neighbours/ppermute | solution.py:41
  77.4 10.7 %conditional.3 = ((bf16[2,3,24,512]{3,2,1,0:T(8,128)(2,1)S(1)}, bf16[2,3,12,512]{3,2,1,0:T(8,128)(2,1)S(1)}, bf16[2,3,24,512]{3,2,1,0:T(8,128)(2,1)S(1)}, bf16[2...) conditional(s32[]{:T(128)} %convert_element_type.5, (s32[3]{0:T(128)S(1)}, bf16[32,64,128]{2,1,0:T(8,128)(2,1)S(1)}, ...), branch_computations={%region_2.3_spmd, %region_3.4_spmd} | conditional | bytes 8 | solution.py:511
  77.4 10.5 %deep_block.1 = (bf16[2,3,24,512]{3,2,1,0:T(8,128)(2,1)S(1)}, bf16[2,3,12,512]{3,2,1,0:T(8,128)(2,1)S(1)}, bf16[2,3,24,512]{3,2,1,0:T(8,128)(2,1)S(1)}, bf16[2,3...) custom-call(s32[3]{0:T(128)S(1)} %get-tuple-element.106.place_ref, bf16[32,64,128]{2,1,0:T(8,128)(2,1)S(1)} %get-tuple-element.107.p0, ...), custom_call_target="tpu_custom_call" | custom-call | tf_op jit(solution)/shard_map/cond/branch_0_fun/deep_block/pallas_call | solution.py:401
  88.2 11.8 %all_to_all.20.parts_ref = bf16[16,48,128]{2,1,0:T(8,128)(2,1)} all-to-all(bf16[16,48,128]{2,1,0:T(8,128)(2,1)S(1)} %bitcast.33), channel_id=1, replica_groups=mesh['segment'=2,'lat'=16,'lon'=16] {'lon'}, dimensions={0} | all-to-all | bytes 393216 | tf_op jit(solution)/shard_map/adapter_sum/all_to_all | solution.py:522
  100.0 1.6 %sum_parts.2 = bf16[16,48,128]{2,1,0:T(8,128)(2,1)} custom-call(bf16[16,48,128]{2,1,0:T(8,128)(2,1)} %all_to_all.20.parts_ref), custom_call_target="tpu_custom_call" | custom-call | tf_op jit(solution)/shard_map/adapter_sum/sum_parts/pallas_call | solution.py:428
  101.6 6.4 %all-to-all-start.2 = ((bf16[16,48,128]{2,1,0:T(8,128)(2,1)}), bf16[16,48,128]{2,1,0:T(8,128)(2,1)S(1)}, u32[]{:S(2)}, u32[]{:S(2)}) async-start(bf16[16,48,128]{2,1,0:T(8,128)(2,1)} %sum_parts.2), calls=%async_computation.2 | async-start | bytes 393216 | tf_op jit(solution)/shard_map/adapter_sum/all_to_all | solution.py:523
  108.0 11.2 %collective-permute-start.11 = (bf16[2,3,24,512]{3,2,1,0:T(8,128)(2,1)S(1)}, bf16[2,3,24,512]{3,2,1,0:T(8,128)(2,1)S(1)}, u32[]{:S(2)}, u32[]{:S(2)}) collective-permute-start(bf16[2,3,24,512]{3,2,1,0:T(8,128)(2,1)S(1)} %get-tuple-element.179), channel_id=1, source_target_pairs={{0,272},{1,273},{2,274},{3,275},{4,276},{5,277},{6,278},{7,279},{8... | collective-permute-start | bytes 442376 | tf_op jit(solution)/shard_map/hand_over/ppermute | solution.py:444
  119.2 1.9 %collective-permute-start.12 = (bf16[2,3,24,512]{3,2,1,0:T(8,128)(2,1)S(1)}, bf16[2,3,24,512]{3,2,1,0:T(8,128)(2,1)S(1)}, u32[]{:S(2)}, u32[]{:S(2)}) collective-permute-start(bf16[2,3,24,512]{3,2,1,0:T(8,128)(2,1)S(1)} %get-tuple-element.180), channel_id=1, source_target_pairs={{0,256},{1,257},{2,258},{3,259},{4,260},{5,261},{6,262},{7,263},{8... | collective-permute-start | bytes 442376 | tf_op jit(solution)/shard_map/hand_over/ppermute | solution.py:444
  121.1 0.0 all-to-all-done.2.parts_ref
  121.1 0.0 copy-start.5
  121.1 0.7 copy-done.5
  121.8 1.6 %sum_parts.3 = bf16[16,48,128]{2,1,0:T(8,128)(2,1)} custom-call(bf16[16,48,128]{2,1,0:T(8,128)(2,1)} %copy-done.5), custom_call_target="tpu_custom_call" | custom-call | tf_op jit(solution)/shard_map/adapter_sum/sum_parts/pallas_call | solution.py:428
  123.4 3.5 %all-to-all-start.3 = ((bf16[16,48,128]{2,1,0:T(8,128)(2,1)}), bf16[16,48,128]{2,1,0:T(8,128)(2,1)S(1)}, u32[]{:S(2)}, u32[]{:S(2)}) async-start(bf16[16,48,128]{2,1,0:T(8,128)(2,1)} %sum_parts.3), calls=%async_computation.3 | async-start | bytes 393216 | tf_op jit(solution)/shard_map/adapter_sum/all_to_all | solution.py:524
  127.0 8.9 %collective-permute-start.9 = (bf16[2,3,12,512]{3,2,1,0:T(8,128)(2,1)S(1)}, bf16[2,3,12,512]{3,2,1,0:T(8,128)(2,1)S(1)}, u32[]{:S(2)}, u32[]{:S(2)}) collective-permute-start(bf16[2,3,12,512]{3,2,1,0:T(8,128)(2,1)S(1)} %get-tuple-element.177), channel_id=1, source_target_pairs={{0,273},{1,274},{2,275},{3,276},{4,277},{5,278},{6,279},{7,280},{8... | collective-permute-start | bytes 221192 | tf_op jit(solution)/shard_map/hand_over/ppermute | solution.py:444
  135.9 1.9 %collective-permute-start.10 = (bf16[2,3,12,512]{3,2,1,0:T(8,128)(2,1)S(1)}, bf16[2,3,12,512]{3,2,1,0:T(8,128)(2,1)S(1)}, u32[]{:S(2)}, u32[]{:S(2)}) collective-permute-start(bf16[2,3,12,512]{3,2,1,0:T(8,128)(2,1)S(1)} %get-tuple-element.178), channel_id=1, source_target_pairs={{0,257},{1,258},{2,259},{3,260},{4,261},{5,262},{6,263},{7,264},{8... | collective-permute-start | bytes 221192 | tf_op jit(solution)/shard_map/hand_over/ppermute | solution.py:444
  137.8 1.7 %collective-permute-done.9 = bf16[2,3,12,512]{3,2,1,0:T(8,128)(2,1)S(1)} collective-permute-done((bf16[2,3,12,512]{3,2,1,0:T(8,128)(2,1)S(1)}, bf16[2,3,12,512]{3,2,1,0:T(8,128)(2,1)S(1)}, u32[]{:S(2)}, u32[]{:S(2)}) %collective-permute-start.9) | collective-permute-done | bytes 73760 | tf_op jit(solution)/shard_map/hand_over/ppermute | solution.py:444
  139.5 4.4 %collective-permute-done.10 = bf16[2,3,12,512]{3,2,1,0:T(8,128)(2,1)S(1)} collective-permute-done((bf16[2,3,12,512]{3,2,1,0:T(8,128)(2,1)S(1)}, bf16[2,3,12,512]{3,2,1,0:T(8,128)(2,1)S(1)}, u32[]{:S(2)}, u32[]{:S(2)}) %collective-permute-start.10) | collective-permute-done | bytes 73760 | tf_op jit(solution)/shard_map/hand_over/ppermute | solution.py:444
  143.9 0.9 fusion.4
  144.8 0.8 reshape.25
  (24 shorter events, 0.1 us)
Async XLA Ops:
  0.6 20.4 %copy-start.1 = (bf16[1,2,6,24,512]{4,3,2,1,0:T(8,128)(2,1)S(1)}, bf16[1,2,6,24,512]{4,3,2,1,0:T(8,128)(2,1)}, u32[]{:S(2)}) copy-start(bf16[1,2,6,24,512]{4,3,2,1,0:T(8,128)(2,1)} %param.16) | copy-start | bytes 884740
  0.6 20.4 %copy-start = (bf16[1,2,6,24,512]{4,3,2,1,0:T(8,128)(2,1)S(1)}, bf16[1,2,6,24,512]{4,3,2,1,0:T(8,128)(2,1)}, u32[]{:S(2)}) copy-start(bf16[1,2,6,24,512]{4,3,2,1,0:T(8,128)(2,1)} %param.15) | copy-start | bytes 884740
  2.7 26.8 %copy-start.7 = (f32[759,8]{0,1:T(8,128)S(1)}, f32[759,8]{0,1:T(8,128)}, u32[]{:S(2)}) copy-start(f32[759,8]{0,1:T(8,128)} %param.20) | copy-start | bytes 72868
  2.7 26.8 %copy-start.8 = (f32[759,8]{0,1:T(8,128)S(1)}, f32[759,8]{0,1:T(8,128)}, u32[]{:S(2)}) copy-start(f32[759,8]{0,1:T(8,128)} %param.19) | copy-start | bytes 72868
  2.7 26.8 %copy-start.6 = (s32[144,144]{1,0:T(8,128)S(1)}, s32[144,144]{1,0:T(8,128)}, u32[]{:S(2)}) copy-start(s32[144,144]{1,0:T(8,128)} %param.18) | copy-start | bytes 248836
  2.7 40.0 %all-to-all-start = ((bf16[32,64,128]{2,1,0:T(8,128)(2,1)}), bf16[32,64,128]{2,1,0:T(8,128)(2,1)S(1)}, u32[]{:S(2)}, u32[]{:S(2)}) async-start(bf16[32,64,128]{2,1,0:T(8,128)(2,1)} %pack_weights.1), calls=%async_computation | async-start | bytes 1048576 | tf_op jit(solution)/shard_map/weights_class/all_to_all | solution.py:475
  21.8 24.8 %collective-permute-start.7 = (bf16[2,2,3,24,512]{4,3,2,1,0:T(8,128)(2,1)}, bf16[2,2,3,24,512]{4,3,2,1,0:T(8,128)(2,1)S(1)}, u32[]{:S(2)}, u32[]{:S(2)}) collective-permute-start(bf16[2,2,3,24,512]{4,3,2,1,0:T(8,128)(2,1)} %pad_maximum_fusion.1), channel_id=1, source_target_pairs={{0,240},{1,241},{2,242},{3,243},{4,244},{5,245},{6,246},{7,247},{8... | collective-permute-start | bytes 884744 | tf_op jit(solution)/shard_map/halos/ppermute | solution.py:452
  29.5 40.0 %copy-start.3 = (f32[1,98304]{1,0:T(1,128)S(1)}, f32[1,98304]{1,0:T(1,128)}, u32[]{:S(2)}) copy-start(f32[1,98304]{1,0:T(1,128)} %param.25) | copy-start | bytes 1179652
  42.7 16.2 %collective-permute-start.6 = (bf16[32,64,128]{2,1,0:T(8,128)(2,1)S(1)}, bf16[32,64,128]{2,1,0:T(8,128)(2,1)S(1)}, u32[]{:S(2)}, u32[]{:S(2)}) collective-permute-start(bf16[32,64,128]{2,1,0:T(8,128)(2,1)S(1)} %all-to-all-done), channel_id=1, source_target_pairs={{0,32},{1,33},{2,34},{3,35},{4,36},{5,37},{6,38},{7,39},{8,40},{9,... | collective-permute-start | bytes 1572872 | tf_op jit(solution)/shard_map/weights_neighbours/ppermute | solution.py:41
  44.7 18.2 %collective-permute-start.5 = (bf16[32,64,128]{2,1,0:T(8,128)(2,1)S(1)}, bf16[32,64,128]{2,1,0:T(8,128)(2,1)S(1)}, u32[]{:S(2)}, u32[]{:S(2)}) collective-permute-start(bf16[32,64,128]{2,1,0:T(8,128)(2,1)S(1)} %all-to-all-done), channel_id=1, source_target_pairs={{0,8},{1,9},{2,10},{3,11},{4,12},{5,13},{6,14},{7,15},{8,16},{9,17... | collective-permute-start | bytes 1572872 | tf_op jit(solution)/shard_map/weights_neighbours/ppermute | solution.py:41
  46.7 9.7 %collective-permute-start.8 = (bf16[2,2,6,12,512]{4,3,2,1,0:T(8,128)(2,1)S(1)}, bf16[2,2,6,12,512]{4,3,2,1,0:T(8,128)(2,1)S(1)}, u32[]{:S(2)}, u32[]{:S(2)}) collective-permute-start(bf16[2,2,6,12,512]{4,3,2,1,0:T(8,128)(2,1)S(1)} %pad_maximum_fusion), channel_id=1, source_target_pairs={{0,15},{1,0},{2,1},{3,2},{4,3},{5,4},{6,5},{7,6},{8,7},{9,8},{10,9... | collective-permute-start | bytes 884744 | tf_op jit(solution)/shard_map/halos/ppermute | solution.py:452
  48.9 23.9 %collective-permute-start.4 = (bf16[32,64,128]{2,1,0:T(8,128)(2,1)S(1)}, bf16[32,64,128]{2,1,0:T(8,128)(2,1)}, u32[]{:S(2)}, u32[]{:S(2)}) collective-permute-start(bf16[32,64,128]{2,1,0:T(8,128)(2,1)S(1)} %all-to-all-done), channel_id=1, source_target_pairs={{0,1},{1,2},{2,3},{3,4},{4,5},{5,6},{6,7},{7,0},{8,9},{9,10},{10,1... | collective-permute-start | bytes 1572872 | tf_op jit(solution)/shard_map/weights_neighbours/ppermute | solution.py:41
  52.0 20.8 %collective-permute-start.3 = (bf16[32,64,128]{2,1,0:T(8,128)(2,1)S(1)}, bf16[32,64,128]{2,1,0:T(8,128)(2,1)}, u32[]{:S(2)}, u32[]{:S(2)}) collective-permute-start(bf16[32,64,128]{2,1,0:T(8,128)(2,1)S(1)} %all-to-all-done), channel_id=1, source_target_pairs={{0,33},{1,34},{2,35},{3,36},{4,37},{5,38},{6,39},{7,32},{8,41},{9,... | collective-permute-start | bytes 1572872 | tf_op jit(solution)/shard_map/weights_neighbours/ppermute | solution.py:41
  56.4 6.5 %copy-start.4 = (bf16[2,2,6,12,512]{4,3,2,1,0:T(8,128)(2,1)}, bf16[2,2,6,12,512]{4,3,2,1,0:T(8,128)(2,1)S(1)}, u32[]{:S(2)}) copy-start(bf16[2,2,6,12,512]{4,3,2,1,0:T(8,128)(2,1)S(1)} %collective-permute-done.8) | copy-start | bytes 884740
  56.4 16.4 %collective-permute-start.2 = (bf16[32,64,128]{2,1,0:T(8,128)(2,1)S(1)}, bf16[32,64,128]{2,1,0:T(8,128)(2,1)}, u32[]{:S(2)}, u32[]{:S(2)}) collective-permute-start(bf16[32,64,128]{2,1,0:T(8,128)(2,1)S(1)} %all-to-all-done), channel_id=1, source_target_pairs={{0,7},{1,0},{2,1},{3,2},{4,3},{5,4},{6,5},{7,6},{8,15},{9,8},{10,9... | collective-permute-start | bytes 1572872 | tf_op jit(solution)/shard_map/weights_neighbours/ppermute | solution.py:41
  58.9 13.9 %collective-permute-start.1 = (bf16[32,64,128]{2,1,0:T(8,128)(2,1)S(1)}, bf16[32,64,128]{2,1,0:T(8,128)(2,1)}, u32[]{:S(2)}, u32[]{:S(2)}) collective-permute-start(bf16[32,64,128]{2,1,0:T(8,128)(2,1)S(1)} %all-to-all-done), channel_id=1, source_target_pairs={{0,24},{1,25},{2,26},{3,27},{4,28},{5,29},{6,30},{7,31},{8,0},{9,1... | collective-permute-start | bytes 1572872 | tf_op jit(solution)/shard_map/weights_neighbours/ppermute | solution.py:41
  62.9 0.8 copy-start.2
  63.7 13.7 %collective-permute-start = (bf16[32,64,128]{2,1,0:T(8,128)(2,1)S(1)}, bf16[32,64,128]{2,1,0:T(8,128)(2,1)}, u32[]{:S(2)}, u32[]{:S(2)}) collective-permute-start(bf16[32,64,128]{2,1,0:T(8,128)(2,1)S(1)} %all-to-all-done), channel_id=1, source_target_pairs={{0,224},{1,225},{2,226},{3,227},{4,228},{5,229},{6,230},{7,231},{8... | collective-permute-start | bytes 1572872 | tf_op jit(solution)/shard_map/weights_neighbours/ppermute | solution.py:41
  101.6 19.5 %all-to-all-start.2 = ((bf16[16,48,128]{2,1,0:T(8,128)(2,1)}), bf16[16,48,128]{2,1,0:T(8,128)(2,1)S(1)}, u32[]{:S(2)}, u32[]{:S(2)}) async-start(bf16[16,48,128]{2,1,0:T(8,128)(2,1)} %sum_parts.2), calls=%async_computation.2 | async-start | bytes 393216 | tf_op jit(solution)/shard_map/adapter_sum/all_to_all | solution.py:523
  108.0 35.9 %collective-permute-start.11 = (bf16[2,3,24,512]{3,2,1,0:T(8,128)(2,1)S(1)}, bf16[2,3,24,512]{3,2,1,0:T(8,128)(2,1)S(1)}, u32[]{:S(2)}, u32[]{:S(2)}) collective-permute-start(bf16[2,3,24,512]{3,2,1,0:T(8,128)(2,1)S(1)} %get-tuple-element.179), channel_id=1, source_target_pairs={{0,272},{1,273},{2,274},{3,275},{4,276},{5,277},{6,278},{7,279},{8... | collective-permute-start | bytes 442376 | tf_op jit(solution)/shard_map/hand_over/ppermute | solution.py:444
  119.2 24.7 %collective-permute-start.12 = (bf16[2,3,24,512]{3,2,1,0:T(8,128)(2,1)S(1)}, bf16[2,3,24,512]{3,2,1,0:T(8,128)(2,1)S(1)}, u32[]{:S(2)}, u32[]{:S(2)}) collective-permute-start(bf16[2,3,24,512]{3,2,1,0:T(8,128)(2,1)S(1)} %get-tuple-element.180), channel_id=1, source_target_pairs={{0,256},{1,257},{2,258},{3,259},{4,260},{5,261},{6,262},{7,263},{8... | collective-permute-start | bytes 442376 | tf_op jit(solution)/shard_map/hand_over/ppermute | solution.py:444
  121.1 0.7 copy-start.5
  123.4 21.4 %all-to-all-start.3 = ((bf16[16,48,128]{2,1,0:T(8,128)(2,1)}), bf16[16,48,128]{2,1,0:T(8,128)(2,1)S(1)}, u32[]{:S(2)}, u32[]{:S(2)}) async-start(bf16[16,48,128]{2,1,0:T(8,128)(2,1)} %sum_parts.3), calls=%async_computation.3 | async-start | bytes 393216 | tf_op jit(solution)/shard_map/adapter_sum/all_to_all | solution.py:524
  127.0 12.5 %collective-permute-start.9 = (bf16[2,3,12,512]{3,2,1,0:T(8,128)(2,1)S(1)}, bf16[2,3,12,512]{3,2,1,0:T(8,128)(2,1)S(1)}, u32[]{:S(2)}, u32[]{:S(2)}) collective-permute-start(bf16[2,3,12,512]{3,2,1,0:T(8,128)(2,1)S(1)} %get-tuple-element.177), channel_id=1, source_target_pairs={{0,273},{1,274},{2,275},{3,276},{4,277},{5,278},{6,279},{7,280},{8... | collective-permute-start | bytes 221192 | tf_op jit(solution)/shard_map/hand_over/ppermute | solution.py:444
  135.9 8.0 %collective-permute-start.10 = (bf16[2,3,12,512]{3,2,1,0:T(8,128)(2,1)S(1)}, bf16[2,3,12,512]{3,2,1,0:T(8,128)(2,1)S(1)}, u32[]{:S(2)}, u32[]{:S(2)}) collective-permute-start(bf16[2,3,12,512]{3,2,1,0:T(8,128)(2,1)S(1)} %get-tuple-element.178), channel_id=1, source_target_pairs={{0,257},{1,258},{2,259},{3,260},{4,261},{5,262},{6,263},{7,264},{8... | collective-permute-start | bytes 221192 | tf_op jit(solution)/shard_map/hand_over/ppermute | solution.py:444

commit v4 on v3

--- a/solution.py
+++ b/solution.py
@@ -72,6 +72,7 @@
 
 def window_row(shape, dim):
     token = lax.broadcasted_iota(jnp.int32, shape, dim)
+    token = jnp.where(token >= 144, token - 144, token)
     token = jnp.where(token >= 72, token - 72, token)
     row = jnp.zeros(shape, jnp.int32)
     for edge in range(12, 72, 12):
@@ -80,26 +81,33 @@
 
 
 def bias_kernel(place_ref, pole_ref, index_ref, table_ref, bias_ref, allowed_ref):
-    for half in range(2):
-        lanes = slice(128 * half, 128 * half + 128)
+    lane = lax.broadcasted_iota(jnp.int32, (WT, 128), 1)
+    for part in range(3):
+        lanes = slice(128 * part, 128 * part + 128)
         index = index_ref[:, lanes]
         low = index & 127
         high = index >> 7
-        for head in range(HEADS):
-            found = jnp.zeros((WT, 128), F32)
+
+        def entries(head):
+            found = None
             for chunk in range(6):
-                entries = jnp.broadcast_to(
-                    table_ref[head : head + 1, 128 * chunk : 128 * chunk + 128], (WT, 128)
-                )
-                taken = jnp.take_along_axis(entries, low, axis=1)
+                row = table_ref[head : head + 1, 128 * chunk : 128 * chunk + 128]
+                taken = jnp.take_along_axis(jnp.broadcast_to(row, (WT, 128)), low, axis=1)
                 found = taken if chunk == 0 else jnp.where(high == chunk, taken, found)
-            bias_ref[head, :, lanes] = found
+            return found
+
+        for pair in range(HEADS // 2):
+            if part == 1:
+                found = jnp.where(lane < WT - 128, entries(2 * pair), entries(2 * pair + 1))
+            else:
+                found = entries(2 * pair + part // 2)
+            bias_ref[pair, :, lanes] = found
     first = place_ref[0] * 6 + 3
-    key_row = window_row((WT, 256), 0)
-    query_row = window_row((WT, 256), 1)
-    key_ok = jnp.zeros((WT, 256), jnp.int32)
-    key_region = jnp.zeros((WT, 256), jnp.int32)
-    query_region = jnp.zeros((WT, 256), jnp.int32)
+    key_row = window_row((WT, 384), 0)
+    query_row = window_row((WT, 384), 1)
+    key_ok = jnp.zeros((WT, 384), jnp.int32)
+    key_region = jnp.zeros((WT, 384), jnp.int32)
+    query_region = jnp.zeros((WT, 384), jnp.int32)
     for row in range(6):
         at = first + row
         moved = jnp.where(at >= 96, 1, 0)
@@ -235,7 +243,7 @@
     deep,
     place_ref, p0, p1, p2, p3, p4, p5, p6, p7, bias_ref, allowed_ref,
     normed_ref, cot_ref, scale_ref, low_q_ref, low_c_ref, aq_ref, bq_ref, ap_ref,
-    own_ref, side_ref, below_ref, corner_ref, grads_ref,
+    main_ref, strip_ref, grads_ref,
     weight, weight_p, xs, cols, aq_s, ap_s, flat,
 ):
     features, rank, windows, counts, starts = sizes(deep)
@@ -272,36 +280,38 @@
     chunks = [chunks[c] + low[:, 128 * c : 128 * c + 128] for c in range(12)]
     d_mixed = nn(cot_b, weight_p[...]) + nt(low_c, a_proj)
 
-    lane = lax.broadcasted_iota(jnp.int32, (WT, 128), 1)
-    allowed = allowed_ref[:, :WT] > 0.0
+    first_head = lax.broadcasted_iota(jnp.int32, (WT, 128), 1) < 64
+    allowed = allowed_ref[:, : 2 * WT] > 0.0
     mixed = [[None] * windows for _ in range(4)]
     d_chunks = [[None] * windows for _ in range(12)]
+
+    def by_head(value):
+        zero = jnp.zeros_like(value)
+        one, two = jnp.where(first_head, value, zero), jnp.where(first_head, zero, value)
+        return jnp.concatenate([one, two], 0)
+
+    def own_lanes(value):
+        return jnp.where(first_head, value[0:WT], value[WT : 2 * WT])
+
     for w in range(windows):
         rows = slice(WT * w, WT * w + WT)
         for pair in range(4):
-            q = chunks[pair][rows].astype(BF)
+            q = by_head(chunks[pair][rows].astype(BF) * 0.125)
             k = chunks[4 + pair][rows].astype(BF)
             v = chunks[8 + pair][rows].astype(BF)
-            d_o = d_mixed[rows, 128 * pair : 128 * pair + 128].astype(BF)
-            found = []
-            for half in range(2):
-                mine = (lane >= 64) if half else (lane < 64)
-                q_half = jnp.where(mine, q * 0.125, jnp.zeros_like(q))
-                v_half = jnp.where(mine, v, jnp.zeros_like(v))
-                s = nt(k, q_half) + bias_ref[2 * pair + half, :, :WT]
-                s = jnp.where(allowed, s, -1000000000.0)
-                e = jnp.exp(s - jnp.max(s, axis=0, keepdims=True))
-                p = e / jnp.sum(e, axis=0, keepdims=True)
-                p_b = p.astype(BF)
-                d_p = nt(v_half, d_o)
-                d_s = p * (d_p - jnp.sum(d_p * p, axis=0, keepdims=True))
-                d_s = jnp.where(allowed, d_s, 0.0).astype(BF)
-                found.append((tn(p_b, v), tn(d_s, k), nn(d_s, q), nn(p_b, d_o)))
-            both = [jnp.where(lane < 64, one, two) for one, two in zip(*found)]
-            mixed[pair][w] = both[0].astype(BF)
-            d_chunks[pair][w] = both[1] * 0.125
-            d_chunks[4 + pair][w] = both[2] * 0.125
-            d_chunks[8 + pair][w] = both[3]
+            d_o = by_head(d_mixed[rows, 128 * pair : 128 * pair + 128].astype(BF))
+            s = nt(k, q) + bias_ref[pair, :, : 2 * WT]
+            s = jnp.where(allowed, s, -1000000000.0)
+            e = jnp.exp(s - jnp.max(s, axis=0, keepdims=True))
+            p = e * (1.0 / jnp.sum(e, axis=0, keepdims=True))
+            p_b = p.astype(BF)
+            d_p = nt(v, d_o)
+            d_s = p * (d_p - jnp.sum(d_p * p, axis=0, keepdims=True))
+            d_s = jnp.where(allowed, d_s, 0.0).astype(BF)
+            mixed[pair][w] = own_lanes(tn(p_b, v)).astype(BF)
+            d_chunks[pair][w] = own_lanes(tn(d_s, k)) * 0.125
+            d_chunks[4 + pair][w] = nn(d_s, q)
+            d_chunks[8 + pair][w] = nn(p_b, d_o)
 
     def joined(parts, axis):
         return parts[0] if len(parts) == 1 else jnp.concatenate(parts, axis)
@@ -343,15 +353,14 @@
     for level in range(2):
         for row in range(6):
             at = 72 * level + 12 * row
-            main, strip = (own_ref, side_ref) if row < 3 else (below_ref, corner_ref)
             if deep:
                 for c in range(4):
                     lanes = slice(128 * c, 128 * c + 128)
                     for odd in range(2):
                         to = 512 * odd + 128 * c
                         cols[c, pl.ds(odd, 12, stride=2), :] = xs[at : at + 12, to : to + 128]
-                    main[level, row % 3, 12:24, lanes] = cols[c, 0:12].astype(BF)
-                    strip[level, row % 3, :, lanes] = cols[c, 12:24].astype(BF)
+                    main_ref[level, row, 12:24, lanes] = cols[c, 0:12].astype(BF)
+                    strip_ref[level, row, :, lanes] = cols[c, 12:24].astype(BF)
             else:
                 for c in range(4):
                     lanes = slice(128 * c, 128 * c + 128)
@@ -359,8 +368,8 @@
                     cols[c, 6:18] = xs[at : at + 12, lanes]
                     cols[c, 18:24] = xs[at + 144 : at + 150, lanes]
                     whole = cols[c].astype(BF)
-                    main[level, row % 3, :, lanes] = whole
-                    strip[level, row % 3, :, lanes] = whole[0:12]
+                    main_ref[level, row, :, lanes] = whole
+                    strip_ref[level, row, :, lanes] = whole[0:12]
 
 
 VMEM = pl.BlockSpec(memory_space=pltpu.VMEM)
@@ -395,14 +404,13 @@
     features = 1024 if deep else 512
     tokens = WT if deep else 2 * WT
     shapes = (
-        ((2, 3, 24, 512), BF), ((2, 3, 12, 512), BF), ((2, 3, 24, 512), BF),
-        ((2, 3, 12, 512), BF), ((768, 128), BF),
+        ((2, 6, 24, 512), BF), ((2, 6, 12, 512), BF), ((768, 128), BF),
     )
     return pl.pallas_call(
         functools.partial(block_kernel, deep),
         out_shape=tuple(jax.ShapeDtypeStruct(*shape) for shape in shapes),
         in_specs=[SMEM] + [VMEM] * (len(operands) - 1),
-        out_specs=(VMEM,) * 5,
+        out_specs=(VMEM,) * 3,
         scratch_shapes=[
             pltpu.VMEM((features, 2048), BF),
             pltpu.VMEM((features, 512), BF),
@@ -417,21 +425,9 @@
     )(*operands)
 
 
-def sum_kernel(parts_ref, out_ref):
-    total = parts_ref[0].astype(F32)
-    for i in range(1, 16):
-        total = total + parts_ref[i].astype(F32)
-    out_ref[...] = jnp.broadcast_to(total.astype(BF)[None], out_ref.shape)
-
-
 def summed(parts):
-    return pl.pallas_call(
-        sum_kernel,
-        out_shape=jax.ShapeDtypeStruct((16, 48, 128), BF),
-        in_specs=[pl.BlockSpec(memory_space=pltpu.VMEM)],
-        out_specs=pl.BlockSpec(memory_space=pltpu.VMEM),
-        name="sum_parts",
-    )(parts)
+    total = jnp.sum(parts.astype(F32), 0).astype(BF)
+    return jnp.broadcast_to(total[None], (16, 48, 128))
 
 
 def hand(value, d_lat, d_lon):
@@ -476,12 +472,12 @@
     with jax.named_scope("bias"):
         table = jnp.where(segment == 1, table_deep, table_shallow)
         table = jnp.pad(table.T, ((0, 0), (0, 768 - table.shape[0])))
-        index = jnp.pad(bias_index.T, ((0, 0), (0, 256 - WT)))
+        index = jnp.pad(jnp.concatenate([bias_index.T] * 2, 1), ((0, 0), (0, 384 - 2 * WT)))
         bias, allowed = pl.pallas_call(
             bias_kernel,
             out_shape=(
-                jax.ShapeDtypeStruct((HEADS, WT, 256), F32),
-                jax.ShapeDtypeStruct((WT, 256), F32),
+                jax.ShapeDtypeStruct((HEADS // 2, WT, 384), F32),
+                jax.ShapeDtypeStruct((WT, 384), F32),
             ),
             in_specs=[SMEM, SMEM, VMEM, VMEM],
             out_specs=(VMEM, VMEM),
@@ -508,28 +504,30 @@
         p5 = neighbour_send(piece, 0, 0, 1)
         p3 = neighbour_send(piece, 0, 0, -1)
 
-    own, side, below, corner, grads = lax.cond(
+    main, strip, grads = lax.cond(
         segment == 0,
         functools.partial(run_block, False),
         functools.partial(run_block, True),
         (place, piece, p1, p2, p3, p4, p5, p6, p7, bias, allowed, *prep),
     )
 
+    with jax.named_scope("adapter_sum_lon"):
+        grads = lax.all_to_all(grads.reshape(16, 48, 128), "lon", 0, 0)
     with jax.named_scope("hand_over"):
-        own, side = hand(own, 0, 0), hand(side, 0, 1)
-        below, corner = hand(below, 1, 0), hand(corner, 1, 1)
-    with jax.named_scope("adapter_sum"):
-        grads = lax.all_to_all(grads.reshape(16, 48, 128), "lon", 0, 0)
+        strip = shift(strip, 0, 1)
+        strip = jnp.pad(strip, ((0, 0), (0, 0), (0, 12), (0, 0)))
+        column = lax.broadcasted_iota(jnp.int32, (1, 1, 24, 1), 2)
+        main = jnp.where(column < jnp.where(segment == 0, 6, 12), strip, main)
+        grads, main = lax.optimization_barrier((grads, main))
+        own, below = hand(main[:, :3], 0, 0), hand(main[:, 3:], 1, 0)
+    with jax.named_scope("adapter_sum_lat"):
         grads = lax.all_to_all(summed(grads), "lat", 0, 0)
+        grads, own, below = lax.optimization_barrier((grads, own, below))
+    with jax.named_scope("adapter_gather"):
         grads = lax.all_to_all(summed(grads), "lon", 0, 0)
         adapter_sum = grads.astype(F32).reshape(1, 98304)
     with jax.named_scope("assemble"):
-        edge = jnp.where(segment == 0, 12, 6)
-        column = lax.broadcasted_iota(jnp.int32, (1, 1, 24, 1), 2)
-        main = jnp.concatenate([below, own], 1)
-        strip = jnp.concatenate([corner, side], 1)
-        strip = jnp.pad(strip, ((0, 0), (0, 0), (0, 12), (0, 0)))
-        gradient = jnp.where(column < edge, strip, main)
+        gradient = jnp.concatenate([below, own], 1)
     return gradient[None], adapter_sum
 
 

time: 146 us -> 142 us (0.973); the launches traced: 146 us -> 140 us
  waiting for transfers between devices: 18.8 us -> 31.1 us
  blocking collectives: 11.8 us -> 0 us
  Pallas kernels: 25.2 us -> 21.7 us
  starting transfers between devices: 83 us -> 79.9 us
    all_to_all x1 -> x0, blocking collectives: 11.8 us -> none  [shards(): grads = lax.all_to_all(grads.reshape(16, 48, 128), 'lon', 0, 0)]
    ppermute x4 -> x2, starting transfers between devices: 23.9 us -> 12.5 us  [hand(): return lax.ppermute(value, ('segment', 'lat', 'lon'), route)]
    all_to_all x1, waiting for transfers between devices: 0.01 us -> 6.7 us  [shards(): grads = lax.all_to_all(summed(grads), 'lon', 0, 0)]
    all_to_all x0 -> x1, waiting for transfers between devices: none -> 6.43 us  [shards(): grads = lax.all_to_all(grads.reshape(16, 48, 128), 'lon', 0, 0)]
    all_to_all x0 -> x1, starting transfers between devices: none -> 4.02 us  [shards(): grads = lax.all_to_all(grads.reshape(16, 48, 128), 'lon', 0, 0)]
    ppermute x2 -> x3, starting transfers between devices: 9.82 us -> 13.4 us  [shift(): return lax.ppermute(value, BOTH, route)]
    pallas_call x3 -> x1, Pallas kernels: 9.73 us -> 6.53 us  [shards(): pl.pallas_call(bias_kernel, out_shape=(jax.ShapeDtypeStruct((HEADS // 2,...]
    ppermute x2 -> x3, waiting for transfers between devices: 2.49 us -> 3.41 us  [shift(): return lax.ppermute(value, BOTH, route)]
  transfers between devices with their start and end apart: 16 -> 16, of which waited for: 6 -> 8; matrix products, arithmetic and copies ran while one was open for 2% -> 2% of each run, Pallas kernels for 8% -> 7%
where the time goes in v4:
time: 142 us; the launch traced here: 140 us
  starting transfers between devices  79.9 us (56%)
  waiting for transfers between devices  31.1 us (22%)
  Pallas kernels  21.7 us (15%)
  local copies, waits for them, and re-layouts  3.54 us (2%)
  other arithmetic  2.74 us (2%)
    ppermute x7, starting transfers between devices, neighbour_send(): return lax.ppermute(value, BOTH, route)  21.1 us
    all_to_all x1, starting transfers between devices, shards(): piece = lax.all_to_all(own_w, BOTH, 0, 0, axis_index_groups=class_groups())  18.3 us
    ppermute x3, starting transfers between devices, shift(): return lax.ppermute(value, BOTH, route)  13.4 us
    ppermute x2, starting transfers between devices, hand(): return lax.ppermute(value, ('segment', 'lat', 'lon'), route)  12.5 us
    pallas_call x1, Pallas kernels, run_block(): pl.pallas_call(functools.partial(block_kernel, deep), out_shape=tuple((ja...  10.2 us
    all_to_all x1, starting transfers between devices, shards(): grads = lax.all_to_all(summed(grads), 'lat', 0, 0)  7.04 us
    all_to_all x1, waiting for transfers between devices, shards(): grads = lax.all_to_all(summed(grads), 'lon', 0, 0)  6.7 us
    pallas_call x1, Pallas kernels, shards(): pl.pallas_call(bias_kernel, out_shape=(jax.ShapeDtypeStruct((HEADS // 2,...  6.53 us
  transfers between devices with their start and end apart: 16, of which 8 were waited for; matrix products, arithmetic and copies ran while one was open for 2% of the time, Pallas kernels for 7%

profile of v4, /device:TPU:1, one launch (start us, length us, event | category | flops | bytes accessed | tf_op | source)
XLA Modules:
  0.0 140.0 jit_solution(8492495012816402722)
XLA Ops:
  0.7 0.1 pad_add_fusion.1.place_ref
  0.8 1.9 %pack_weights.1 = bf16[32,64,128]{2,1,0:T(8,128)(2,1)} custom-call(s32[3]{0:T(128)S(1)} %pad_add_fusion.1.place_ref, bf16[32,96]{1,0:T(8,128)(2,1)} %qs_ref.1, bf16[32,32]{1,0:T(8,128)(2,1)} %ps_ref.1, bf16[64,96]{1,0:T(8,128)(2,1)} %qd_ref.1, bf16[32,64]{1,0:T(8,128)(2,1)} %pd_ref.1), custom_call_target="tpu_custom_call" | custom-call | tf_op jit(solution)/shard_map/pack/pack_weights/pallas_call | solution.py:463
  2.6 18.3 %all-to-all-start = ((bf16[32,64,128]{2,1,0:T(8,128)(2,1)}), bf16[32,64,128]{2,1,0:T(8,128)(2,1)S(1)}, u32[]{:S(2)}, u32[]{:S(2)}) async-start(bf16[32,64,128]{2,1,0:T(8,128)(2,1)} %pack_weights.1), calls=%async_computation | async-start | bytes 1048576 | tf_op jit(solution)/shard_map/weights_class/all_to_all | solution.py:471
  21.0 0.0 copy-start.3
  21.0 0.7 pad_maximum_fusion.1
  21.7 7.6 %collective-permute-start.7 = (bf16[2,2,3,24,512]{4,3,2,1,0:T(8,128)(2,1)}, bf16[2,2,3,24,512]{4,3,2,1,0:T(8,128)(2,1)S(1)}, u32[]{:S(2)}, u32[]{:S(2)}) collective-permute-start(bf16[2,2,3,24,512]{4,3,2,1,0:T(8,128)(2,1)} %pad_maximum_fusion.1), channel_id=1, source_target_pairs={{0,240},{1,241},{2,242},{3,243},{4,244},{5,245},{6,246},{7,247},{8... | collective-permute-start | bytes 884744 | tf_op jit(solution)/shard_map/halos/ppermute | solution.py:448
  29.4 0.0 copy-start.4
  29.4 0.0 copy-start.5
  29.4 0.1 copy.13
  29.5 0.6 copy-done.4
  30.1 0.0 copy-done.5
  30.2 0.1 pad_add_fusion
  30.3 0.7 pad.12.index_ref
  31.0 0.6 pad.13.table_ref
  31.6 6.5 %bias_table.1 = (f32[4,144,384]{2,1,0:T(8,128)S(1)}, f32[144,384]{1,0:T(8,128)}) custom-call(s32[3]{0:T(128)S(1)} %pad_add_fusion.1.place_ref, s32[96]{0:T(128)} %pole_ref.1, s32[144,384]{1,0:T(8,128)} %pad.12.index_ref, f32[8,768]{1,0:T(8,128)} %pad.13.table_ref), custom_call_target="tpu_custom_call" | custom-call | tf_op jit(solution)/shard_map/bias/bias_table/pallas_call | solution.py:476
  38.1 4.5 %all-to-all-done = bf16[32,64,128]{2,1,0:T(8,128)(2,1)S(1)} async-done(((bf16[32,64,128]{2,1,0:T(8,128)(2,1)}), bf16[32,64,128]{2,1,0:T(8,128)(2,1)S(1)}, u32[]{:S(2)}, u32[]{:S(2)}) %all-to-all-start) | async-done | bytes 524320 | tf_op jit(solution)/shard_map/weights_class/all_to_all | solution.py:471
  42.6 2.0 %collective-permute-start.6 = (bf16[32,64,128]{2,1,0:T(8,128)(2,1)S(1)}, bf16[32,64,128]{2,1,0:T(8,128)(2,1)S(1)}, u32[]{:S(2)}, u32[]{:S(2)}) collective-permute-start(bf16[32,64,128]{2,1,0:T(8,128)(2,1)S(1)} %all-to-all-done), channel_id=1, source_target_pairs={{0,32},{1,33},{2,34},{3,35},{4,36},{5,37},{6,38},{7,39},{8,40},{9,... | collective-permute-start | bytes 1572872 | tf_op jit(solution)/shard_map/weights_neighbours/ppermute | solution.py:41
  44.6 1.9 %collective-permute-start.5 = (bf16[32,64,128]{2,1,0:T(8,128)(2,1)S(1)}, bf16[32,64,128]{2,1,0:T(8,128)(2,1)S(1)}, u32[]{:S(2)}, u32[]{:S(2)}) collective-permute-start(bf16[32,64,128]{2,1,0:T(8,128)(2,1)S(1)} %all-to-all-done), channel_id=1, source_target_pairs={{0,8},{1,9},{2,10},{3,11},{4,12},{5,13},{6,14},{7,15},{8,16},{9,17... | collective-permute-start | bytes 1572872 | tf_op jit(solution)/shard_map/weights_neighbours/ppermute | solution.py:41
  46.6 0.0 collective-permute-done.7
  46.6 0.1 pad_maximum_fusion
  46.7 2.2 %collective-permute-start.8 = (bf16[2,2,6,12,512]{4,3,2,1,0:T(8,128)(2,1)S(1)}, bf16[2,2,6,12,512]{4,3,2,1,0:T(8,128)(2,1)S(1)}, u32[]{:S(2)}, u32[]{:S(2)}) collective-permute-start(bf16[2,2,6,12,512]{4,3,2,1,0:T(8,128)(2,1)S(1)} %pad_maximum_fusion), channel_id=1, source_target_pairs={{0,15},{1,0},{2,1},{3,2},{4,3},{5,4},{6,5},{7,6},{8,7},{9,8},{10,9... | collective-permute-start | bytes 884744 | tf_op jit(solution)/shard_map/halos/ppermute | solution.py:448
  48.8 3.1 %collective-permute-start.4 = (bf16[32,64,128]{2,1,0:T(8,128)(2,1)S(1)}, bf16[32,64,128]{2,1,0:T(8,128)(2,1)}, u32[]{:S(2)}, u32[]{:S(2)}) collective-permute-start(bf16[32,64,128]{2,1,0:T(8,128)(2,1)S(1)} %all-to-all-done), channel_id=1, source_target_pairs={{0,1},{1,2},{2,3},{3,4},{4,5},{5,6},{6,7},{7,0},{8,9},{9,10},{10,1... | collective-permute-start | bytes 1572872 | tf_op jit(solution)/shard_map/weights_neighbours/ppermute | solution.py:41
  52.0 1.9 %collective-permute-start.3 = (bf16[32,64,128]{2,1,0:T(8,128)(2,1)S(1)}, bf16[32,64,128]{2,1,0:T(8,128)(2,1)}, u32[]{:S(2)}, u32[]{:S(2)}) collective-permute-start(bf16[32,64,128]{2,1,0:T(8,128)(2,1)S(1)} %all-to-all-done), channel_id=1, source_target_pairs={{0,33},{1,34},{2,35},{3,36},{4,37},{5,38},{6,39},{7,32},{8,41},{9,... | collective-permute-start | bytes 1572872 | tf_op jit(solution)/shard_map/weights_neighbours/ppermute | solution.py:41
  53.9 2.5 %collective-permute-done.8 = bf16[2,2,6,12,512]{4,3,2,1,0:T(8,128)(2,1)S(1)} collective-permute-done((bf16[2,2,6,12,512]{4,3,2,1,0:T(8,128)(2,1)S(1)}, bf16[2,2,6,12,512]{4,3,2,1,0:T(8,128)(2,1)S(1)}, u32[]{:S(2)}, u32[]{:S(2)}) %collective-permute-start.8) | collective-permute-done | bytes 294944 | tf_op jit(solution)/shard_map/halos/ppermute | solution.py:448
  56.4 2.4 %collective-permute-start.2 = (bf16[32,64,128]{2,1,0:T(8,128)(2,1)S(1)}, bf16[32,64,128]{2,1,0:T(8,128)(2,1)}, u32[]{:S(2)}, u32[]{:S(2)}) collective-permute-start(bf16[32,64,128]{2,1,0:T(8,128)(2,1)S(1)} %all-to-all-done), channel_id=1, source_target_pairs={{0,7},{1,0},{2,1},{3,2},{4,3},{5,4},{6,5},{7,6},{8,15},{9,8},{10,9... | collective-permute-start | bytes 1572872 | tf_op jit(solution)/shard_map/weights_neighbours/ppermute | solution.py:41
  58.8 4.0 %collective-permute-start.1 = (bf16[32,64,128]{2,1,0:T(8,128)(2,1)S(1)}, bf16[32,64,128]{2,1,0:T(8,128)(2,1)}, u32[]{:S(2)}, u32[]{:S(2)}) collective-permute-start(bf16[32,64,128]{2,1,0:T(8,128)(2,1)S(1)} %all-to-all-done), channel_id=1, source_target_pairs={{0,24},{1,25},{2,26},{3,27},{4,28},{5,29},{6,30},{7,31},{8,0},{9,1... | collective-permute-start | bytes 1572872 | tf_op jit(solution)/shard_map/weights_neighbours/ppermute | solution.py:41
  62.8 5.8 %collective-permute-start = (bf16[32,64,128]{2,1,0:T(8,128)(2,1)S(1)}, bf16[32,64,128]{2,1,0:T(8,128)(2,1)}, u32[]{:S(2)}, u32[]{:S(2)}) collective-permute-start(bf16[32,64,128]{2,1,0:T(8,128)(2,1)S(1)} %all-to-all-done), channel_id=1, source_target_pairs={{0,224},{1,225},{2,226},{3,227},{4,228},{5,229},{6,230},{7,231},{8... | collective-permute-start | bytes 1572872 | tf_op jit(solution)/shard_map/weights_neighbours/ppermute | solution.py:41
  68.6 3.1 %conditional.2 = ((bf16[288,512]{1,0:T(8,128)(2,1)}, bf16[288,512]{1,0:T(8,128)(2,1)}, f32[288,128]{1,0:T(8,128)S(1)}, bf16[288,32]{1,0:T(8,128)(2,1)}, bf16[288...) conditional(s32[]{:T(128)} %convert_element_type.6, ...), branch_computations={%region_0.1_spmd, %region_1.2_spmd} | conditional | bytes 8 | solution.py:492
  68.7 3.1 %deep_prep.1 = (bf16[288,512]{1,0:T(8,128)(2,1)}, bf16[288,512]{1,0:T(8,128)(2,1)}, f32[288,128]{1,0:T(8,128)S(1)}, bf16[288,32]{1,0:T(8,128)(2,1)}, bf16[288,32...) custom-call(bf16[2,6,24,512]{3,2,1,0:T(8,128)(2,1)S(1)} %get-tuple-element.96.x_ref, ...), custom_call_target="tpu_custom_call" | custom-call | tf_op jit(solution)/shard_map/prep/cond/branch_0_fun/deep_prep/pallas_call | solution.py:385
  71.8 0.9 collective-permute-done.4
  72.7 3.8 %collective-permute-done = bf16[32,64,128]{2,1,0:T(8,128)(2,1)} collective-permute-done((bf16[32,64,128]{2,1,0:T(8,128)(2,1)S(1)}, bf16[32,64,128]{2,1,0:T(8,128)(2,1)}, u32[]{:S(2)}, u32[]{:S(2)}) %collective-permute-start) | collective-permute-done | bytes 524320 | tf_op jit(solution)/shard_map/weights_neighbours/ppermute | solution.py:41
  76.6 10.2 %conditional.3 = ((bf16[2,6,24,512]{3,2,1,0:T(8,128)(2,1)S(1)}, bf16[2,6,12,512]{3,2,1,0:T(8,128)(2,1)S(1)}, bf16[768,128]{1,0:T(8,128)(2,1)})) conditional(s32[]{:T(128)} %convert_element_type.6, (s32[3]{0:T(128)S(1)}, bf16[32,64,128]{2,1,0:T(8,128)(2,1)S(1)}, bf16[32,64,128]{2,1,0:T(8,128)(2,1)}, bf16[32,64,128]{2,1,0:T(8,128)(2,1)}, ...), branch_computations={%region_2.3_spmd, %region_3.4_spmd} | conditional | bytes 8 | solution.py:507
  76.6 10.2 %deep_block.1 = (bf16[2,6,24,512]{3,2,1,0:T(8,128)(2,1)S(1)}, bf16[2,6,12,512]{3,2,1,0:T(8,128)(2,1)S(1)}, bf16[768,128]{1,0:T(8,128)(2,1)}) custom-call(s32[3]{0:T(128)S(1)} %get-tuple-element.106.place_ref, bf16[32,64,128]{2,1,0:T(8,128)(2,1)S(1)} %get-tuple-element.107.p0, bf16[32,64,128]{2,1,0:T(8,128)(2,1)} %get-tuple-element.108.p1, ...), custom_call_target="tpu_custom_call" | custom-call | tf_op jit(solution)/shard_map/cond/branch_0_fun/deep_block/pallas_call | solution.py:409
  86.8 3.5 %collective-permute-start.9 = (bf16[2,6,12,512]{3,2,1,0:T(8,128)(2,1)S(1)}, bf16[2,6,12,512]{3,2,1,0:T(8,128)(2,1)S(1)}, u32[]{:S(2)}, u32[]{:S(2)}) collective-permute-start(bf16[2,6,12,512]{3,2,1,0:T(8,128)(2,1)S(1)} %get-tuple-element.181), channel_id=1, source_target_pairs={{0,1},{1,2},{2,3},{3,4},{4,5},{5,6},{6,7},{7,8},{8,9},{9,10},{10,1... | collective-permute-start | bytes 442376 | tf_op jit(solution)/shard_map/hand_over/ppermute | solution.py:448
  90.3 4.0 %all-to-all-start.1 = ((bf16[16,48,128]{2,1,0:T(8,128)(2,1)}), bf16[16,48,128]{2,1,0:T(8,128)(2,1)S(1)}, u32[]{:S(2)}, u32[]{:S(2)}) async-start(bf16[16,48,128]{2,1,0:T(8,128)(2,1)} %bitcast.12), calls=%async_computation.1 | async-start | bytes 393216 | tf_op jit(solution)/shard_map/adapter_sum_lon/all_to_all | solution.py:515
  94.4 0.9 collective-permute-done.9
  95.3 0.2 pad_select_fusion
  95.5 6.4 %all-to-all-done.1 = bf16[16,48,128]{2,1,0:T(8,128)(2,1)S(1)} async-done(((bf16[16,48,128]{2,1,0:T(8,128)(2,1)}), bf16[16,48,128]{2,1,0:T(8,128)(2,1)S(1)}, u32[]{:S(2)}, u32[]{:S(2)}) %all-to-all-start.1) | async-done | bytes 196640 | tf_op jit(solution)/shard_map/adapter_sum_lon/all_to_all | solution.py:515
  102.0 0.7 broadcast_in_dim.24
  102.7 7.0 %all-to-all-start.2 = ((bf16[16,48,128]{2,1,0:T(8,128)(2,1)}), bf16[16,48,128]{2,1,0:T(8,128)(2,1)S(1)}, u32[]{:S(2)}, u32[]{:S(2)}) async-start(bf16[16,48,128]{2,1,0:T(8,128)(2,1)} %broadcast_in_dim.24), calls=%async_computation.2 | async-start | bytes 393216 | tf_op jit(solution)/shard_map/adapter_sum_lat/all_to_all | solution.py:524
  109.7 10.6 %collective-permute-start.11 = (bf16[2,3,24,512]{3,2,1,0:T(8,128)(2,1)S(1)}, bf16[2,3,24,512]{3,2,1,0:T(8,128)(2,1)S(1)}, u32[]{:S(2)}, u32[]{:S(2)}) collective-permute-start(bf16[2,3,24,512]{3,2,1,0:T(8,128)(2,1)S(1)} %get-tuple-element.188), channel_id=1, source_target_pairs={{0,272},{1,273},{2,274},{3,275},{4,276},{5,277},{6,278},{7,279},{8... | collective-permute-start | bytes 442376 | tf_op jit(solution)/shard_map/hand_over/ppermute | solution.py:440
  120.3 1.9 %collective-permute-start.10 = (bf16[2,3,24,512]{3,2,1,0:T(8,128)(2,1)S(1)}, bf16[2,3,24,512]{3,2,1,0:T(8,128)(2,1)S(1)}, u32[]{:S(2)}, u32[]{:S(2)}) collective-permute-start(bf16[2,3,24,512]{3,2,1,0:T(8,128)(2,1)S(1)} %get-tuple-element.189), channel_id=1, source_target_pairs={{0,256},{1,257},{2,258},{3,259},{4,260},{5,261},{6,262},{7,263},{8... | collective-permute-start | bytes 442376 | tf_op jit(solution)/shard_map/hand_over/ppermute | solution.py:440
  122.3 5.2 %collective-permute-done.11 = bf16[2,3,24,512]{3,2,1,0:T(8,128)(2,1)S(1)} collective-permute-done((bf16[2,3,24,512]{3,2,1,0:T(8,128)(2,1)S(1)}, bf16[2,3,24,512]{3,2,1,0:T(8,128)(2,1)S(1)}, u32[]{:S(2)}, u32[]{:S(2)}) %collective-permute-start.11) | collective-permute-done | bytes 147488 | tf_op jit(solution)/shard_map/hand_over/ppermute | solution.py:440
  127.6 0.7 broadcast_in_dim.26
  128.3 3.5 %all-to-all-start.3 = ((bf16[16,48,128]{2,1,0:T(8,128)(2,1)}), bf16[16,48,128]{2,1,0:T(8,128)(2,1)S(1)}, u32[]{:S(2)}, u32[]{:S(2)}) async-start(bf16[16,48,128]{2,1,0:T(8,128)(2,1)} %broadcast_in_dim.26), calls=%async_computation.3 | async-start | bytes 393216 | tf_op jit(solution)/shard_map/adapter_gather/all_to_all | solution.py:527
  131.8 0.7 maximum_bitcast_fusion
  132.5 6.7 %all-to-all-done.3 = bf16[16,48,128]{2,1,0:T(8,128)(2,1)S(1)} async-done(((bf16[16,48,128]{2,1,0:T(8,128)(2,1)}), bf16[16,48,128]{2,1,0:T(8,128)(2,1)S(1)}, u32[]{:S(2)}, u32[]{:S(2)}) %all-to-all-start.3) | async-done | bytes 196640 | tf_op jit(solution)/shard_map/adapter_gather/all_to_all | solution.py:527
  139.2 0.8 reshape.27
  (22 shorter events, 0.2 us)
Async XLA Ops:
  2.6 18.3 %copy-start = (bf16[1,2,6,24,512]{4,3,2,1,0:T(8,128)(2,1)S(1)}, bf16[1,2,6,24,512]{4,3,2,1,0:T(8,128)(2,1)}, u32[]{:S(2)}) copy-start(bf16[1,2,6,24,512]{4,3,2,1,0:T(8,128)(2,1)} %param.15) | copy-start | bytes 884740
  2.6 18.3 %copy-start.1 = (bf16[1,2,6,24,512]{4,3,2,1,0:T(8,128)(2,1)S(1)}, bf16[1,2,6,24,512]{4,3,2,1,0:T(8,128)(2,1)}, u32[]{:S(2)}) copy-start(bf16[1,2,6,24,512]{4,3,2,1,0:T(8,128)(2,1)} %param.16) | copy-start | bytes 884740
  2.6 40.0 %all-to-all-start = ((bf16[32,64,128]{2,1,0:T(8,128)(2,1)}), bf16[32,64,128]{2,1,0:T(8,128)(2,1)S(1)}, u32[]{:S(2)}, u32[]{:S(2)}) async-start(bf16[32,64,128]{2,1,0:T(8,128)(2,1)} %pack_weights.1), calls=%async_computation | async-start | bytes 1048576 | tf_op jit(solution)/shard_map/weights_class/all_to_all | solution.py:471
  21.0 8.4 %copy-start.3 = (s32[144,144]{1,0:T(8,128)S(1)}, s32[144,144]{1,0:T(8,128)}, u32[]{:S(2)}) copy-start(s32[144,144]{1,0:T(8,128)} %param.18) | copy-start | bytes 248836
  21.7 24.8 %collective-permute-start.7 = (bf16[2,2,3,24,512]{4,3,2,1,0:T(8,128)(2,1)}, bf16[2,2,3,24,512]{4,3,2,1,0:T(8,128)(2,1)S(1)}, u32[]{:S(2)}, u32[]{:S(2)}) collective-permute-start(bf16[2,2,3,24,512]{4,3,2,1,0:T(8,128)(2,1)} %pad_maximum_fusion.1), channel_id=1, source_target_pairs={{0,240},{1,241},{2,242},{3,243},{4,244},{5,245},{6,246},{7,247},{8... | collective-permute-start | bytes 884744 | tf_op jit(solution)/shard_map/halos/ppermute | solution.py:448
  29.4 0.7 copy-start.4
  29.4 0.7 copy-start.5
  42.6 16.2 %collective-permute-start.6 = (bf16[32,64,128]{2,1,0:T(8,128)(2,1)S(1)}, bf16[32,64,128]{2,1,0:T(8,128)(2,1)S(1)}, u32[]{:S(2)}, u32[]{:S(2)}) collective-permute-start(bf16[32,64,128]{2,1,0:T(8,128)(2,1)S(1)} %all-to-all-done), channel_id=1, source_target_pairs={{0,32},{1,33},{2,34},{3,35},{4,36},{5,37},{6,38},{7,39},{8,40},{9,... | collective-permute-start | bytes 1572872 | tf_op jit(solution)/shard_map/weights_neighbours/ppermute | solution.py:41
  44.6 18.2 %collective-permute-start.5 = (bf16[32,64,128]{2,1,0:T(8,128)(2,1)S(1)}, bf16[32,64,128]{2,1,0:T(8,128)(2,1)S(1)}, u32[]{:S(2)}, u32[]{:S(2)}) collective-permute-start(bf16[32,64,128]{2,1,0:T(8,128)(2,1)S(1)} %all-to-all-done), channel_id=1, source_target_pairs={{0,8},{1,9},{2,10},{3,11},{4,12},{5,13},{6,14},{7,15},{8,16},{9,17... | collective-permute-start | bytes 1572872 | tf_op jit(solution)/shard_map/weights_neighbours/ppermute | solution.py:41
  46.7 9.7 %collective-permute-start.8 = (bf16[2,2,6,12,512]{4,3,2,1,0:T(8,128)(2,1)S(1)}, bf16[2,2,6,12,512]{4,3,2,1,0:T(8,128)(2,1)S(1)}, u32[]{:S(2)}, u32[]{:S(2)}) collective-permute-start(bf16[2,2,6,12,512]{4,3,2,1,0:T(8,128)(2,1)S(1)} %pad_maximum_fusion), channel_id=1, source_target_pairs={{0,15},{1,0},{2,1},{3,2},{4,3},{5,4},{6,5},{7,6},{8,7},{9,8},{10,9... | collective-permute-start | bytes 884744 | tf_op jit(solution)/shard_map/halos/ppermute | solution.py:448
  48.8 23.9 %collective-permute-start.4 = (bf16[32,64,128]{2,1,0:T(8,128)(2,1)S(1)}, bf16[32,64,128]{2,1,0:T(8,128)(2,1)}, u32[]{:S(2)}, u32[]{:S(2)}) collective-permute-start(bf16[32,64,128]{2,1,0:T(8,128)(2,1)S(1)} %all-to-all-done), channel_id=1, source_target_pairs={{0,1},{1,2},{2,3},{3,4},{4,5},{5,6},{6,7},{7,0},{8,9},{9,10},{10,1... | collective-permute-start | bytes 1572872 | tf_op jit(solution)/shard_map/weights_neighbours/ppermute | solution.py:41
  52.0 20.8 %collective-permute-start.3 = (bf16[32,64,128]{2,1,0:T(8,128)(2,1)S(1)}, bf16[32,64,128]{2,1,0:T(8,128)(2,1)}, u32[]{:S(2)}, u32[]{:S(2)}) collective-permute-start(bf16[32,64,128]{2,1,0:T(8,128)(2,1)S(1)} %all-to-all-done), channel_id=1, source_target_pairs={{0,33},{1,34},{2,35},{3,36},{4,37},{5,38},{6,39},{7,32},{8,41},{9,... | collective-permute-start | bytes 1572872 | tf_op jit(solution)/shard_map/weights_neighbours/ppermute | solution.py:41
  56.4 6.5 %copy-start.2 = (bf16[2,2,6,12,512]{4,3,2,1,0:T(8,128)(2,1)}, bf16[2,2,6,12,512]{4,3,2,1,0:T(8,128)(2,1)S(1)}, u32[]{:S(2)}) copy-start(bf16[2,2,6,12,512]{4,3,2,1,0:T(8,128)(2,1)S(1)} %collective-permute-done.8) | copy-start | bytes 884740
  56.4 16.4 %collective-permute-start.2 = (bf16[32,64,128]{2,1,0:T(8,128)(2,1)S(1)}, bf16[32,64,128]{2,1,0:T(8,128)(2,1)}, u32[]{:S(2)}, u32[]{:S(2)}) collective-permute-start(bf16[32,64,128]{2,1,0:T(8,128)(2,1)S(1)} %all-to-all-done), channel_id=1, source_target_pairs={{0,7},{1,0},{2,1},{3,2},{4,3},{5,4},{6,5},{7,6},{8,15},{9,8},{10,9... | collective-permute-start | bytes 1572872 | tf_op jit(solution)/shard_map/weights_neighbours/ppermute | solution.py:41
  58.8 13.9 %collective-permute-start.1 = (bf16[32,64,128]{2,1,0:T(8,128)(2,1)S(1)}, bf16[32,64,128]{2,1,0:T(8,128)(2,1)}, u32[]{:S(2)}, u32[]{:S(2)}) collective-permute-start(bf16[32,64,128]{2,1,0:T(8,128)(2,1)S(1)} %all-to-all-done), channel_id=1, source_target_pairs={{0,24},{1,25},{2,26},{3,27},{4,28},{5,29},{6,30},{7,31},{8,0},{9,1... | collective-permute-start | bytes 1572872 | tf_op jit(solution)/shard_map/weights_neighbours/ppermute | solution.py:41
  62.8 13.7 %collective-permute-start = (bf16[32,64,128]{2,1,0:T(8,128)(2,1)S(1)}, bf16[32,64,128]{2,1,0:T(8,128)(2,1)}, u32[]{:S(2)}, u32[]{:S(2)}) collective-permute-start(bf16[32,64,128]{2,1,0:T(8,128)(2,1)S(1)} %all-to-all-done), channel_id=1, source_target_pairs={{0,224},{1,225},{2,226},{3,227},{4,228},{5,229},{6,230},{7,231},{8... | collective-permute-start | bytes 1572872 | tf_op jit(solution)/shard_map/weights_neighbours/ppermute | solution.py:41
  86.8 8.5 %collective-permute-start.9 = (bf16[2,6,12,512]{3,2,1,0:T(8,128)(2,1)S(1)}, bf16[2,6,12,512]{3,2,1,0:T(8,128)(2,1)S(1)}, u32[]{:S(2)}, u32[]{:S(2)}) collective-permute-start(bf16[2,6,12,512]{3,2,1,0:T(8,128)(2,1)S(1)} %get-tuple-element.181), channel_id=1, source_target_pairs={{0,1},{1,2},{2,3},{3,4},{4,5},{5,6},{6,7},{7,8},{8,9},{9,10},{10,1... | collective-permute-start | bytes 442376 | tf_op jit(solution)/shard_map/hand_over/ppermute | solution.py:448
  90.3 11.6 %all-to-all-start.1 = ((bf16[16,48,128]{2,1,0:T(8,128)(2,1)}), bf16[16,48,128]{2,1,0:T(8,128)(2,1)S(1)}, u32[]{:S(2)}, u32[]{:S(2)}) async-start(bf16[16,48,128]{2,1,0:T(8,128)(2,1)} %bitcast.12), calls=%async_computation.1 | async-start | bytes 393216 | tf_op jit(solution)/shard_map/adapter_sum_lon/all_to_all | solution.py:515
  102.7 24.9 %all-to-all-start.2 = ((bf16[16,48,128]{2,1,0:T(8,128)(2,1)}), bf16[16,48,128]{2,1,0:T(8,128)(2,1)S(1)}, u32[]{:S(2)}, u32[]{:S(2)}) async-start(bf16[16,48,128]{2,1,0:T(8,128)(2,1)} %broadcast_in_dim.24), calls=%async_computation.2 | async-start | bytes 393216 | tf_op jit(solution)/shard_map/adapter_sum_lat/all_to_all | solution.py:524
  109.7 17.8 %collective-permute-start.11 = (bf16[2,3,24,512]{3,2,1,0:T(8,128)(2,1)S(1)}, bf16[2,3,24,512]{3,2,1,0:T(8,128)(2,1)S(1)}, u32[]{:S(2)}, u32[]{:S(2)}) collective-permute-start(bf16[2,3,24,512]{3,2,1,0:T(8,128)(2,1)S(1)} %get-tuple-element.188), channel_id=1, source_target_pairs={{0,272},{1,273},{2,274},{3,275},{4,276},{5,277},{6,278},{7,279},{8... | collective-permute-start | bytes 442376 | tf_op jit(solution)/shard_map/hand_over/ppermute | solution.py:440
  120.3 7.2 %collective-permute-start.10 = (bf16[2,3,24,512]{3,2,1,0:T(8,128)(2,1)S(1)}, bf16[2,3,24,512]{3,2,1,0:T(8,128)(2,1)S(1)}, u32[]{:S(2)}, u32[]{:S(2)}) collective-permute-start(bf16[2,3,24,512]{3,2,1,0:T(8,128)(2,1)S(1)} %get-tuple-element.189), channel_id=1, source_target_pairs={{0,256},{1,257},{2,258},{3,259},{4,260},{5,261},{6,262},{7,263},{8... | collective-permute-start | bytes 442376 | tf_op jit(solution)/shard_map/hand_over/ppermute | solution.py:440
  128.3 11.0 %all-to-all-start.3 = ((bf16[16,48,128]{2,1,0:T(8,128)(2,1)}), bf16[16,48,128]{2,1,0:T(8,128)(2,1)S(1)}, u32[]{:S(2)}, u32[]{:S(2)}) async-start(bf16[16,48,128]{2,1,0:T(8,128)(2,1)} %broadcast_in_dim.26), calls=%async_computation.3 | async-start | bytes 393216 | tf_op jit(solution)/shard_map/adapter_gather/all_to_all | solution.py:527

commit v5 on v4

--- a/solution.py
+++ b/solution.py
@@ -513,21 +513,20 @@
 
     with jax.named_scope("adapter_sum_lon"):
         grads = lax.all_to_all(grads.reshape(16, 48, 128), "lon", 0, 0)
-    with jax.named_scope("hand_over"):
+    with jax.named_scope("shift_back"):
         strip = shift(strip, 0, 1)
         strip = jnp.pad(strip, ((0, 0), (0, 0), (0, 12), (0, 0)))
         column = lax.broadcasted_iota(jnp.int32, (1, 1, 24, 1), 2)
         main = jnp.where(column < jnp.where(segment == 0, 6, 12), strip, main)
-        grads, main = lax.optimization_barrier((grads, main))
-        own, below = hand(main[:, :3], 0, 0), hand(main[:, 3:], 1, 0)
+        below = shift(main[:, 3:], 1, 0)
     with jax.named_scope("adapter_sum_lat"):
         grads = lax.all_to_all(summed(grads), "lat", 0, 0)
-        grads, own, below = lax.optimization_barrier((grads, own, below))
+        grads, below = lax.optimization_barrier((grads, below))
     with jax.named_scope("adapter_gather"):
         grads = lax.all_to_all(summed(grads), "lon", 0, 0)
         adapter_sum = grads.astype(F32).reshape(1, 98304)
-    with jax.named_scope("assemble"):
-        gradient = jnp.concatenate([below, own], 1)
+    with jax.named_scope("hand_over"):
+        gradient = hand(jnp.concatenate([below, main[:, :3]], 1), 0, 0)
     return gradient[None], adapter_sum
 
 

time: 142 us -> 141 us (level)
  the two profiles are of different devices: /device:TPU:1 before, /device:TPU:2 now
where the time goes in v5:
time: 141 us; the launch traced here: 140 us
  starting transfers between devices  78.4 us (56%)
  waiting for transfers between devices  32.8 us (23%)
  Pallas kernels  21.4 us (15%)
  local copies, waits for them, and re-layouts  4.25 us (3%)
  other arithmetic  2.03 us (1%)
    ppermute x7, starting transfers between devices, neighbour_send(): return lax.ppermute(value, BOTH, route)  21 us
    all_to_all x1, starting transfers between devices, shards(): piece = lax.all_to_all(own_w, BOTH, 0, 0, axis_index_groups=class_groups())  18.9 us
    ppermute x4, starting transfers between devices, shift(): return lax.ppermute(value, BOTH, route)  17.7 us
    pallas_call x1, Pallas kernels, run_block(): pl.pallas_call(functools.partial(block_kernel, deep), out_shape=tuple((ja...  10.3 us
    ppermute x4, waiting for transfers between devices, shift(): return lax.ppermute(value, BOTH, route)  9.59 us
    all_to_all x1, starting transfers between devices, shards(): grads = lax.all_to_all(summed(grads), 'lat', 0, 0)  6.86 us
    all_to_all x1, starting transfers between devices, shards(): grads = lax.all_to_all(grads.reshape(16, 48, 128), 'lon', 0, 0)  6.84 us
    pallas_call x1, Pallas kernels, shards(): pl.pallas_call(bias_kernel, out_shape=(jax.ShapeDtypeStruct((HEADS // 2,...  6.53 us
  transfers between devices with their start and end apart: 16, of which 10 were waited for; matrix products, arithmetic and copies ran while one was open for 2% of the time, Pallas kernels for 7%

profile of v5, /device:TPU:2, one launch (start us, length us, event | category | flops | bytes accessed | tf_op | source)
XLA Modules:
  0.0 139.8 jit_solution(11840246379043095317)
XLA Ops:
  0.7 0.1 pad_add_fusion.1.place_ref
  0.8 1.8 %pack_weights.1 = bf16[32,64,128]{2,1,0:T(8,128)(2,1)} custom-call(s32[3]{0:T(128)S(1)} %pad_add_fusion.1.place_ref, bf16[32,96]{1,0:T(8,128)(2,1)} %qs_ref.1, bf16[32,32]{1,0:T(8,128)(2,1)} %ps_ref.1, bf16[64,96]{1,0:T(8,128)(2,1)} %qd_ref.1, bf16[32,64]{1,0:T(8,128)(2,1)} %pd_ref.1), custom_call_target="tpu_custom_call" | custom-call | tf_op jit(solution)/shard_map/pack/pack_weights/pallas_call | solution.py:463
  2.6 18.9 %all-to-all-start = ((bf16[32,64,128]{2,1,0:T(8,128)(2,1)}), bf16[32,64,128]{2,1,0:T(8,128)(2,1)S(1)}, u32[]{:S(2)}, u32[]{:S(2)}) async-start(bf16[32,64,128]{2,1,0:T(8,128)(2,1)} %pack_weights.1), calls=%async_computation | async-start | bytes 1048576 | tf_op jit(solution)/shard_map/weights_class/all_to_all | solution.py:471
  21.5 0.0 copy-start.3
  21.5 0.7 pad_maximum_fusion.1
  22.3 4.0 %collective-permute-start.7 = (bf16[2,2,3,24,512]{4,3,2,1,0:T(8,128)(2,1)}, bf16[2,2,3,24,512]{4,3,2,1,0:T(8,128)(2,1)S(1)}, u32[]{:S(2)}, u32[]{:S(2)}) collective-permute-start(bf16[2,2,3,24,512]{4,3,2,1,0:T(8,128)(2,1)} %pad_maximum_fusion.1), channel_id=1, source_target_pairs={{0,240},{1,241},{2,242},{3,243},{4,244},{5,245},{6,246},{7,247},{8... | collective-permute-start | bytes 884744 | tf_op jit(solution)/shard_map/halos/ppermute | solution.py:448
  26.3 0.0 copy-start.4
  26.3 0.1 copy.13
  26.4 0.6 copy-done.4
  27.0 0.0 copy-done.5
  27.0 0.1 pad_add_fusion
  27.1 0.7 pad.12.index_ref
  27.8 0.6 pad.13.table_ref
  28.4 6.5 %bias_table.1 = (f32[4,144,384]{2,1,0:T(8,128)S(1)}, f32[144,384]{1,0:T(8,128)}) custom-call(s32[3]{0:T(128)S(1)} %pad_add_fusion.1.place_ref, s32[96]{0:T(128)} %pole_ref.1, s32[144,384]{1,0:T(8,128)} %pad.12.index_ref, f32[8,768]{1,0:T(8,128)} %pad.13.table_ref), custom_call_target="tpu_custom_call" | custom-call | tf_op jit(solution)/shard_map/bias/bias_table/pallas_call | solution.py:476
  35.0 6.2 %all-to-all-done = bf16[32,64,128]{2,1,0:T(8,128)(2,1)S(1)} async-done(((bf16[32,64,128]{2,1,0:T(8,128)(2,1)}), bf16[32,64,128]{2,1,0:T(8,128)(2,1)S(1)}, u32[]{:S(2)}, u32[]{:S(2)}) %all-to-all-start) | async-done | bytes 524320 | tf_op jit(solution)/shard_map/weights_class/all_to_all | solution.py:471
  41.1 2.2 %collective-permute-start.6 = (bf16[32,64,128]{2,1,0:T(8,128)(2,1)S(1)}, bf16[32,64,128]{2,1,0:T(8,128)(2,1)S(1)}, u32[]{:S(2)}, u32[]{:S(2)}) collective-permute-start(bf16[32,64,128]{2,1,0:T(8,128)(2,1)S(1)} %all-to-all-done), channel_id=1, source_target_pairs={{0,32},{1,33},{2,34},{3,35},{4,36},{5,37},{6,38},{7,39},{8,40},{9,... | collective-permute-start | bytes 1572872 | tf_op jit(solution)/shard_map/weights_neighbours/ppermute | solution.py:41
  43.3 1.9 %collective-permute-start.5 = (bf16[32,64,128]{2,1,0:T(8,128)(2,1)S(1)}, bf16[32,64,128]{2,1,0:T(8,128)(2,1)S(1)}, u32[]{:S(2)}, u32[]{:S(2)}) collective-permute-start(bf16[32,64,128]{2,1,0:T(8,128)(2,1)S(1)} %all-to-all-done), channel_id=1, source_target_pairs={{0,8},{1,9},{2,10},{3,11},{4,12},{5,13},{6,14},{7,15},{8,16},{9,17... | collective-permute-start | bytes 1572872 | tf_op jit(solution)/shard_map/weights_neighbours/ppermute | solution.py:41
  45.3 0.1 pad_maximum_fusion
  45.4 6.4 %collective-permute-start.8 = (bf16[2,2,6,12,512]{4,3,2,1,0:T(8,128)(2,1)S(1)}, bf16[2,2,6,12,512]{4,3,2,1,0:T(8,128)(2,1)S(1)}, u32[]{:S(2)}, u32[]{:S(2)}) collective-permute-start(bf16[2,2,6,12,512]{4,3,2,1,0:T(8,128)(2,1)S(1)} %pad_maximum_fusion), channel_id=1, source_target_pairs={{0,15},{1,0},{2,1},{3,2},{4,3},{5,4},{6,5},{7,6},{8,7},{9,8},{10,9... | collective-permute-start | bytes 884744 | tf_op jit(solution)/shard_map/halos/ppermute | solution.py:448
  51.8 1.9 %collective-permute-start.4 = (bf16[32,64,128]{2,1,0:T(8,128)(2,1)S(1)}, bf16[32,64,128]{2,1,0:T(8,128)(2,1)}, u32[]{:S(2)}, u32[]{:S(2)}) collective-permute-start(bf16[32,64,128]{2,1,0:T(8,128)(2,1)S(1)} %all-to-all-done), channel_id=1, source_target_pairs={{0,1},{1,2},{2,3},{3,4},{4,5},{5,6},{6,7},{7,0},{8,9},{9,10},{10,1... | collective-permute-start | bytes 1572872 | tf_op jit(solution)/shard_map/weights_neighbours/ppermute | solution.py:41
  53.8 2.3 %collective-permute-start.3 = (bf16[32,64,128]{2,1,0:T(8,128)(2,1)S(1)}, bf16[32,64,128]{2,1,0:T(8,128)(2,1)}, u32[]{:S(2)}, u32[]{:S(2)}) collective-permute-start(bf16[32,64,128]{2,1,0:T(8,128)(2,1)S(1)} %all-to-all-done), channel_id=1, source_target_pairs={{0,33},{1,34},{2,35},{3,36},{4,37},{5,38},{6,39},{7,32},{8,41},{9,... | collective-permute-start | bytes 1572872 | tf_op jit(solution)/shard_map/weights_neighbours/ppermute | solution.py:41
  56.1 1.0 collective-permute-done.8
  57.1 5.2 %collective-permute-start.2 = (bf16[32,64,128]{2,1,0:T(8,128)(2,1)S(1)}, bf16[32,64,128]{2,1,0:T(8,128)(2,1)}, u32[]{:S(2)}, u32[]{:S(2)}) collective-permute-start(bf16[32,64,128]{2,1,0:T(8,128)(2,1)S(1)} %all-to-all-done), channel_id=1, source_target_pairs={{0,7},{1,0},{2,1},{3,2},{4,3},{5,4},{6,5},{7,6},{8,15},{9,8},{10,9... | collective-permute-start | bytes 1572872 | tf_op jit(solution)/shard_map/weights_neighbours/ppermute | solution.py:41
  62.3 3.8 %collective-permute-start.1 = (bf16[32,64,128]{2,1,0:T(8,128)(2,1)S(1)}, bf16[32,64,128]{2,1,0:T(8,128)(2,1)}, u32[]{:S(2)}, u32[]{:S(2)}) collective-permute-start(bf16[32,64,128]{2,1,0:T(8,128)(2,1)S(1)} %all-to-all-done), channel_id=1, source_target_pairs={{0,24},{1,25},{2,26},{3,27},{4,28},{5,29},{6,30},{7,31},{8,0},{9,1... | collective-permute-start | bytes 1572872 | tf_op jit(solution)/shard_map/weights_neighbours/ppermute | solution.py:41
  66.1 3.7 %collective-permute-start = (bf16[32,64,128]{2,1,0:T(8,128)(2,1)S(1)}, bf16[32,64,128]{2,1,0:T(8,128)(2,1)}, u32[]{:S(2)}, u32[]{:S(2)}) collective-permute-start(bf16[32,64,128]{2,1,0:T(8,128)(2,1)S(1)} %all-to-all-done), channel_id=1, source_target_pairs={{0,224},{1,225},{2,226},{3,227},{4,228},{5,229},{6,230},{7,231},{8... | collective-permute-start | bytes 1572872 | tf_op jit(solution)/shard_map/weights_neighbours/ppermute | solution.py:41
  69.8 2.7 %conditional.2 = ((bf16[288,512]{1,0:T(8,128)(2,1)}, bf16[288,512]{1,0:T(8,128)(2,1)}, f32[288,128]{1,0:T(8,128)S(1)}, bf16[288,32]{1,0:T(8,128)(2,1)}, bf16[288...) conditional(s32[]{:T(128)} %convert_element_type.6, ...), branch_computations={%region_0.1_spmd, %region_1.2_spmd} | conditional | bytes 8 | solution.py:492
  69.9 2.7 %shallow_prep.1 = (bf16[288,512]{1,0:T(8,128)(2,1)}, bf16[288,512]{1,0:T(8,128)(2,1)}, f32[288,128]{1,0:T(8,128)S(1)}, bf16[288,32]{1,0:T(8,128)(2,1)}, bf16[288...) custom-call(bf16[2,6,24,512]{3,2,1,0:T(8,128)(2,1)S(1)} %get-tuple-element.101.x, ...), custom_call_target="tpu_custom_call" | custom-call | tf_op jit(solution)/shard_map/prep/cond/branch_1_fun/shallow_prep/pallas_call | solution.py:385
  72.5 2.9 %collective-permute-done.4 = bf16[32,64,128]{2,1,0:T(8,128)(2,1)} collective-permute-done((bf16[32,64,128]{2,1,0:T(8,128)(2,1)S(1)}, bf16[32,64,128]{2,1,0:T(8,128)(2,1)}, u32[]{:S(2)}, u32[]{:S(2)}) %collective-permute-start.4) | collective-permute-done | bytes 524320 | tf_op jit(solution)/shard_map/weights_neighbours/ppermute | solution.py:41
  75.4 2.9 %collective-permute-done = bf16[32,64,128]{2,1,0:T(8,128)(2,1)} collective-permute-done((bf16[32,64,128]{2,1,0:T(8,128)(2,1)S(1)}, bf16[32,64,128]{2,1,0:T(8,128)(2,1)}, u32[]{:S(2)}, u32[]{:S(2)}) %collective-permute-start) | collective-permute-done | bytes 524320 | tf_op jit(solution)/shard_map/weights_neighbours/ppermute | solution.py:41
  78.4 10.3 %conditional.3 = ((bf16[2,6,24,512]{3,2,1,0:T(8,128)(2,1)S(1)}, bf16[2,6,12,512]{3,2,1,0:T(8,128)(2,1)S(1)}, bf16[768,128]{1,0:T(8,128)(2,1)})) conditional(s32[]{:T(128)} %convert_element_type.6, (s32[3]{0:T(128)S(1)}, bf16[32,64,128]{2,1,0:T(8,128)(2,1)S(1)}, bf16[32,64,128]{2,1,0:T(8,128)(2,1)}, bf16[32,64,128]{2,1,0:T(8,128)(2,1)}, ...), branch_computations={%region_2.3_spmd, %region_3.4_spmd} | conditional | bytes 8 | solution.py:507
  78.4 10.3 %shallow_block.1 = (bf16[2,6,24,512]{3,2,1,0:T(8,128)(2,1)S(1)}, bf16[2,6,12,512]{3,2,1,0:T(8,128)(2,1)S(1)}, bf16[768,128]{1,0:T(8,128)(2,1)}) custom-call(s32[3]{0:T(128)S(1)} %get-tuple-element.125.place_ref, bf16[32,64,128]{2,1,0:T(8,128)(2,1)S(1)} %get-tuple-element.126.p0, bf16[32,64,128]{2,1,0:T(8,128)(2,1)} %get-tuple-element.127.p1, ...), custom_call_target="tpu_custom_call" | custom-call | tf_op jit(solution)/shard_map/cond/branch_1_fun/shallow_block/pallas_call | solution.py:409
  88.7 1.9 %collective-permute-start.9 = (bf16[2,6,12,512]{3,2,1,0:T(8,128)(2,1)S(1)}, bf16[2,6,12,512]{3,2,1,0:T(8,128)(2,1)S(1)}, u32[]{:S(2)}, u32[]{:S(2)}) collective-permute-start(bf16[2,6,12,512]{3,2,1,0:T(8,128)(2,1)S(1)} %get-tuple-element.178), channel_id=1, source_target_pairs={{0,1},{1,2},{2,3},{3,4},{4,5},{5,6},{6,7},{7,8},{8,9},{9,10},{10,1... | collective-permute-start | bytes 442376 | tf_op jit(solution)/shard_map/shift_back/ppermute | solution.py:448
  90.6 6.8 %all-to-all-start.1 = ((bf16[16,48,128]{2,1,0:T(8,128)(2,1)}), bf16[16,48,128]{2,1,0:T(8,128)(2,1)S(1)}, u32[]{:S(2)}, u32[]{:S(2)}) async-start(bf16[16,48,128]{2,1,0:T(8,128)(2,1)} %bitcast.12), calls=%async_computation.1 | async-start | bytes 393216 | tf_op jit(solution)/shard_map/adapter_sum_lon/all_to_all | solution.py:515
  97.5 2.9 %collective-permute-done.9 = bf16[2,6,12,512]{3,2,1,0:T(8,128)(2,1)S(1)} collective-permute-done((bf16[2,6,12,512]{3,2,1,0:T(8,128)(2,1)S(1)}, bf16[2,6,12,512]{3,2,1,0:T(8,128)(2,1)S(1)}, u32[]{:S(2)}, u32[]{:S(2)}) %collective-permute-start.9) | collective-permute-done | bytes 147488 | tf_op jit(solution)/shard_map/shift_back/ppermute | solution.py:448
  100.3 0.2 pad_select_fusion
  100.5 4.7 %all-to-all-done.1 = bf16[16,48,128]{2,1,0:T(8,128)(2,1)S(1)} async-done(((bf16[16,48,128]{2,1,0:T(8,128)(2,1)}), bf16[16,48,128]{2,1,0:T(8,128)(2,1)S(1)}, u32[]{:S(2)}, u32[]{:S(2)}) %all-to-all-start.1) | async-done | bytes 196640 | tf_op jit(solution)/shard_map/adapter_sum_lon/all_to_all | solution.py:515
  105.3 0.7 broadcast_in_dim.14
  106.0 6.9 %all-to-all-start.2 = ((bf16[16,48,128]{2,1,0:T(8,128)(2,1)}), bf16[16,48,128]{2,1,0:T(8,128)(2,1)S(1)}, u32[]{:S(2)}, u32[]{:S(2)}) async-start(bf16[16,48,128]{2,1,0:T(8,128)(2,1)} %broadcast_in_dim.14), calls=%async_computation.2 | async-start | bytes 393216 | tf_op jit(solution)/shard_map/adapter_sum_lat/all_to_all | solution.py:523
  112.9 5.3 %collective-permute-start.10 = (bf16[2,3,24,512]{3,2,1,0:T(8,128)(2,1)S(1)}, bf16[2,3,24,512]{3,2,1,0:T(8,128)(2,1)S(1)}, u32[]{:S(2)}, u32[]{:S(2)}) collective-permute-start(bf16[2,3,24,512]{3,2,1,0:T(8,128)(2,1)S(1)} %get-tuple-element.182), channel_id=1, source_target_pairs={{0,16},{1,17},{2,18},{3,19},{4,20},{5,21},{6,22},{7,23},{8,24},{9,... | collective-permute-start | bytes 442376 | tf_op jit(solution)/shard_map/shift_back/ppermute | solution.py:448
  118.2 5.7 %collective-permute-done.10 = bf16[2,3,24,512]{3,2,1,0:T(8,128)(2,1)S(1)} collective-permute-done((bf16[2,3,24,512]{3,2,1,0:T(8,128)(2,1)S(1)}, bf16[2,3,24,512]{3,2,1,0:T(8,128)(2,1)S(1)}, u32[]{:S(2)}, u32[]{:S(2)}) %collective-permute-start.10) | collective-permute-done | bytes 147488 | tf_op jit(solution)/shard_map/shift_back/ppermute | solution.py:448
  123.9 0.6 all-to-all-done.2
  124.6 0.7 broadcast_in_dim.26
  125.3 5.2 %all-to-all-start.3 = ((bf16[16,48,128]{2,1,0:T(8,128)(2,1)}), bf16[16,48,128]{2,1,0:T(8,128)(2,1)S(1)}, u32[]{:S(2)}, u32[]{:S(2)}) async-start(bf16[16,48,128]{2,1,0:T(8,128)(2,1)} %broadcast_in_dim.26), calls=%async_computation.3 | async-start | bytes 393216 | tf_op jit(solution)/shard_map/adapter_gather/all_to_all | solution.py:526
  130.6 1.9 %collective-permute-start.11 = (bf16[2,6,24,512]{3,2,1,0:T(8,128)(2,1)S(1)}, bf16[2,6,24,512]{3,2,1,0:T(8,128)(2,1)S(1)}, u32[]{:S(2)}, u32[]{:S(2)}) collective-permute-start(bf16[2,6,24,512]{3,2,1,0:T(8,128)(2,1)S(1)} %pad_maximum_fusion.2), channel_id=1, source_target_pairs={{0,256},{1,257},{2,258},{3,259},{4,260},{5,261},{6,262},{7,263},{8... | collective-permute-start | bytes 884744 | tf_op jit(solution)/shard_map/hand_over/ppermute | solution.py:440
  132.5 1.5 %collective-permute-done.11 = bf16[2,6,24,512]{3,2,1,0:T(8,128)(2,1)S(1)} collective-permute-done((bf16[2,6,24,512]{3,2,1,0:T(8,128)(2,1)S(1)}, bf16[2,6,24,512]{3,2,1,0:T(8,128)(2,1)S(1)}, u32[]{:S(2)}, u32[]{:S(2)}) %collective-permute-start.11) | collective-permute-done | bytes 294944 | tf_op jit(solution)/shard_map/hand_over/ppermute | solution.py:440
  134.1 4.3 %all-to-all-done.3 = bf16[16,48,128]{2,1,0:T(8,128)(2,1)S(1)} async-done(((bf16[16,48,128]{2,1,0:T(8,128)(2,1)}), bf16[16,48,128]{2,1,0:T(8,128)(2,1)S(1)}, u32[]{:S(2)}, u32[]{:S(2)}) %all-to-all-start.3) | async-done | bytes 196640 | tf_op jit(solution)/shard_map/adapter_gather/all_to_all | solution.py:526
  138.3 0.8 reshape.27
  139.1 0.7 copy.37
  (23 shorter events, 0.2 us)
Async XLA Ops:
  2.6 18.9 %copy-start = (bf16[1,2,6,24,512]{4,3,2,1,0:T(8,128)(2,1)S(1)}, bf16[1,2,6,24,512]{4,3,2,1,0:T(8,128)(2,1)}, u32[]{:S(2)}) copy-start(bf16[1,2,6,24,512]{4,3,2,1,0:T(8,128)(2,1)} %param.15) | copy-start | bytes 884740
  2.6 18.9 %copy-start.1 = (bf16[1,2,6,24,512]{4,3,2,1,0:T(8,128)(2,1)S(1)}, bf16[1,2,6,24,512]{4,3,2,1,0:T(8,128)(2,1)}, u32[]{:S(2)}) copy-start(bf16[1,2,6,24,512]{4,3,2,1,0:T(8,128)(2,1)} %param.16) | copy-start | bytes 884740
  2.6 38.5 %all-to-all-start = ((bf16[32,64,128]{2,1,0:T(8,128)(2,1)}), bf16[32,64,128]{2,1,0:T(8,128)(2,1)S(1)}, u32[]{:S(2)}, u32[]{:S(2)}) async-start(bf16[32,64,128]{2,1,0:T(8,128)(2,1)} %pack_weights.1), calls=%async_computation | async-start | bytes 1048576 | tf_op jit(solution)/shard_map/weights_class/all_to_all | solution.py:471
  21.5 4.7 %copy-start.3 = (s32[144,144]{1,0:T(8,128)S(1)}, s32[144,144]{1,0:T(8,128)}, u32[]{:S(2)}) copy-start(s32[144,144]{1,0:T(8,128)} %param.18) | copy-start | bytes 248836
  22.3 23.0 %collective-permute-start.7 = (bf16[2,2,3,24,512]{4,3,2,1,0:T(8,128)(2,1)}, bf16[2,2,3,24,512]{4,3,2,1,0:T(8,128)(2,1)S(1)}, u32[]{:S(2)}, u32[]{:S(2)}) collective-permute-start(bf16[2,2,3,24,512]{4,3,2,1,0:T(8,128)(2,1)} %pad_maximum_fusion.1), channel_id=1, source_target_pairs={{0,240},{1,241},{2,242},{3,243},{4,244},{5,245},{6,246},{7,247},{8... | collective-permute-start | bytes 884744 | tf_op jit(solution)/shard_map/halos/ppermute | solution.py:448
  26.3 0.7 copy-start.4
  26.3 0.7 copy-start.5
  41.1 21.2 %collective-permute-start.6 = (bf16[32,64,128]{2,1,0:T(8,128)(2,1)S(1)}, bf16[32,64,128]{2,1,0:T(8,128)(2,1)S(1)}, u32[]{:S(2)}, u32[]{:S(2)}) collective-permute-start(bf16[32,64,128]{2,1,0:T(8,128)(2,1)S(1)} %all-to-all-done), channel_id=1, source_target_pairs={{0,32},{1,33},{2,34},{3,35},{4,36},{5,37},{6,38},{7,39},{8,40},{9,... | collective-permute-start | bytes 1572872 | tf_op jit(solution)/shard_map/weights_neighbours/ppermute | solution.py:41
  43.3 22.8 %collective-permute-start.5 = (bf16[32,64,128]{2,1,0:T(8,128)(2,1)S(1)}, bf16[32,64,128]{2,1,0:T(8,128)(2,1)S(1)}, u32[]{:S(2)}, u32[]{:S(2)}) collective-permute-start(bf16[32,64,128]{2,1,0:T(8,128)(2,1)S(1)} %all-to-all-done), channel_id=1, source_target_pairs={{0,8},{1,9},{2,10},{3,11},{4,12},{5,13},{6,14},{7,15},{8,16},{9,17... | collective-permute-start | bytes 1572872 | tf_op jit(solution)/shard_map/weights_neighbours/ppermute | solution.py:41
  45.4 11.7 %collective-permute-start.8 = (bf16[2,2,6,12,512]{4,3,2,1,0:T(8,128)(2,1)S(1)}, bf16[2,2,6,12,512]{4,3,2,1,0:T(8,128)(2,1)S(1)}, u32[]{:S(2)}, u32[]{:S(2)}) collective-permute-start(bf16[2,2,6,12,512]{4,3,2,1,0:T(8,128)(2,1)S(1)} %pad_maximum_fusion), channel_id=1, source_target_pairs={{0,15},{1,0},{2,1},{3,2},{4,3},{5,4},{6,5},{7,6},{8,7},{9,8},{10,9... | collective-permute-start | bytes 884744 | tf_op jit(solution)/shard_map/halos/ppermute | solution.py:448
  51.8 23.6 %collective-permute-start.4 = (bf16[32,64,128]{2,1,0:T(8,128)(2,1)S(1)}, bf16[32,64,128]{2,1,0:T(8,128)(2,1)}, u32[]{:S(2)}, u32[]{:S(2)}) collective-permute-start(bf16[32,64,128]{2,1,0:T(8,128)(2,1)S(1)} %all-to-all-done), channel_id=1, source_target_pairs={{0,1},{1,2},{2,3},{3,4},{4,5},{5,6},{6,7},{7,0},{8,9},{9,10},{10,1... | collective-permute-start | bytes 1572872 | tf_op jit(solution)/shard_map/weights_neighbours/ppermute | solution.py:41
  53.8 21.7 %collective-permute-start.3 = (bf16[32,64,128]{2,1,0:T(8,128)(2,1)S(1)}, bf16[32,64,128]{2,1,0:T(8,128)(2,1)}, u32[]{:S(2)}, u32[]{:S(2)}) collective-permute-start(bf16[32,64,128]{2,1,0:T(8,128)(2,1)S(1)} %all-to-all-done), channel_id=1, source_target_pairs={{0,33},{1,34},{2,35},{3,36},{4,37},{5,38},{6,39},{7,32},{8,41},{9,... | collective-permute-start | bytes 1572872 | tf_op jit(solution)/shard_map/weights_neighbours/ppermute | solution.py:41
  57.1 9.0 %copy-start.2 = (bf16[2,2,6,12,512]{4,3,2,1,0:T(8,128)(2,1)}, bf16[2,2,6,12,512]{4,3,2,1,0:T(8,128)(2,1)S(1)}, u32[]{:S(2)}) copy-start(bf16[2,2,6,12,512]{4,3,2,1,0:T(8,128)(2,1)S(1)} %collective-permute-done.8) | copy-start | bytes 884740
  57.1 18.3 %collective-permute-start.2 = (bf16[32,64,128]{2,1,0:T(8,128)(2,1)S(1)}, bf16[32,64,128]{2,1,0:T(8,128)(2,1)}, u32[]{:S(2)}, u32[]{:S(2)}) collective-permute-start(bf16[32,64,128]{2,1,0:T(8,128)(2,1)S(1)} %all-to-all-done), channel_id=1, source_target_pairs={{0,7},{1,0},{2,1},{3,2},{4,3},{5,4},{6,5},{7,6},{8,15},{9,8},{10,9... | collective-permute-start | bytes 1572872 | tf_op jit(solution)/shard_map/weights_neighbours/ppermute | solution.py:41
  62.3 13.1 %collective-permute-start.1 = (bf16[32,64,128]{2,1,0:T(8,128)(2,1)S(1)}, bf16[32,64,128]{2,1,0:T(8,128)(2,1)}, u32[]{:S(2)}, u32[]{:S(2)}) collective-permute-start(bf16[32,64,128]{2,1,0:T(8,128)(2,1)S(1)} %all-to-all-done), channel_id=1, source_target_pairs={{0,24},{1,25},{2,26},{3,27},{4,28},{5,29},{6,30},{7,31},{8,0},{9,1... | collective-permute-start | bytes 1572872 | tf_op jit(solution)/shard_map/weights_neighbours/ppermute | solution.py:41
  66.1 12.2 %collective-permute-start = (bf16[32,64,128]{2,1,0:T(8,128)(2,1)S(1)}, bf16[32,64,128]{2,1,0:T(8,128)(2,1)}, u32[]{:S(2)}, u32[]{:S(2)}) collective-permute-start(bf16[32,64,128]{2,1,0:T(8,128)(2,1)S(1)} %all-to-all-done), channel_id=1, source_target_pairs={{0,224},{1,225},{2,226},{3,227},{4,228},{5,229},{6,230},{7,231},{8... | collective-permute-start | bytes 1572872 | tf_op jit(solution)/shard_map/weights_neighbours/ppermute | solution.py:41
  88.7 11.6 %collective-permute-start.9 = (bf16[2,6,12,512]{3,2,1,0:T(8,128)(2,1)S(1)}, bf16[2,6,12,512]{3,2,1,0:T(8,128)(2,1)S(1)}, u32[]{:S(2)}, u32[]{:S(2)}) collective-permute-start(bf16[2,6,12,512]{3,2,1,0:T(8,128)(2,1)S(1)} %get-tuple-element.178), channel_id=1, source_target_pairs={{0,1},{1,2},{2,3},{3,4},{4,5},{5,6},{6,7},{7,8},{8,9},{9,10},{10,1... | collective-permute-start | bytes 442376 | tf_op jit(solution)/shard_map/shift_back/ppermute | solution.py:448
  90.6 14.6 %all-to-all-start.1 = ((bf16[16,48,128]{2,1,0:T(8,128)(2,1)}), bf16[16,48,128]{2,1,0:T(8,128)(2,1)S(1)}, u32[]{:S(2)}, u32[]{:S(2)}) async-start(bf16[16,48,128]{2,1,0:T(8,128)(2,1)} %bitcast.12), calls=%async_computation.1 | async-start | bytes 393216 | tf_op jit(solution)/shard_map/adapter_sum_lon/all_to_all | solution.py:515
  106.0 18.6 %all-to-all-start.2 = ((bf16[16,48,128]{2,1,0:T(8,128)(2,1)}), bf16[16,48,128]{2,1,0:T(8,128)(2,1)S(1)}, u32[]{:S(2)}, u32[]{:S(2)}) async-start(bf16[16,48,128]{2,1,0:T(8,128)(2,1)} %broadcast_in_dim.14), calls=%async_computation.2 | async-start | bytes 393216 | tf_op jit(solution)/shard_map/adapter_sum_lat/all_to_all | solution.py:523
  112.9 11.1 %collective-permute-start.10 = (bf16[2,3,24,512]{3,2,1,0:T(8,128)(2,1)S(1)}, bf16[2,3,24,512]{3,2,1,0:T(8,128)(2,1)S(1)}, u32[]{:S(2)}, u32[]{:S(2)}) collective-permute-start(bf16[2,3,24,512]{3,2,1,0:T(8,128)(2,1)S(1)} %get-tuple-element.182), channel_id=1, source_target_pairs={{0,16},{1,17},{2,18},{3,19},{4,20},{5,21},{6,22},{7,23},{8,24},{9,... | collective-permute-start | bytes 442376 | tf_op jit(solution)/shard_map/shift_back/ppermute | solution.py:448
  125.3 13.0 %all-to-all-start.3 = ((bf16[16,48,128]{2,1,0:T(8,128)(2,1)}), bf16[16,48,128]{2,1,0:T(8,128)(2,1)S(1)}, u32[]{:S(2)}, u32[]{:S(2)}) async-start(bf16[16,48,128]{2,1,0:T(8,128)(2,1)} %broadcast_in_dim.26), calls=%async_computation.3 | async-start | bytes 393216 | tf_op jit(solution)/shard_map/adapter_gather/all_to_all | solution.py:526
  130.6 3.5 %collective-permute-start.11 = (bf16[2,6,24,512]{3,2,1,0:T(8,128)(2,1)S(1)}, bf16[2,6,24,512]{3,2,1,0:T(8,128)(2,1)S(1)}, u32[]{:S(2)}, u32[]{:S(2)}) collective-permute-start(bf16[2,6,24,512]{3,2,1,0:T(8,128)(2,1)S(1)} %pad_maximum_fusion.2), channel_id=1, source_target_pairs={{0,256},{1,257},{2,258},{3,259},{4,260},{5,261},{6,262},{7,263},{8... | collective-permute-start | bytes 884744 | tf_op jit(solution)/shard_map/hand_over/ppermute | solution.py:440

commit v6 on v5

--- a/solution.py
+++ b/solution.py
@@ -521,7 +521,6 @@
         below = shift(main[:, 3:], 1, 0)
     with jax.named_scope("adapter_sum_lat"):
         grads = lax.all_to_all(summed(grads), "lat", 0, 0)
-        grads, below = lax.optimization_barrier((grads, below))
     with jax.named_scope("adapter_gather"):
         grads = lax.all_to_all(summed(grads), "lon", 0, 0)
         adapter_sum = grads.astype(F32).reshape(1, 98304)

time: 141 us -> 141 us (level)
    ppermute x4, waiting for transfers between devices: 9.59 us -> 3.87 us  [shift(): return lax.ppermute(value, BOTH, route)]
    all_to_all x1, waiting for transfers between devices: 0.64 us -> 6.36 us  [shards(): grads = lax.all_to_all(summed(grads), 'lat', 0, 0)]
  transfers between devices with their start and end apart: 16 -> 16, of which waited for: 10 -> 9; matrix products, arithmetic and copies ran while one was open for 2% -> 2% of each run, Pallas kernels for 7% -> 7%
where the time goes in v6:
time: 141 us; the launch traced here: 140 us
  starting transfers between devices  78.4 us (56%)
  waiting for transfers between devices  32.8 us (23%)
  Pallas kernels  21.4 us (15%)
  local copies, waits for them, and re-layouts  4.25 us (3%)
  other arithmetic  2.03 us (1%)
    ppermute x7, starting transfers between devices, neighbour_send(): return lax.ppermute(value, BOTH, route)  21 us
    all_to_all x1, starting transfers between devices, shards(): piece = lax.all_to_all(own_w, BOTH, 0, 0, axis_index_groups=class_groups())  18.9 us
    ppermute x4, starting transfers between devices, shift(): return lax.ppermute(value, BOTH, route)  17.7 us
    pallas_call x1, Pallas kernels, run_block(): pl.pallas_call(functools.partial(block_kernel, deep), out_shape=tuple((ja...  10.3 us
    all_to_all x1, starting transfers between devices, shards(): grads = lax.all_to_all(summed(grads), 'lat', 0, 0)  6.86 us
    all_to_all x1, starting transfers between devices, shards(): grads = lax.all_to_all(grads.reshape(16, 48, 128), 'lon', 0, 0)  6.84 us
    pallas_call x1, Pallas kernels, shards(): pl.pallas_call(bias_kernel, out_shape=(jax.ShapeDtypeStruct((HEADS // 2,...  6.53 us
    all_to_all x1, waiting for transfers between devices, shards(): grads = lax.all_to_all(summed(grads), 'lat', 0, 0)  6.36 us
  transfers between devices with their start and end apart: 16, of which 9 were waited for; matrix products, arithmetic and copies ran while one was open for 2% of the time, Pallas kernels for 7%

profile of v6, /device:TPU:2, one launch (start us, length us, event | category | flops | bytes accessed | tf_op | source)
XLA Modules:
  0.0 139.8 jit_solution(16506843336281592420)
XLA Ops:
  0.7 0.1 pad_add_fusion.1.place_ref
  0.8 1.8 %pack_weights.1 = bf16[32,64,128]{2,1,0:T(8,128)(2,1)} custom-call(s32[3]{0:T(128)S(1)} %pad_add_fusion.1.place_ref, bf16[32,96]{1,0:T(8,128)(2,1)} %qs_ref.1, bf16[32,32]{1,0:T(8,128)(2,1)} %ps_ref.1, bf16[64,96]{1,0:T(8,128)(2,1)} %qd_ref.1, bf16[32,64]{1,0:T(8,128)(2,1)} %pd_ref.1), custom_call_target="tpu_custom_call" | custom-call | tf_op jit(solution)/shard_map/pack/pack_weights/pallas_call | solution.py:463
  2.6 18.9 %all-to-all-start = ((bf16[32,64,128]{2,1,0:T(8,128)(2,1)}), bf16[32,64,128]{2,1,0:T(8,128)(2,1)S(1)}, u32[]{:S(2)}, u32[]{:S(2)}) async-start(bf16[32,64,128]{2,1,0:T(8,128)(2,1)} %pack_weights.1), calls=%async_computation | async-start | bytes 1048576 | tf_op jit(solution)/shard_map/weights_class/all_to_all | solution.py:471
  21.5 0.0 copy-start.3
  21.5 0.7 pad_maximum_fusion.1
  22.3 4.0 %collective-permute-start.7 = (bf16[2,2,3,24,512]{4,3,2,1,0:T(8,128)(2,1)}, bf16[2,2,3,24,512]{4,3,2,1,0:T(8,128)(2,1)S(1)}, u32[]{:S(2)}, u32[]{:S(2)}) collective-permute-start(bf16[2,2,3,24,512]{4,3,2,1,0:T(8,128)(2,1)} %pad_maximum_fusion.1), channel_id=1, source_target_pairs={{0,240},{1,241},{2,242},{3,243},{4,244},{5,245},{6,246},{7,247},{8... | collective-permute-start | bytes 884744 | tf_op jit(solution)/shard_map/halos/ppermute | solution.py:448
  26.3 0.0 copy-start.4
  26.3 0.0 copy-start.5
  26.3 0.1 copy.14
  26.4 0.6 copy-done.4
  27.0 0.0 copy-done.5
  27.0 0.1 pad_add_fusion
  27.1 0.7 pad.12.index_ref
  27.8 0.6 pad.13.table_ref
  28.4 6.5 %bias_table.1 = (f32[4,144,384]{2,1,0:T(8,128)S(1)}, f32[144,384]{1,0:T(8,128)}) custom-call(s32[3]{0:T(128)S(1)} %pad_add_fusion.1.place_ref, s32[96]{0:T(128)} %pole_ref.1, s32[144,384]{1,0:T(8,128)} %pad.12.index_ref, f32[8,768]{1,0:T(8,128)} %pad.13.table_ref), custom_call_target="tpu_custom_call" | custom-call | tf_op jit(solution)/shard_map/bias/bias_table/pallas_call | solution.py:476
  35.0 6.2 %all-to-all-done = bf16[32,64,128]{2,1,0:T(8,128)(2,1)S(1)} async-done(((bf16[32,64,128]{2,1,0:T(8,128)(2,1)}), bf16[32,64,128]{2,1,0:T(8,128)(2,1)S(1)}, u32[]{:S(2)}, u32[]{:S(2)}) %all-to-all-start) | async-done | bytes 524320 | tf_op jit(solution)/shard_map/weights_class/all_to_all | solution.py:471
  41.1 2.2 %collective-permute-start.6 = (bf16[32,64,128]{2,1,0:T(8,128)(2,1)S(1)}, bf16[32,64,128]{2,1,0:T(8,128)(2,1)S(1)}, u32[]{:S(2)}, u32[]{:S(2)}) collective-permute-start(bf16[32,64,128]{2,1,0:T(8,128)(2,1)S(1)} %all-to-all-done), channel_id=1, source_target_pairs={{0,32},{1,33},{2,34},{3,35},{4,36},{5,37},{6,38},{7,39},{8,40},{9,... | collective-permute-start | bytes 1572872 | tf_op jit(solution)/shard_map/weights_neighbours/ppermute | solution.py:41
  43.3 1.9 %collective-permute-start.5 = (bf16[32,64,128]{2,1,0:T(8,128)(2,1)S(1)}, bf16[32,64,128]{2,1,0:T(8,128)(2,1)S(1)}, u32[]{:S(2)}, u32[]{:S(2)}) collective-permute-start(bf16[32,64,128]{2,1,0:T(8,128)(2,1)S(1)} %all-to-all-done), channel_id=1, source_target_pairs={{0,8},{1,9},{2,10},{3,11},{4,12},{5,13},{6,14},{7,15},{8,16},{9,17... | collective-permute-start | bytes 1572872 | tf_op jit(solution)/shard_map/weights_neighbours/ppermute | solution.py:41
  45.3 0.1 pad_maximum_fusion
  45.4 6.4 %collective-permute-start.8 = (bf16[2,2,6,12,512]{4,3,2,1,0:T(8,128)(2,1)S(1)}, bf16[2,2,6,12,512]{4,3,2,1,0:T(8,128)(2,1)S(1)}, u32[]{:S(2)}, u32[]{:S(2)}) collective-permute-start(bf16[2,2,6,12,512]{4,3,2,1,0:T(8,128)(2,1)S(1)} %pad_maximum_fusion), channel_id=1, source_target_pairs={{0,15},{1,0},{2,1},{3,2},{4,3},{5,4},{6,5},{7,6},{8,7},{9,8},{10,9... | collective-permute-start | bytes 884744 | tf_op jit(solution)/shard_map/halos/ppermute | solution.py:448
  51.8 1.9 %collective-permute-start.4 = (bf16[32,64,128]{2,1,0:T(8,128)(2,1)S(1)}, bf16[32,64,128]{2,1,0:T(8,128)(2,1)}, u32[]{:S(2)}, u32[]{:S(2)}) collective-permute-start(bf16[32,64,128]{2,1,0:T(8,128)(2,1)S(1)} %all-to-all-done), channel_id=1, source_target_pairs={{0,1},{1,2},{2,3},{3,4},{4,5},{5,6},{6,7},{7,0},{8,9},{9,10},{10,1... | collective-permute-start | bytes 1572872 | tf_op jit(solution)/shard_map/weights_neighbours/ppermute | solution.py:41
  53.8 2.3 %collective-permute-start.3 = (bf16[32,64,128]{2,1,0:T(8,128)(2,1)S(1)}, bf16[32,64,128]{2,1,0:T(8,128)(2,1)}, u32[]{:S(2)}, u32[]{:S(2)}) collective-permute-start(bf16[32,64,128]{2,1,0:T(8,128)(2,1)S(1)} %all-to-all-done), channel_id=1, source_target_pairs={{0,33},{1,34},{2,35},{3,36},{4,37},{5,38},{6,39},{7,32},{8,41},{9,... | collective-permute-start | bytes 1572872 | tf_op jit(solution)/shard_map/weights_neighbours/ppermute | solution.py:41
  56.1 1.0 collective-permute-done.8
  57.1 5.2 %collective-permute-start.2 = (bf16[32,64,128]{2,1,0:T(8,128)(2,1)S(1)}, bf16[32,64,128]{2,1,0:T(8,128)(2,1)}, u32[]{:S(2)}, u32[]{:S(2)}) collective-permute-start(bf16[32,64,128]{2,1,0:T(8,128)(2,1)S(1)} %all-to-all-done), channel_id=1, source_target_pairs={{0,7},{1,0},{2,1},{3,2},{4,3},{5,4},{6,5},{7,6},{8,15},{9,8},{10,9... | collective-permute-start | bytes 1572872 | tf_op jit(solution)/shard_map/weights_neighbours/ppermute | solution.py:41
  62.3 3.8 %collective-permute-start.1 = (bf16[32,64,128]{2,1,0:T(8,128)(2,1)S(1)}, bf16[32,64,128]{2,1,0:T(8,128)(2,1)}, u32[]{:S(2)}, u32[]{:S(2)}) collective-permute-start(bf16[32,64,128]{2,1,0:T(8,128)(2,1)S(1)} %all-to-all-done), channel_id=1, source_target_pairs={{0,24},{1,25},{2,26},{3,27},{4,28},{5,29},{6,30},{7,31},{8,0},{9,1... | collective-permute-start | bytes 1572872 | tf_op jit(solution)/shard_map/weights_neighbours/ppermute | solution.py:41
  66.1 3.7 %collective-permute-start = (bf16[32,64,128]{2,1,0:T(8,128)(2,1)S(1)}, bf16[32,64,128]{2,1,0:T(8,128)(2,1)}, u32[]{:S(2)}, u32[]{:S(2)}) collective-permute-start(bf16[32,64,128]{2,1,0:T(8,128)(2,1)S(1)} %all-to-all-done), channel_id=1, source_target_pairs={{0,224},{1,225},{2,226},{3,227},{4,228},{5,229},{6,230},{7,231},{8... | collective-permute-start | bytes 1572872 | tf_op jit(solution)/shard_map/weights_neighbours/ppermute | solution.py:41
  69.8 2.7 %conditional.2 = ((bf16[288,512]{1,0:T(8,128)(2,1)}, bf16[288,512]{1,0:T(8,128)(2,1)}, f32[288,128]{1,0:T(8,128)S(1)}, bf16[288,32]{1,0:T(8,128)(2,1)}, bf16[288...) conditional(s32[]{:T(128)} %convert_element_type.6, ...), branch_computations={%region_0.1_spmd, %region_1.2_spmd} | conditional | bytes 8 | solution.py:492
  69.9 2.7 %shallow_prep.1 = (bf16[288,512]{1,0:T(8,128)(2,1)}, bf16[288,512]{1,0:T(8,128)(2,1)}, f32[288,128]{1,0:T(8,128)S(1)}, bf16[288,32]{1,0:T(8,128)(2,1)}, bf16[288...) custom-call(bf16[2,6,24,512]{3,2,1,0:T(8,128)(2,1)S(1)} %get-tuple-element.101.x, ...), custom_call_target="tpu_custom_call" | custom-call | tf_op jit(solution)/shard_map/prep/cond/branch_1_fun/shallow_prep/pallas_call | solution.py:385
  72.5 2.9 %collective-permute-done.4 = bf16[32,64,128]{2,1,0:T(8,128)(2,1)} collective-permute-done((bf16[32,64,128]{2,1,0:T(8,128)(2,1)S(1)}, bf16[32,64,128]{2,1,0:T(8,128)(2,1)}, u32[]{:S(2)}, u32[]{:S(2)}) %collective-permute-start.4) | collective-permute-done | bytes 524320 | tf_op jit(solution)/shard_map/weights_neighbours/ppermute | solution.py:41
  75.4 2.9 %collective-permute-done = bf16[32,64,128]{2,1,0:T(8,128)(2,1)} collective-permute-done((bf16[32,64,128]{2,1,0:T(8,128)(2,1)S(1)}, bf16[32,64,128]{2,1,0:T(8,128)(2,1)}, u32[]{:S(2)}, u32[]{:S(2)}) %collective-permute-start) | collective-permute-done | bytes 524320 | tf_op jit(solution)/shard_map/weights_neighbours/ppermute | solution.py:41
  78.4 10.3 %conditional.3 = ((bf16[2,6,24,512]{3,2,1,0:T(8,128)(2,1)S(1)}, bf16[2,6,12,512]{3,2,1,0:T(8,128)(2,1)S(1)}, bf16[768,128]{1,0:T(8,128)(2,1)})) conditional(s32[]{:T(128)} %convert_element_type.6, (s32[3]{0:T(128)S(1)}, bf16[32,64,128]{2,1,0:T(8,128)(2,1)S(1)}, bf16[32,64,128]{2,1,0:T(8,128)(2,1)}, bf16[32,64,128]{2,1,0:T(8,128)(2,1)}, ...), branch_computations={%region_2.3_spmd, %region_3.4_spmd} | conditional | bytes 8 | solution.py:507
  78.4 10.3 %shallow_block.1 = (bf16[2,6,24,512]{3,2,1,0:T(8,128)(2,1)S(1)}, bf16[2,6,12,512]{3,2,1,0:T(8,128)(2,1)S(1)}, bf16[768,128]{1,0:T(8,128)(2,1)}) custom-call(s32[3]{0:T(128)S(1)} %get-tuple-element.125.place_ref, bf16[32,64,128]{2,1,0:T(8,128)(2,1)S(1)} %get-tuple-element.126.p0, bf16[32,64,128]{2,1,0:T(8,128)(2,1)} %get-tuple-element.127.p1, ...), custom_call_target="tpu_custom_call" | custom-call | tf_op jit(solution)/shard_map/cond/branch_1_fun/shallow_block/pallas_call | solution.py:409
  88.7 1.9 %collective-permute-start.9 = (bf16[2,6,12,512]{3,2,1,0:T(8,128)(2,1)S(1)}, bf16[2,6,12,512]{3,2,1,0:T(8,128)(2,1)S(1)}, u32[]{:S(2)}, u32[]{:S(2)}) collective-permute-start(bf16[2,6,12,512]{3,2,1,0:T(8,128)(2,1)S(1)} %get-tuple-element.175), channel_id=1, source_target_pairs={{0,1},{1,2},{2,3},{3,4},{4,5},{5,6},{6,7},{7,8},{8,9},{9,10},{10,1... | collective-permute-start | bytes 442376 | tf_op jit(solution)/shard_map/shift_back/ppermute | solution.py:448
  90.6 6.8 %all-to-all-start.1 = ((bf16[16,48,128]{2,1,0:T(8,128)(2,1)}), bf16[16,48,128]{2,1,0:T(8,128)(2,1)S(1)}, u32[]{:S(2)}, u32[]{:S(2)}) async-start(bf16[16,48,128]{2,1,0:T(8,128)(2,1)} %bitcast.13), calls=%async_computation.1 | async-start | bytes 393216 | tf_op jit(solution)/shard_map/adapter_sum_lon/all_to_all | solution.py:515
  97.5 2.9 %collective-permute-done.9 = bf16[2,6,12,512]{3,2,1,0:T(8,128)(2,1)S(1)} collective-permute-done((bf16[2,6,12,512]{3,2,1,0:T(8,128)(2,1)S(1)}, bf16[2,6,12,512]{3,2,1,0:T(8,128)(2,1)S(1)}, u32[]{:S(2)}, u32[]{:S(2)}) %collective-permute-start.9) | collective-permute-done | bytes 147488 | tf_op jit(solution)/shard_map/shift_back/ppermute | solution.py:448
  100.3 0.2 pad_select_fusion
  100.5 4.7 %all-to-all-done.1 = bf16[16,48,128]{2,1,0:T(8,128)(2,1)S(1)} async-done(((bf16[16,48,128]{2,1,0:T(8,128)(2,1)}), bf16[16,48,128]{2,1,0:T(8,128)(2,1)S(1)}, u32[]{:S(2)}, u32[]{:S(2)}) %all-to-all-start.1) | async-done | bytes 196640 | tf_op jit(solution)/shard_map/adapter_sum_lon/all_to_all | solution.py:515
  105.3 0.7 broadcast_in_dim.25
  106.0 6.9 %all-to-all-start.2 = ((bf16[16,48,128]{2,1,0:T(8,128)(2,1)}), bf16[16,48,128]{2,1,0:T(8,128)(2,1)S(1)}, u32[]{:S(2)}, u32[]{:S(2)}) async-start(bf16[16,48,128]{2,1,0:T(8,128)(2,1)} %broadcast_in_dim.25), calls=%async_computation.2 | async-start | bytes 393216 | tf_op jit(solution)/shard_map/adapter_sum_lat/all_to_all | solution.py:523
  112.9 5.3 %collective-permute-start.10 = (bf16[2,3,24,512]{3,2,1,0:T(8,128)(2,1)S(1)}, bf16[2,3,24,512]{3,2,1,0:T(8,128)(2,1)S(1)}, u32[]{:S(2)}, u32[]{:S(2)}) collective-permute-start(bf16[2,3,24,512]{3,2,1,0:T(8,128)(2,1)S(1)} %get-tuple-element.178), channel_id=1, source_target_pairs={{0,16},{1,17},{2,18},{3,19},{4,20},{5,21},{6,22},{7,23},{8,24},{9,... | collective-permute-start | bytes 442376 | tf_op jit(solution)/shard_map/shift_back/ppermute | solution.py:448
  118.2 6.4 %all-to-all-done.2 = bf16[16,48,128]{2,1,0:T(8,128)(2,1)S(1)} async-done(((bf16[16,48,128]{2,1,0:T(8,128)(2,1)}), bf16[16,48,128]{2,1,0:T(8,128)(2,1)S(1)}, u32[]{:S(2)}, u32[]{:S(2)}) %all-to-all-start.2) | async-done | bytes 196640 | tf_op jit(solution)/shard_map/adapter_sum_lat/all_to_all | solution.py:523
  124.6 0.7 broadcast_in_dim.26
  125.3 5.2 %all-to-all-start.3 = ((bf16[16,48,128]{2,1,0:T(8,128)(2,1)}), bf16[16,48,128]{2,1,0:T(8,128)(2,1)S(1)}, u32[]{:S(2)}, u32[]{:S(2)}) async-start(bf16[16,48,128]{2,1,0:T(8,128)(2,1)} %broadcast_in_dim.26), calls=%async_computation.3 | async-start | bytes 393216 | tf_op jit(solution)/shard_map/adapter_gather/all_to_all | solution.py:525
  130.6 1.9 %collective-permute-start.11 = (bf16[2,6,24,512]{3,2,1,0:T(8,128)(2,1)S(1)}, bf16[2,6,24,512]{3,2,1,0:T(8,128)(2,1)S(1)}, u32[]{:S(2)}, u32[]{:S(2)}) collective-permute-start(bf16[2,6,24,512]{3,2,1,0:T(8,128)(2,1)S(1)} %pad_maximum_fusion.2), channel_id=1, source_target_pairs={{0,256},{1,257},{2,258},{3,259},{4,260},{5,261},{6,262},{7,263},{8... | collective-permute-start | bytes 884744 | tf_op jit(solution)/shard_map/hand_over/ppermute | solution.py:440
  132.5 1.5 %collective-permute-done.11 = bf16[2,6,24,512]{3,2,1,0:T(8,128)(2,1)S(1)} collective-permute-done((bf16[2,6,24,512]{3,2,1,0:T(8,128)(2,1)S(1)}, bf16[2,6,24,512]{3,2,1,0:T(8,128)(2,1)S(1)}, u32[]{:S(2)}, u32[]{:S(2)}) %collective-permute-start.11) | collective-permute-done | bytes 294944 | tf_op jit(solution)/shard_map/hand_over/ppermute | solution.py:440
  134.1 4.3 %all-to-all-done.3 = bf16[16,48,128]{2,1,0:T(8,128)(2,1)S(1)} async-done(((bf16[16,48,128]{2,1,0:T(8,128)(2,1)}), bf16[16,48,128]{2,1,0:T(8,128)(2,1)S(1)}, u32[]{:S(2)}, u32[]{:S(2)}) %all-to-all-start.3) | async-done | bytes 196640 | tf_op jit(solution)/shard_map/adapter_gather/all_to_all | solution.py:525
  138.3 0.8 reshape.27
  139.1 0.7 copy.38
  (23 shorter events, 0.2 us)
Async XLA Ops:
  2.6 18.9 %copy-start = (bf16[1,2,6,24,512]{4,3,2,1,0:T(8,128)(2,1)S(1)}, bf16[1,2,6,24,512]{4,3,2,1,0:T(8,128)(2,1)}, u32[]{:S(2)}) copy-start(bf16[1,2,6,24,512]{4,3,2,1,0:T(8,128)(2,1)} %param.15) | copy-start | bytes 884740
  2.6 18.9 %copy-start.1 = (bf16[1,2,6,24,512]{4,3,2,1,0:T(8,128)(2,1)S(1)}, bf16[1,2,6,24,512]{4,3,2,1,0:T(8,128)(2,1)}, u32[]{:S(2)}) copy-start(bf16[1,2,6,24,512]{4,3,2,1,0:T(8,128)(2,1)} %param.16) | copy-start | bytes 884740
  2.6 38.5 %all-to-all-start = ((bf16[32,64,128]{2,1,0:T(8,128)(2,1)}), bf16[32,64,128]{2,1,0:T(8,128)(2,1)S(1)}, u32[]{:S(2)}, u32[]{:S(2)}) async-start(bf16[32,64,128]{2,1,0:T(8,128)(2,1)} %pack_weights.1), calls=%async_computation | async-start | bytes 1048576 | tf_op jit(solution)/shard_map/weights_class/all_to_all | solution.py:471
  21.5 4.7 %copy-start.3 = (s32[144,144]{1,0:T(8,128)S(1)}, s32[144,144]{1,0:T(8,128)}, u32[]{:S(2)}) copy-start(s32[144,144]{1,0:T(8,128)} %param.18) | copy-start | bytes 248836
  22.3 23.0 %collective-permute-start.7 = (bf16[2,2,3,24,512]{4,3,2,1,0:T(8,128)(2,1)}, bf16[2,2,3,24,512]{4,3,2,1,0:T(8,128)(2,1)S(1)}, u32[]{:S(2)}, u32[]{:S(2)}) collective-permute-start(bf16[2,2,3,24,512]{4,3,2,1,0:T(8,128)(2,1)} %pad_maximum_fusion.1), channel_id=1, source_target_pairs={{0,240},{1,241},{2,242},{3,243},{4,244},{5,245},{6,246},{7,247},{8... | collective-permute-start | bytes 884744 | tf_op jit(solution)/shard_map/halos/ppermute | solution.py:448
  26.3 0.7 copy-start.4
  26.3 0.7 copy-start.5
  41.1 21.2 %collective-permute-start.6 = (bf16[32,64,128]{2,1,0:T(8,128)(2,1)S(1)}, bf16[32,64,128]{2,1,0:T(8,128)(2,1)S(1)}, u32[]{:S(2)}, u32[]{:S(2)}) collective-permute-start(bf16[32,64,128]{2,1,0:T(8,128)(2,1)S(1)} %all-to-all-done), channel_id=1, source_target_pairs={{0,32},{1,33},{2,34},{3,35},{4,36},{5,37},{6,38},{7,39},{8,40},{9,... | collective-permute-start | bytes 1572872 | tf_op jit(solution)/shard_map/weights_neighbours/ppermute | solution.py:41
  43.3 22.8 %collective-permute-start.5 = (bf16[32,64,128]{2,1,0:T(8,128)(2,1)S(1)}, bf16[32,64,128]{2,1,0:T(8,128)(2,1)S(1)}, u32[]{:S(2)}, u32[]{:S(2)}) collective-permute-start(bf16[32,64,128]{2,1,0:T(8,128)(2,1)S(1)} %all-to-all-done), channel_id=1, source_target_pairs={{0,8},{1,9},{2,10},{3,11},{4,12},{5,13},{6,14},{7,15},{8,16},{9,17... | collective-permute-start | bytes 1572872 | tf_op jit(solution)/shard_map/weights_neighbours/ppermute | solution.py:41
  45.4 11.7 %collective-permute-start.8 = (bf16[2,2,6,12,512]{4,3,2,1,0:T(8,128)(2,1)S(1)}, bf16[2,2,6,12,512]{4,3,2,1,0:T(8,128)(2,1)S(1)}, u32[]{:S(2)}, u32[]{:S(2)}) collective-permute-start(bf16[2,2,6,12,512]{4,3,2,1,0:T(8,128)(2,1)S(1)} %pad_maximum_fusion), channel_id=1, source_target_pairs={{0,15},{1,0},{2,1},{3,2},{4,3},{5,4},{6,5},{7,6},{8,7},{9,8},{10,9... | collective-permute-start | bytes 884744 | tf_op jit(solution)/shard_map/halos/ppermute | solution.py:448
  51.8 23.6 %collective-permute-start.4 = (bf16[32,64,128]{2,1,0:T(8,128)(2,1)S(1)}, bf16[32,64,128]{2,1,0:T(8,128)(2,1)}, u32[]{:S(2)}, u32[]{:S(2)}) collective-permute-start(bf16[32,64,128]{2,1,0:T(8,128)(2,1)S(1)} %all-to-all-done), channel_id=1, source_target_pairs={{0,1},{1,2},{2,3},{3,4},{4,5},{5,6},{6,7},{7,0},{8,9},{9,10},{10,1... | collective-permute-start | bytes 1572872 | tf_op jit(solution)/shard_map/weights_neighbours/ppermute | solution.py:41
  53.8 21.7 %collective-permute-start.3 = (bf16[32,64,128]{2,1,0:T(8,128)(2,1)S(1)}, bf16[32,64,128]{2,1,0:T(8,128)(2,1)}, u32[]{:S(2)}, u32[]{:S(2)}) collective-permute-start(bf16[32,64,128]{2,1,0:T(8,128)(2,1)S(1)} %all-to-all-done), channel_id=1, source_target_pairs={{0,33},{1,34},{2,35},{3,36},{4,37},{5,38},{6,39},{7,32},{8,41},{9,... | collective-permute-start | bytes 1572872 | tf_op jit(solution)/shard_map/weights_neighbours/ppermute | solution.py:41
  57.1 9.0 %copy-start.2 = (bf16[2,2,6,12,512]{4,3,2,1,0:T(8,128)(2,1)}, bf16[2,2,6,12,512]{4,3,2,1,0:T(8,128)(2,1)S(1)}, u32[]{:S(2)}) copy-start(bf16[2,2,6,12,512]{4,3,2,1,0:T(8,128)(2,1)S(1)} %collective-permute-done.8) | copy-start | bytes 884740
  57.1 18.3 %collective-permute-start.2 = (bf16[32,64,128]{2,1,0:T(8,128)(2,1)S(1)}, bf16[32,64,128]{2,1,0:T(8,128)(2,1)}, u32[]{:S(2)}, u32[]{:S(2)}) collective-permute-start(bf16[32,64,128]{2,1,0:T(8,128)(2,1)S(1)} %all-to-all-done), channel_id=1, source_target_pairs={{0,7},{1,0},{2,1},{3,2},{4,3},{5,4},{6,5},{7,6},{8,15},{9,8},{10,9... | collective-permute-start | bytes 1572872 | tf_op jit(solution)/shard_map/weights_neighbours/ppermute | solution.py:41
  62.3 13.1 %collective-permute-start.1 = (bf16[32,64,128]{2,1,0:T(8,128)(2,1)S(1)}, bf16[32,64,128]{2,1,0:T(8,128)(2,1)}, u32[]{:S(2)}, u32[]{:S(2)}) collective-permute-start(bf16[32,64,128]{2,1,0:T(8,128)(2,1)S(1)} %all-to-all-done), channel_id=1, source_target_pairs={{0,24},{1,25},{2,26},{3,27},{4,28},{5,29},{6,30},{7,31},{8,0},{9,1... | collective-permute-start | bytes 1572872 | tf_op jit(solution)/shard_map/weights_neighbours/ppermute | solution.py:41
  66.1 12.2 %collective-permute-start = (bf16[32,64,128]{2,1,0:T(8,128)(2,1)S(1)}, bf16[32,64,128]{2,1,0:T(8,128)(2,1)}, u32[]{:S(2)}, u32[]{:S(2)}) collective-permute-start(bf16[32,64,128]{2,1,0:T(8,128)(2,1)S(1)} %all-to-all-done), channel_id=1, source_target_pairs={{0,224},{1,225},{2,226},{3,227},{4,228},{5,229},{6,230},{7,231},{8... | collective-permute-start | bytes 1572872 | tf_op jit(solution)/shard_map/weights_neighbours/ppermute | solution.py:41
  88.7 11.6 %collective-permute-start.9 = (bf16[2,6,12,512]{3,2,1,0:T(8,128)(2,1)S(1)}, bf16[2,6,12,512]{3,2,1,0:T(8,128)(2,1)S(1)}, u32[]{:S(2)}, u32[]{:S(2)}) collective-permute-start(bf16[2,6,12,512]{3,2,1,0:T(8,128)(2,1)S(1)} %get-tuple-element.175), channel_id=1, source_target_pairs={{0,1},{1,2},{2,3},{3,4},{4,5},{5,6},{6,7},{7,8},{8,9},{9,10},{10,1... | collective-permute-start | bytes 442376 | tf_op jit(solution)/shard_map/shift_back/ppermute | solution.py:448
  90.6 14.6 %all-to-all-start.1 = ((bf16[16,48,128]{2,1,0:T(8,128)(2,1)}), bf16[16,48,128]{2,1,0:T(8,128)(2,1)S(1)}, u32[]{:S(2)}, u32[]{:S(2)}) async-start(bf16[16,48,128]{2,1,0:T(8,128)(2,1)} %bitcast.13), calls=%async_computation.1 | async-start | bytes 393216 | tf_op jit(solution)/shard_map/adapter_sum_lon/all_to_all | solution.py:515
  106.0 18.6 %all-to-all-start.2 = ((bf16[16,48,128]{2,1,0:T(8,128)(2,1)}), bf16[16,48,128]{2,1,0:T(8,128)(2,1)S(1)}, u32[]{:S(2)}, u32[]{:S(2)}) async-start(bf16[16,48,128]{2,1,0:T(8,128)(2,1)} %broadcast_in_dim.25), calls=%async_computation.2 | async-start | bytes 393216 | tf_op jit(solution)/shard_map/adapter_sum_lat/all_to_all | solution.py:523
  112.9 17.7 %collective-permute-start.10 = (bf16[2,3,24,512]{3,2,1,0:T(8,128)(2,1)S(1)}, bf16[2,3,24,512]{3,2,1,0:T(8,128)(2,1)S(1)}, u32[]{:S(2)}, u32[]{:S(2)}) collective-permute-start(bf16[2,3,24,512]{3,2,1,0:T(8,128)(2,1)S(1)} %get-tuple-element.178), channel_id=1, source_target_pairs={{0,16},{1,17},{2,18},{3,19},{4,20},{5,21},{6,22},{7,23},{8,24},{9,... | collective-permute-start | bytes 442376 | tf_op jit(solution)/shard_map/shift_back/ppermute | solution.py:448
  125.3 13.0 %all-to-all-start.3 = ((bf16[16,48,128]{2,1,0:T(8,128)(2,1)}), bf16[16,48,128]{2,1,0:T(8,128)(2,1)S(1)}, u32[]{:S(2)}, u32[]{:S(2)}) async-start(bf16[16,48,128]{2,1,0:T(8,128)(2,1)} %broadcast_in_dim.26), calls=%async_computation.3 | async-start | bytes 393216 | tf_op jit(solution)/shard_map/adapter_gather/all_to_all | solution.py:525
  130.6 3.5 %collective-permute-start.11 = (bf16[2,6,24,512]{3,2,1,0:T(8,128)(2,1)S(1)}, bf16[2,6,24,512]{3,2,1,0:T(8,128)(2,1)S(1)}, u32[]{:S(2)}, u32[]{:S(2)}) collective-permute-start(bf16[2,6,24,512]{3,2,1,0:T(8,128)(2,1)S(1)} %pad_maximum_fusion.2), channel_id=1, source_target_pairs={{0,256},{1,257},{2,258},{3,259},{4,260},{5,261},{6,262},{7,263},{8... | collective-permute-start | bytes 884744 | tf_op jit(solution)/shard_map/hand_over/ppermute | solution.py:440
